TPU v7x, 256 devices: a whole 4x4x8 slice. The times are simulated.
256 devices in a mesh: prow: 16 (over x, z_hi), pcol: 16 (over z_lo, y, core).
Axes of the slice: x: 4, y: 4, z: 8 (z_hi: 4, z_lo: 2; z = z_hi * 2 + z_lo), core: 2. Of those that a mesh axis runs over, the one named last changes fastest.
Arguments:
- separator_inverse: float32 [12288, 12288], P('prow', 'pcol'), may hold values from -6 to 6
- panel: float32 [12288, 2048], P('pcol', 'prow'), may hold values from -0.0546875 to 0.0546875
- block_rows: int32 [16], replicated, may hold values 0 or 1
- pivot_inverse: float32 [2048, 2048], P('prow', 'pcol'), may hold values from -4 to 4
Outputs:
- off_diagonal: float32 [12288, 2048], P('prow', 'pcol')
- child_inverse: float32 [2048, 2048], P('prow', 'pcol')
All inputs are finite; a program needn't handle non-finite values.
Results may differ from a plain program's by a relative error of at most 0.000088.
Values sent between devices are 32-bit elements; how exact they have to be, the bound alone decides.
No kernel may reach another device: no remote copies, remote signals or barrier semaphores. Data moves between devices by JAX's collectives and lax.ppermute only.
A program may use at most 128 MiB of HBM per device.

v0:
```python
import functools

import jax
import jax.numpy as jnp
from jax import lax
from jax.experimental import pallas as pl
from jax.experimental.pallas import tpu as pltpu
from jax.sharding import PartitionSpec as P

BS = 768
AXES = ("prow", "pcol")
SIZES = (16, 32, 16)
FROM = (0, 16, 48)
STEPS = (0, 1, -1, 2)
COST = pl.CostEstimate(flops=1000, bytes_accessed=1000, transcendentals=0)
VMEM = pl.BlockSpec(memory_space=pltpu.VMEM)
SMEM = pl.BlockSpec(memory_space=pltpu.SMEM)
ANY = pl.BlockSpec(memory_space=pl.ANY)


def places():
    for x in range(4):
        for zh in range(4):
            for zl in range(2):
                for y in range(4):
                    for core in range(2):
                        yield x, zh, zl, y, core


def index_of(x, zh, zl, y, core):
    return ((x % 4) * 4 + zh % 4) * 16 + (zl % 2) * 8 + (y % 4) * 2 + core % 2


def shift(dx=0, dzh=0, dzl=0, dy=0, dcore=0):
    return [
        (index_of(x, zh, zl, y, c), index_of(x + dx, zh + dzh, zl + dzl, y + dy, c + dcore))
        for x, zh, zl, y, c in places()
    ]


def row_of(j):
    j0, j1, j2, j3 = j & 1, (j >> 1) & 1, (j >> 2) & 1, j >> 3
    return j3 + 2 * (j0 ^ j1) + 4 * j1 + 8 * (j2 ^ j0)


TO_COLUMN = [(k * 16 + j, row_of(j) * 16 + k) for k in range(16) for j in range(16)]
TO_PLACE = [(row_of(j) * 16 + i, i * 16 + j) for i in range(16) for j in range(16)]


def send(value, pairs):
    return lax.ppermute(value, AXES, pairs)


def ring_gather(value, axis):
    return [value] + [send(value, shift(**{axis: step})) for step in STEPS[1:]]


def ring_forward(value, axis):
    half = value.shape[0] // 2
    up, down = (send(value, shift(**{axis: step})) for step in STEPS[1:3])
    far = [send(up[:half], shift(**{axis: 1})), send(down[half:], shift(**{axis: -1}))]
    return [value, up, down, *far]


def ring_scatter(values, axis):
    got = [send(value, shift(**{axis: step})) for step, value in zip(STEPS[1:], values[1:])]
    return (values[0] + got[0]) + (got[1] + got[2])


def pick(value, at):
    return lax.dynamic_index_in_dim(value, at, 0, keepdims=False)


def split(value):
    high = lax.reduce_precision(value, 8, 7)
    return high.astype(jnp.bfloat16), (value - high).astype(jnp.bfloat16)


def dot_nt(a, b):
    return lax.dot_general(a, b, (((1,), (1,)), ((), ())), preferred_element_type=jnp.float32)


def store_split(high_ref, low_ref, at, value):
    high = value.astype(jnp.bfloat16)
    high_ref[at] = high
    low_ref[at] = (value - high.astype(jnp.float32)).astype(jnp.bfloat16)


def ring_slot(step):
    step = lax.rem(step + 8, 4)
    return jnp.where(step == 3, 2, jnp.where(step == 2, 3, step))


def product_kernel(rows, me_ref, c0, c1, c2, c3, h0, l0, h1, l1, o0, o1, o2, o3, high, low):
    x, zh, y = me_ref[0], me_ref[1], me_ref[2]
    for sx, ref in enumerate((c0, c1, c2, c3)):
        for sz in range(4):
            xs = lax.rem(x - STEPS[sx] + 4, 4)
            zs = lax.rem(zh - STEPS[sz] + 4, 4)
            to = ring_slot(2 * lax.rem(xs, 2) + zs // 2 - y)
            place = (to * 2 + xs // 2) * 2 + lax.rem(zs, 2)
            at = pl.ds(pl.multiple_of(place * rows, rows), rows)
            store_split(high, low, (at, slice(None)), ref[sz * rows : (sz + 1) * rows, :])
    own, other = slice(0, BS), slice(BS, 2 * BS)
    for n in range(0, BS, 256):
        cols = slice(n, n + 256)
        sums = dot_nt(high[:, own], h0[cols, :]) + dot_nt(high[:, other], h1[cols, :])
        sums += dot_nt(low[:, own], h0[cols, :]) + dot_nt(low[:, other], h1[cols, :])
        sums += dot_nt(high[:, own], l0[cols, :]) + dot_nt(high[:, other], l1[cols, :])
        for i, out in enumerate((o0, o1, o2, o3)):
            out[:, cols] = sums[4 * rows * i : 4 * rows * (i + 1)]


def product(me, parts, sep):
    rows = parts[0].shape[0] // 4
    outs = pl.pallas_call(
        functools.partial(product_kernel, rows),
        out_shape=[jax.ShapeDtypeStruct((4 * rows, BS), jnp.float32)] * 4
        + [jax.ShapeDtypeStruct((16 * rows, 2 * BS), jnp.bfloat16)] * 2,
        in_specs=[SMEM] + [VMEM] * 8,
        out_specs=[VMEM] * 6,
        compiler_params=pltpu.CompilerParams(vmem_limit_bytes=18 << 20),
        cost_estimate=COST,
        name="product",
    )(me, *parts, *sep)
    return outs[:4], outs[4:]


def gram_kernel(*refs):
    high, low, own, other, outs, chigh, clow = refs[0:3], refs[3:6], refs[6], refs[7], refs[8:12], refs[12], refs[13]
    store_split(chigh, clow, (slice(None), slice(0, BS)), own[...])
    store_split(chigh, clow, (slice(None), slice(BS, 2 * BS)), other[...])
    for t, rows in enumerate(SIZES):
        sums = dot_nt(high[t][...], chigh[...]) + dot_nt(low[t][...], chigh[...]) + dot_nt(high[t][...], clow[...])
        for i, out in enumerate(outs):
            for e in range(4):
                at = 64 * e + FROM[t]
                out[at : at + rows, :] = sums[(4 * i + e) * rows : (4 * i + e + 1) * rows]


def gram_parts(panels, own, other):
    return pl.pallas_call(
        gram_kernel,
        out_shape=[jax.ShapeDtypeStruct((256, 128), jnp.float32)] * 4,
        in_specs=[VMEM] * 8,
        out_specs=[VMEM] * 4,
        scratch_shapes=[pltpu.VMEM((128, 2 * BS), jnp.bfloat16)] * 2,
        compiler_params=pltpu.CompilerParams(vmem_limit_bytes=14 << 20),
        cost_estimate=COST,
        name="gram",
    )(*[p[0] for p in panels], *[p[1] for p in panels], own, other)


def join_kernel(sizes, parts, *refs):
    values = [ref[...] for ref in refs[: min(parts, 3)]]
    values.append(jnp.concatenate([ref[...] for ref in refs[3:parts]]) if parts > 4 else refs[3][...])
    start = 0
    for rows, out in zip(sizes, refs[len(refs) - len(sizes) :]):
        for j, value in enumerate(values):
            out[rows * j : rows * (j + 1), :] = value[start : start + rows]
        start += rows


def join(parts, sizes, riders=(), others=()):
    return pl.pallas_call(
        functools.partial(join_kernel, sizes, len(parts)),
        out_shape=[jax.ShapeDtypeStruct(rider.shape, rider.dtype) for rider in riders]
        + [jax.ShapeDtypeStruct((4 * rows, parts[0].shape[1]), jnp.float32) for rows in sizes],
        in_specs=[VMEM] * len(parts) + [ANY] * (len(riders) + len(others)),
        out_specs=[ANY] * len(riders) + [VMEM] * len(sizes),
        input_output_aliases={len(parts) + i: i for i in range(len(riders))},
        compiler_params=pltpu.CompilerParams(vmem_limit_bytes=4 << 20),
        cost_estimate=COST,
        name="join",
    )(*parts, *riders, *others)


def tie_kernel(*refs):
    pass


def tie(value, *others):
    return pl.pallas_call(
        tie_kernel,
        out_shape=jax.ShapeDtypeStruct(value.shape, value.dtype),
        in_specs=[ANY] * (1 + len(others)),
        out_specs=ANY,
        input_output_aliases={0: 0},
        compiler_params=pltpu.CompilerParams(vmem_limit_bytes=1 << 20),
        cost_estimate=COST,
        name="tie",
    )(value, *others)


def local(separator_inverse, panel, block_rows, pivot_inverse):
    r = lax.axis_index("prow")
    c = lax.axis_index("pcol")
    x, zh = r // 4, lax.rem(r, 4)
    zl, y, core = c // 8, lax.rem(c // 2, 4), lax.rem(c, 2)
    first = core == 0
    keep_c = pick(block_rows, c).astype(jnp.float32)
    keep_r = pick(block_rows, r).astype(jnp.float32)
    swap = shift(dcore=1)
    me = jnp.stack([x, zh, y]).astype(jnp.int32)

    def from_chips(part):
        part = part.reshape(2, 2, -1, BS)
        return keep_r * (pick(part, zl) + send(pick(part, 1 - zl), shift(dzl=1)))

    panel_t = (panel * keep_c).T
    low, high = panel_t[:64], panel_t[64:]
    mine = jnp.where(first, low, high)
    theirs = jnp.where(first, high, low)
    mine = jnp.concatenate([mine, send(theirs, swap)], axis=1)
    sep_other = send(separator_inverse, swap)
    sep = split(separator_inverse) + split(sep_other)

    lead, rest = mine[: SIZES[0]], mine[SIZES[0] :]
    rest, col0 = join(ring_gather(lead, "dzh"), SIZES[:1], [rest])
    x0 = ring_gather(col0, "dx")
    x0[0], col1, col2 = join(ring_forward(rest, "dzh"), SIZES[1:], [col0], [*x0[1:], *sep[2:]])
    x1 = ring_gather(col1, "dx")
    out0, panel0 = product(me, x0, sep)
    own = [from_chips(ring_scatter(out0, "dy"))]
    x2 = ring_gather(tie(col2, *x1[1:], own[0]), "dx")
    out1, panel1 = product(me, x1, sep)
    sums1 = ring_scatter(out1, "dy")
    out2, panel2 = product(me, x2, sep)
    sums2 = ring_scatter(out2, "dy")
    own += [from_chips(sums1), from_chips(sums2)]

    def whole(value):
        mine, theirs = pick(value, core), send(pick(value, 1 - core), swap)
        return jnp.where(first, jnp.concatenate([mine, theirs]), jnp.concatenate([theirs, mine]))

    kept = whole(jnp.concatenate(own, axis=1))
    column = send(kept, TO_COLUMN)
    gram = gram_parts((panel0, panel1, panel2), column, send(column, swap))
    off_diagonal = -kept.T
    gram = ring_scatter(gram, "dy").reshape(2, 2, 64, 128)
    gram = whole(pick(gram, zl) + send(pick(gram, 1 - zl), shift(dzl=1)))
    gram = send(gram, TO_PLACE)
    return off_diagonal, pivot_inverse + gram


def solution(mesh):
    in_specs = (P("prow", "pcol"), P("pcol", "prow"), P(), P("prow", "pcol"))
    out_specs = (P("prow", "pcol"), P("prow", "pcol"))
    return jax.shard_map(local, mesh=mesh, in_specs=in_specs, out_specs=out_specs, check_vma=False)
```

profile of v0, /device:TPU:24, one launch (start us, length us, event | category | flops | bytes accessed | tf_op | source)
XLA Modules:
  0.0 224.7 jit_solution(13409048467008695124)
XLA Ops:
  5.7 3.3 %collective-permute-start.1 = (f32[16,1536]{1,0:T(8,128)S(1)}, f32[16,1536]{1,0:T(8,128)S(1)}, u32[]{:S(2)}, u32[]{:S(2)}) collective-permute-start(f32[16,1536]{1,0:T(8,128)S(1)} %pad_maximum_fusion.2.refs_0_), channel_id=1, source_target_pairs={{0,16},{1,17},{2,18},{3,19},{4,20},{5,21},{6,22},{7,23},{8,24},{9,... | collective-permute-start | bytes 294920 | tf_op jit(solution)/shard_map/ppermute | solution.py:51
  9.0 3.1 %collective-permute-start.2 = (f32[16,1536]{1,0:T(8,128)S(1)}, f32[16,1536]{1,0:T(8,128)S(1)}, u32[]{:S(2)}, u32[]{:S(2)}) collective-permute-start(f32[16,1536]{1,0:T(8,128)S(1)} %pad_maximum_fusion.2.refs_0_), channel_id=1, source_target_pairs={{0,48},{1,49},{2,50},{3,51},{4,52},{5,53},{6,54},{7,55},{8,56},{9,... | collective-permute-start | bytes 294920 | tf_op jit(solution)/shard_map/ppermute | solution.py:51
  12.1 4.9 %collective-permute-start.3 = (f32[16,1536]{1,0:T(8,128)S(1)}, f32[16,1536]{1,0:T(8,128)S(1)}, u32[]{:S(2)}, u32[]{:S(2)}) collective-permute-start(f32[16,1536]{1,0:T(8,128)S(1)} %pad_maximum_fusion.2.refs_0_), channel_id=1, source_target_pairs={{0,32},{1,33},{2,34},{3,35},{4,36},{5,37},{6,38},{7,39},{8,40},{9,... | collective-permute-start | bytes 294920 | tf_op jit(solution)/shard_map/ppermute | solution.py:51
  17.1 2.4 %collective-permute-done.2.refs_2_ = f32[16,1536]{1,0:T(8,128)S(1)} collective-permute-done((f32[16,1536]{1,0:T(8,128)S(1)}, f32[16,1536]{1,0:T(8,128)S(1)}, u32[]{:S(2)}, u32[]{:S(2)}) %collective-permute-start.2) | collective-permute-done | bytes 98336 | tf_op jit(solution)/shard_map/ppermute | solution.py:51
  19.4 3.7 %collective-permute-done.3.refs_3_ = f32[16,1536]{1,0:T(8,128)S(1)} collective-permute-done((f32[16,1536]{1,0:T(8,128)S(1)}, f32[16,1536]{1,0:T(8,128)S(1)}, u32[]{:S(2)}, u32[]{:S(2)}) %collective-permute-start.3) | collective-permute-done | bytes 98336 | tf_op jit(solution)/shard_map/ppermute | solution.py:51
  23.2 3.7 %collective-permute-start.4 = (f32[48,1536]{1,0:T(8,128)S(1)}, f32[48,1536]{1,0:T(8,128)S(1)}, u32[]{:S(2)}, u32[]{:S(2)}) collective-permute-start(f32[48,1536]{1,0:T(8,128)S(1)} %get-tuple-element.29.refs_0_), channel_id=1, source_target_pairs={{0,16},{1,17},{2,18},{3,19},{4,20},{5,21},{6,22},{7,23},{8,24},{9,... | collective-permute-start | bytes 884744 | tf_op jit(solution)/shard_map/ppermute | solution.py:51
  27.7 3.1 %collective-permute-start.10 = (f32[64,1536]{1,0:T(8,128)S(1)}, f32[64,1536]{1,0:T(8,128)S(1)}, u32[]{:S(2)}, u32[]{:S(2)}) collective-permute-start(f32[64,1536]{1,0:T(8,128)S(1)} %get-tuple-element.30.refs_5_), channel_id=1, source_target_pairs={{0,128},{1,129},{2,130},{3,131},{4,132},{5,133},{6,134},{7,135},{8... | collective-permute-start | bytes 1179656 | tf_op jit(solution)/shard_map/ppermute | solution.py:51
  33.0 2.8 %collective-permute-start.9 = (f32[64,1536]{1,0:T(8,128)S(1)}, f32[64,1536]{1,0:T(8,128)S(1)}, u32[]{:S(2)}, u32[]{:S(2)}) collective-permute-start(f32[64,1536]{1,0:T(8,128)S(1)} %get-tuple-element.30.refs_5_), channel_id=1, source_target_pairs={{0,192},{1,193},{2,194},{3,195},{4,196},{5,197},{6,198},{7,199},{8... | collective-permute-start | bytes 1179656 | tf_op jit(solution)/shard_map/ppermute | solution.py:51
  35.9 2.4 %collective-permute-start.6 = (f32[24,1536]{1,0:T(8,128)S(1)}, f32[24,1536]{1,0:T(8,128)S(1)}, u32[]{:S(2)}, u32[]{:S(2)}) collective-permute-start(f32[24,1536]{1,0:T(8,128)S(1)} %slice.26), channel_id=1, source_target_pairs={{0,16},{1,17},{2,18},{3,19},{4,20},{5,21},{6,22},{7,23},{8,24},{9,... | collective-permute-start | bytes 442376 | tf_op jit(solution)/shard_map/ppermute | solution.py:51
  42.2 4.6 %collective-permute-done.8.refs_6_.c1 = f32[64,1536]{1,0:T(8,128)S(1)} collective-permute-done((f32[64,1536]{1,0:T(8,128)S(1)}, f32[64,1536]{1,0:T(8,128)S(1)}, u32[]{:S(2)}, u32[]{:S(2)}) %collective-permute-start.8) | collective-permute-done | bytes 393248 | tf_op jit(solution)/shard_map/ppermute | solution.py:51
  47.9 3.6 %product.3 = (f32[64,768]{1,0:T(8,128)S(1)}, f32[64,768]{1,0:T(8,128)S(1)}, f32[64,768]{1,0:T(8,128)}, f32[64,768]{1,0:T(8,128)}, bf16[256,1536]{1,0:T(8,128)(2,1)S(1)}, /*index=5*/bf16[256,1536]{1,0:T(8,128)(2,1)S(1)}) custom-call(s32[3]{0:T(128)S(1)} %pad_add_fusion.me_ref, f32[64,1536]{1,0:T(8,128)S(1)} %get-tuple-element.31.c0, ...), custom_call_target="tpu_custom_call" | custom-call | flops 1000 | bytes 1000 | tf_op jit(solution)/shard_map/product/pallas_call | solution.py:116
  69.0 4.6 %collective-permute-start.15 = (f32[2,16,768]{2,1,0:T(8,128)}, f32[2,16,768]{2,1,0:T(8,128)}, u32[]{:S(2)}, u32[]{:S(2)}) collective-permute-start(f32[2,16,768]{2,1,0:T(8,128)} %dynamic-slice_bitcast_fusion.4), channel_id=1, source_target_pairs={{0,8},{1,9},{2,10},{3,11},{4,12},{5,13},{6,14},{7,15},{8,0},{9,1},... | collective-permute-start | bytes 294920 | tf_op jit(solution)/shard_map/ppermute | solution.py:51
  74.2 2.3 %collective-permute-done.15 = f32[2,16,768]{2,1,0:T(8,128)} collective-permute-done((f32[2,16,768]{2,1,0:T(8,128)}, f32[2,16,768]{2,1,0:T(8,128)}, u32[]{:S(2)}, u32[]{:S(2)}) %collective-permute-start.15) | collective-permute-done | bytes 98336 | tf_op jit(solution)/shard_map/ppermute | solution.py:51
  77.5 16.6 %collective-permute-done.16.c1.refs_1_ = f32[128,1536]{1,0:T(8,128)} collective-permute-done((f32[128,1536]{1,0:T(8,128)}, f32[128,1536]{1,0:T(8,128)}, u32[]{:S(2)}, u32[]{:S(2)}) %collective-permute-start.16) | collective-permute-done | bytes 786464 | tf_op jit(solution)/shard_map/ppermute | solution.py:51
  95.1 2.4 %collective-permute-start.24 = (f32[64,1536]{1,0:T(8,128)}, f32[64,1536]{1,0:T(8,128)}, u32[]{:S(2)}, u32[]{:S(2)}) collective-permute-start(f32[64,1536]{1,0:T(8,128)} %tie.1.c0), channel_id=1, source_target_pairs={{0,192},{1,193},{2,194},{3,195},{4,196},{5,197},{6,198},{7,199},{8... | collective-permute-start | bytes 1179656 | tf_op jit(solution)/shard_map/ppermute | solution.py:51
  98.6 7.4 %product.4 = (f32[128,768]{1,0:T(8,128)S(1)}, f32[128,768]{1,0:T(8,128)}, f32[128,768]{1,0:T(8,128)}, f32[128,768]{1,0:T(8,128)}, bf16[512,1536]{1,0:T(8,128)(2,1)S(1)}, /*index=5*/bf16[512,1536]{1,0:T(8,128)(2,1)S(1)}) custom-call(s32[3]{0:T(128)S(1)} %pad_add_fusion.me_ref, f32[128,1536]{1,0:T(8,128)} %get-tuple-element.36.c0, ...), custom_call_target="tpu_custom_call" | custom-call | flops 1000 | bytes 1000 | tf_op jit(solution)/shard_map/product/pallas_call | solution.py:116
  116.5 3.6 %product.5 = (f32[64,768]{1,0:T(8,128)S(1)}, f32[64,768]{1,0:T(8,128)S(1)}, f32[64,768]{1,0:T(8,128)S(1)}, f32[64,768]{1,0:T(8,128)S(1)}, bf16[256,1536]{1,0:T(8,128)(2,1)S(1)}, /*index=5*/bf16[256,1536]{1,0:T(8,128)(2,1)S(1)}) custom-call(s32[3]{0:T(128)S(1)} %pad_add_fusion.me_ref, f32[64,1536]{1,0:T(8,128)} %tie.1.c0, f32[64,1536]{1,0:T(8,128)S(1)} %copy-done.14, ...), custom_call_target="tpu_custom_call" | custom-call | flops 1000 | bytes 1000 | tf_op jit(solution)/shard_map/product/pallas_call | solution.py:116
  122.2 6.3 %collective-permute-done.19 = f32[128,768]{1,0:T(8,128)} collective-permute-done((f32[128,768]{1,0:T(8,128)}, f32[128,768]{1,0:T(8,128)}, u32[]{:S(2)}, u32[]{:S(2)}) %collective-permute-start.19) | collective-permute-done | bytes 393248 | tf_op jit(solution)/shard_map/ppermute | solution.py:51
  128.5 3.5 %collective-permute-done.20 = f32[128,768]{1,0:T(8,128)} collective-permute-done((f32[128,768]{1,0:T(8,128)}, f32[128,768]{1,0:T(8,128)}, u32[]{:S(2)}, u32[]{:S(2)}) %collective-permute-start.20) | collective-permute-done | bytes 393248 | tf_op jit(solution)/shard_map/ppermute | solution.py:51
  133.4 6.3 %collective-permute-start.22 = (f32[2,32,768]{2,1,0:T(8,128)S(1)}, f32[2,32,768]{2,1,0:T(8,128)S(1)}, u32[]{:S(2)}, u32[]{:S(2)}) collective-permute-start(f32[2,32,768]{2,1,0:T(8,128)S(1)} %dynamic-slice_bitcast_fusion.2), channel_id=1, source_target_pairs={{0,8},{1,9},{2,10},{3,11},{4,12},{5,13},{6,14},{7,15},{8,0},{9,1},... | collective-permute-start | bytes 589832 | tf_op jit(solution)/shard_map/ppermute | solution.py:51
  139.8 2.7 %collective-permute-start.29 = (f32[2,16,768]{2,1,0:T(8,128)S(1)}, f32[2,16,768]{2,1,0:T(8,128)S(1)}, u32[]{:S(2)}, u32[]{:S(2)}) collective-permute-start(f32[2,16,768]{2,1,0:T(8,128)S(1)} %dynamic-slice_bitcast_fusion.3), channel_id=1, source_target_pairs={{0,8},{1,9},{2,10},{3,11},{4,12},{5,13},{6,14},{7,15},{8,0},{9,1},... | collective-permute-start | bytes 294920 | tf_op jit(solution)/shard_map/ppermute | solution.py:51
  146.8 10.2 %collective-permute-start.31 = (f32[128,768]{1,0:T(8,128)S(1)}, f32[128,768]{1,0:T(8,128)S(1)}, u32[]{:S(2)}, u32[]{:S(2)}) collective-permute-start(f32[128,768]{1,0:T(8,128)S(1)} %get-tuple-element.59), channel_id=1, source_target_pairs={{0,0},{1,160},{2,96},{3,192},{4,128},{5,32},{6,224},{7,64},{8,16},... | collective-permute-start | bytes 1179656 | tf_op jit(solution)/shard_map/ppermute | solution.py:51
  157.0 15.1 %collective-permute-done.31.refs_6_ = f32[128,768]{1,0:T(8,128)S(1)} collective-permute-done((f32[128,768]{1,0:T(8,128)S(1)}, f32[128,768]{1,0:T(8,128)S(1)}, u32[]{:S(2)}, u32[]{:S(2)}) %collective-permute-start.31) | collective-permute-done | bytes 393248 | tf_op jit(solution)/shard_map/ppermute | solution.py:51
  173.9 2.6 %gram.1 = (f32[256,128]{1,0:T(8,128)S(1)}, f32[256,128]{1,0:T(8,128)S(1)}, f32[256,128]{1,0:T(8,128)S(1)}, f32[256,128]{1,0:T(8,128)S(1)}) custom-call(bf16[256,1536]{1,0:T(8,128)(2,1)S(1)} %copy-done.10, bf16[512,1536]{1,0:T(8,128)(2,1)S(1)} %copy-done.4, bf16[256,1536]{1,0:T(8,128)(2,1)S(1)} %get-tuple-element.48.refs_2_, ...), custom_call_target="tpu_custom_call" | custom-call | flops 1000 | bytes 1000 | tf_op jit(solution)/shard_map/gram/pallas_call | solution.py:142
  176.6 10.9 %collective-permute-start.34 = (f32[256,128]{1,0:T(8,128)S(1)}, f32[256,128]{1,0:T(8,128)S(1)}, u32[]{:S(2)}, u32[]{:S(2)}) collective-permute-start(f32[256,128]{1,0:T(8,128)S(1)} %get-tuple-element.54), channel_id=1, source_target_pairs={{0,6},{1,7},{2,0},{3,1},{4,2},{5,3},{6,4},{7,5},{8,14},{9,15},{10,... | collective-permute-start | bytes 393224 | tf_op jit(solution)/shard_map/ppermute | solution.py:51
  187.5 5.9 %collective-permute-start.35 = (f32[256,128]{1,0:T(8,128)S(1)}, f32[256,128]{1,0:T(8,128)S(1)}, u32[]{:S(2)}, u32[]{:S(2)}) collective-permute-start(f32[256,128]{1,0:T(8,128)S(1)} %get-tuple-element.55), channel_id=1, source_target_pairs={{0,4},{1,5},{2,6},{3,7},{4,0},{5,1},{6,2},{7,3},{8,12},{9,13},{10,... | collective-permute-start | bytes 393224 | tf_op jit(solution)/shard_map/ppermute | solution.py:51
  193.4 2.3 %collective-permute-done.34 = f32[256,128]{1,0:T(8,128)S(1)} collective-permute-done((f32[256,128]{1,0:T(8,128)S(1)}, f32[256,128]{1,0:T(8,128)S(1)}, u32[]{:S(2)}, u32[]{:S(2)}) %collective-permute-start.34) | collective-permute-done | bytes 131104 | tf_op jit(solution)/shard_map/ppermute | solution.py:51
  195.7 4.0 %collective-permute-done.35 = f32[256,128]{1,0:T(8,128)S(1)} collective-permute-done((f32[256,128]{1,0:T(8,128)S(1)}, f32[256,128]{1,0:T(8,128)S(1)}, u32[]{:S(2)}, u32[]{:S(2)}) %collective-permute-start.35) | collective-permute-done | bytes 131104 | tf_op jit(solution)/shard_map/ppermute | solution.py:51
  199.7 6.4 %collective-permute-start.36 = (f32[2,64,128]{2,1,0:T(8,128)S(1)}, f32[2,64,128]{2,1,0:T(8,128)S(1)}, u32[]{:S(2)}, u32[]{:S(2)}) collective-permute-start(f32[2,64,128]{2,1,0:T(8,128)S(1)} %dynamic-slice_bitcast_fusion.5), channel_id=1, source_target_pairs={{0,8},{1,9},{2,10},{3,11},{4,12},{5,13},{6,14},{7,15},{8,0},{9,1},... | collective-permute-start | bytes 196616 | tf_op jit(solution)/shard_map/ppermute | solution.py:51
  206.1 2.2 collective-permute-done.36
  209.7 3.7 %collective-permute-start.38 = (f32[128,128]{1,0:T(8,128)S(1)}, f32[128,128]{1,0:T(8,128)S(1)}, u32[]{:S(2)}, u32[]{:S(2)}) collective-permute-start(f32[128,128]{1,0:T(8,128)S(1)} %maximum_select_fusion.1), channel_id=1, source_target_pairs={{0,0},{160,1},{96,2},{192,3},{128,4},{32,5},{224,6},{64,7},{16,8},... | collective-permute-start | bytes 196616 | tf_op jit(solution)/shard_map/ppermute | solution.py:51
  214.4 9.7 %collective-permute-done.38 = f32[128,128]{1,0:T(8,128)S(1)} collective-permute-done((f32[128,128]{1,0:T(8,128)S(1)}, f32[128,128]{1,0:T(8,128)S(1)}, u32[]{:S(2)}, u32[]{:S(2)}) %collective-permute-start.38) | collective-permute-done | bytes 65568 | tf_op jit(solution)/shard_map/ppermute | solution.py:51
  (127 shorter events, 56.1 us)
Async XLA Ops:
  0.6 37.7 %collective-permute-start.11 = (f32[768,768]{1,0:T(8,128)}, f32[768,768]{1,0:T(8,128)}, u32[]{:S(2)}, u32[]{:S(2)}) collective-permute-start(f32[768,768]{1,0:T(8,128)} %param.4), channel_id=1, source_target_pairs={{0,1},{1,0},{2,3},{3,2},{4,5},{5,4},{6,7},{7,6},{8,9},{9,8},{10,11... | collective-permute-start | bytes 7077896 | tf_op jit(solution)/shard_map/ppermute | solution.py:51
  5.7 11.4 %collective-permute-start.1 = (f32[16,1536]{1,0:T(8,128)S(1)}, f32[16,1536]{1,0:T(8,128)S(1)}, u32[]{:S(2)}, u32[]{:S(2)}) collective-permute-start(f32[16,1536]{1,0:T(8,128)S(1)} %pad_maximum_fusion.2.refs_0_), channel_id=1, source_target_pairs={{0,16},{1,17},{2,18},{3,19},{4,20},{5,21},{6,22},{7,23},{8,24},{9,... | collective-permute-start | bytes 294920 | tf_op jit(solution)/shard_map/ppermute | solution.py:51
  9.0 10.5 %collective-permute-start.2 = (f32[16,1536]{1,0:T(8,128)S(1)}, f32[16,1536]{1,0:T(8,128)S(1)}, u32[]{:S(2)}, u32[]{:S(2)}) collective-permute-start(f32[16,1536]{1,0:T(8,128)S(1)} %pad_maximum_fusion.2.refs_0_), channel_id=1, source_target_pairs={{0,48},{1,49},{2,50},{3,51},{4,52},{5,53},{6,54},{7,55},{8,56},{9,... | collective-permute-start | bytes 294920 | tf_op jit(solution)/shard_map/ppermute | solution.py:51
  12.1 11.0 %collective-permute-start.3 = (f32[16,1536]{1,0:T(8,128)S(1)}, f32[16,1536]{1,0:T(8,128)S(1)}, u32[]{:S(2)}, u32[]{:S(2)}) collective-permute-start(f32[16,1536]{1,0:T(8,128)S(1)} %pad_maximum_fusion.2.refs_0_), channel_id=1, source_target_pairs={{0,32},{1,33},{2,34},{3,35},{4,36},{5,37},{6,38},{7,39},{8,40},{9,... | collective-permute-start | bytes 294920 | tf_op jit(solution)/shard_map/ppermute | solution.py:51
  23.2 9.8 %collective-permute-start.4 = (f32[48,1536]{1,0:T(8,128)S(1)}, f32[48,1536]{1,0:T(8,128)S(1)}, u32[]{:S(2)}, u32[]{:S(2)}) collective-permute-start(f32[48,1536]{1,0:T(8,128)S(1)} %get-tuple-element.29.refs_0_), channel_id=1, source_target_pairs={{0,16},{1,17},{2,18},{3,19},{4,20},{5,21},{6,22},{7,23},{8,24},{9,... | collective-permute-start | bytes 884744 | tf_op jit(solution)/shard_map/ppermute | solution.py:51
  26.9 9.0 %collective-permute-start.5 = (f32[48,1536]{1,0:T(8,128)S(1)}, f32[48,1536]{1,0:T(8,128)S(1)}, u32[]{:S(2)}, u32[]{:S(2)}) collective-permute-start(f32[48,1536]{1,0:T(8,128)S(1)} %get-tuple-element.29.refs_0_), channel_id=1, source_target_pairs={{0,48},{1,49},{2,50},{3,51},{4,52},{5,53},{6,54},{7,55},{8,56},{9,... | collective-permute-start | bytes 884744 | tf_op jit(solution)/shard_map/ppermute | solution.py:51
  27.7 14.5 %collective-permute-start.10 = (f32[64,1536]{1,0:T(8,128)S(1)}, f32[64,1536]{1,0:T(8,128)S(1)}, u32[]{:S(2)}, u32[]{:S(2)}) collective-permute-start(f32[64,1536]{1,0:T(8,128)S(1)} %get-tuple-element.30.refs_5_), channel_id=1, source_target_pairs={{0,128},{1,129},{2,130},{3,131},{4,132},{5,133},{6,134},{7,135},{8... | collective-permute-start | bytes 1179656 | tf_op jit(solution)/shard_map/ppermute | solution.py:51
  30.8 15.9 %collective-permute-start.8 = (f32[64,1536]{1,0:T(8,128)S(1)}, f32[64,1536]{1,0:T(8,128)S(1)}, u32[]{:S(2)}, u32[]{:S(2)}) collective-permute-start(f32[64,1536]{1,0:T(8,128)S(1)} %get-tuple-element.30.refs_5_), channel_id=1, source_target_pairs={{0,64},{1,65},{2,66},{3,67},{4,68},{5,69},{6,70},{7,71},{8,72},{9,... | collective-permute-start | bytes 1179656 | tf_op jit(solution)/shard_map/ppermute | solution.py:51
  33.0 13.8 %collective-permute-start.9 = (f32[64,1536]{1,0:T(8,128)S(1)}, f32[64,1536]{1,0:T(8,128)S(1)}, u32[]{:S(2)}, u32[]{:S(2)}) collective-permute-start(f32[64,1536]{1,0:T(8,128)S(1)} %get-tuple-element.30.refs_5_), channel_id=1, source_target_pairs={{0,192},{1,193},{2,194},{3,195},{4,196},{5,197},{6,198},{7,199},{8... | collective-permute-start | bytes 1179656 | tf_op jit(solution)/shard_map/ppermute | solution.py:51
  35.9 11.0 %collective-permute-start.6 = (f32[24,1536]{1,0:T(8,128)S(1)}, f32[24,1536]{1,0:T(8,128)S(1)}, u32[]{:S(2)}, u32[]{:S(2)}) collective-permute-start(f32[24,1536]{1,0:T(8,128)S(1)} %slice.26), channel_id=1, source_target_pairs={{0,16},{1,17},{2,18},{3,19},{4,20},{5,21},{6,22},{7,23},{8,24},{9,... | collective-permute-start | bytes 442376 | tf_op jit(solution)/shard_map/ppermute | solution.py:51
  38.3 8.5 %collective-permute-start.7 = (f32[24,1536]{1,0:T(8,128)S(1)}, f32[24,1536]{1,0:T(8,128)S(1)}, u32[]{:S(2)}, u32[]{:S(2)}) collective-permute-start(f32[24,1536]{1,0:T(8,128)S(1)} %slice.27), channel_id=1, source_target_pairs={{0,48},{1,49},{2,50},{3,51},{4,52},{5,53},{6,54},{7,55},{8,56},{9,... | collective-permute-start | bytes 442376 | tf_op jit(solution)/shard_map/ppermute | solution.py:51
  54.2 12.2 %collective-permute-start.13 = (f32[64,768]{1,0:T(8,128)}, f32[64,768]{1,0:T(8,128)}, u32[]{:S(2)}, u32[]{:S(2)}) collective-permute-start(f32[64,768]{1,0:T(8,128)} %get-tuple-element.34), channel_id=1, source_target_pairs={{0,6},{1,7},{2,0},{3,1},{4,2},{5,3},{6,4},{7,5},{8,14},{9,15},{10,... | collective-permute-start | bytes 589832 | tf_op jit(solution)/shard_map/ppermute | solution.py:51
  56.0 10.4 %collective-permute-start.14 = (f32[64,768]{1,0:T(8,128)}, f32[64,768]{1,0:T(8,128)}, u32[]{:S(2)}, u32[]{:S(2)}) collective-permute-start(f32[64,768]{1,0:T(8,128)} %get-tuple-element.35), channel_id=1, source_target_pairs={{0,4},{1,5},{2,6},{3,7},{4,0},{5,1},{6,2},{7,3},{8,12},{9,13},{10,... | collective-permute-start | bytes 589832 | tf_op jit(solution)/shard_map/ppermute | solution.py:51
  57.3 36.8 %collective-permute-start.16 = (f32[128,1536]{1,0:T(8,128)}, f32[128,1536]{1,0:T(8,128)}, u32[]{:S(2)}, u32[]{:S(2)}) collective-permute-start(f32[128,1536]{1,0:T(8,128)} %get-tuple-element.36.c0), channel_id=1, source_target_pairs={{0,64},{1,65},{2,66},{3,67},{4,68},{5,69},{6,70},{7,71},{8,72},{9,... | collective-permute-start | bytes 2359304 | tf_op jit(solution)/shard_map/ppermute | solution.py:51
  58.7 35.3 %collective-permute-start.17 = (f32[128,1536]{1,0:T(8,128)}, f32[128,1536]{1,0:T(8,128)}, u32[]{:S(2)}, u32[]{:S(2)}) collective-permute-start(f32[128,1536]{1,0:T(8,128)} %get-tuple-element.36.c0), channel_id=1, source_target_pairs={{0,192},{1,193},{2,194},{3,195},{4,196},{5,197},{6,198},{7,199},{8... | collective-permute-start | bytes 2359304 | tf_op jit(solution)/shard_map/ppermute | solution.py:51
  62.5 31.6 %collective-permute-start.18 = (f32[128,1536]{1,0:T(8,128)}, f32[128,1536]{1,0:T(8,128)}, u32[]{:S(2)}, u32[]{:S(2)}) collective-permute-start(f32[128,1536]{1,0:T(8,128)} %get-tuple-element.36.c0), channel_id=1, source_target_pairs={{0,128},{1,129},{2,130},{3,131},{4,132},{5,133},{6,134},{7,135},{8... | collective-permute-start | bytes 2359304 | tf_op jit(solution)/shard_map/ppermute | solution.py:51
  94.1 17.2 %collective-permute-start.23 = (f32[64,1536]{1,0:T(8,128)}, f32[64,1536]{1,0:T(8,128)S(1)}, u32[]{:S(2)}, u32[]{:S(2)}) collective-permute-start(f32[64,1536]{1,0:T(8,128)} %tie.1.c0), channel_id=1, source_target_pairs={{0,64},{1,65},{2,66},{3,67},{4,68},{5,69},{6,70},{7,71},{8,72},{9,... | collective-permute-start | bytes 1179656 | tf_op jit(solution)/shard_map/ppermute | solution.py:51
  95.1 19.1 %collective-permute-start.24 = (f32[64,1536]{1,0:T(8,128)}, f32[64,1536]{1,0:T(8,128)}, u32[]{:S(2)}, u32[]{:S(2)}) collective-permute-start(f32[64,1536]{1,0:T(8,128)} %tie.1.c0), channel_id=1, source_target_pairs={{0,192},{1,193},{2,194},{3,195},{4,196},{5,197},{6,198},{7,199},{8... | collective-permute-start | bytes 1179656 | tf_op jit(solution)/shard_map/ppermute | solution.py:51
  97.4 16.8 %collective-permute-start.25 = (f32[64,1536]{1,0:T(8,128)}, f32[64,1536]{1,0:T(8,128)}, u32[]{:S(2)}, u32[]{:S(2)}) collective-permute-start(f32[64,1536]{1,0:T(8,128)} %tie.1.c0), channel_id=1, source_target_pairs={{0,128},{1,129},{2,130},{3,131},{4,132},{5,133},{6,134},{7,135},{8... | collective-permute-start | bytes 1179656 | tf_op jit(solution)/shard_map/ppermute | solution.py:51
  109.1 19.4 %collective-permute-start.19 = (f32[128,768]{1,0:T(8,128)}, f32[128,768]{1,0:T(8,128)}, u32[]{:S(2)}, u32[]{:S(2)}) collective-permute-start(f32[128,768]{1,0:T(8,128)} %get-tuple-element.38), channel_id=1, source_target_pairs={{0,2},{1,3},{2,4},{3,5},{4,6},{5,7},{6,0},{7,1},{8,10},{9,11},{10,... | collective-permute-start | bytes 1179656 | tf_op jit(solution)/shard_map/ppermute | solution.py:51
  111.3 20.7 %collective-permute-start.20 = (f32[128,768]{1,0:T(8,128)}, f32[128,768]{1,0:T(8,128)}, u32[]{:S(2)}, u32[]{:S(2)}) collective-permute-start(f32[128,768]{1,0:T(8,128)} %get-tuple-element.39), channel_id=1, source_target_pairs={{0,6},{1,7},{2,0},{3,1},{4,2},{5,3},{6,4},{7,5},{8,14},{9,15},{10,... | collective-permute-start | bytes 1179656 | tf_op jit(solution)/shard_map/ppermute | solution.py:51
  112.1 19.9 %collective-permute-start.21 = (f32[128,768]{1,0:T(8,128)}, f32[128,768]{1,0:T(8,128)}, u32[]{:S(2)}, u32[]{:S(2)}) collective-permute-start(f32[128,768]{1,0:T(8,128)} %get-tuple-element.40), channel_id=1, source_target_pairs={{0,4},{1,5},{2,6},{3,7},{4,0},{5,1},{6,2},{7,3},{8,12},{9,13},{10,... | collective-permute-start | bytes 1179656 | tf_op jit(solution)/shard_map/ppermute | solution.py:51
  120.1 19.6 %collective-permute-start.26 = (f32[64,768]{1,0:T(8,128)S(1)}, f32[64,768]{1,0:T(8,128)S(1)}, u32[]{:S(2)}, u32[]{:S(2)}) collective-permute-start(f32[64,768]{1,0:T(8,128)S(1)} %get-tuple-element.43), channel_id=1, source_target_pairs={{0,2},{1,3},{2,4},{3,5},{4,6},{5,7},{6,0},{7,1},{8,10},{9,11},{10,... | collective-permute-start | bytes 589832 | tf_op jit(solution)/shard_map/ppermute | solution.py:51
  121.6 18.0 %collective-permute-start.27 = (f32[64,768]{1,0:T(8,128)S(1)}, f32[64,768]{1,0:T(8,128)S(1)}, u32[]{:S(2)}, u32[]{:S(2)}) collective-permute-start(f32[64,768]{1,0:T(8,128)S(1)} %get-tuple-element.44), channel_id=1, source_target_pairs={{0,6},{1,7},{2,0},{3,1},{4,2},{5,3},{6,4},{7,5},{8,14},{9,15},{10,... | collective-permute-start | bytes 589832 | tf_op jit(solution)/shard_map/ppermute | solution.py:51
  128.5 11.2 %collective-permute-start.28 = (f32[64,768]{1,0:T(8,128)S(1)}, f32[64,768]{1,0:T(8,128)S(1)}, u32[]{:S(2)}, u32[]{:S(2)}) collective-permute-start(f32[64,768]{1,0:T(8,128)S(1)} %get-tuple-element.45), channel_id=1, source_target_pairs={{0,4},{1,5},{2,6},{3,7},{4,0},{5,1},{6,2},{7,3},{8,12},{9,13},{10,... | collective-permute-start | bytes 589832 | tf_op jit(solution)/shard_map/ppermute | solution.py:51
  133.4 9.9 %collective-permute-start.22 = (f32[2,32,768]{2,1,0:T(8,128)S(1)}, f32[2,32,768]{2,1,0:T(8,128)S(1)}, u32[]{:S(2)}, u32[]{:S(2)}) collective-permute-start(f32[2,32,768]{2,1,0:T(8,128)S(1)} %dynamic-slice_bitcast_fusion.2), channel_id=1, source_target_pairs={{0,8},{1,9},{2,10},{3,11},{4,12},{5,13},{6,14},{7,15},{8,0},{9,1},... | collective-permute-start | bytes 589832 | tf_op jit(solution)/shard_map/ppermute | solution.py:51
  146.8 25.4 %collective-permute-start.31 = (f32[128,768]{1,0:T(8,128)S(1)}, f32[128,768]{1,0:T(8,128)S(1)}, u32[]{:S(2)}, u32[]{:S(2)}) collective-permute-start(f32[128,768]{1,0:T(8,128)S(1)} %get-tuple-element.59), channel_id=1, source_target_pairs={{0,0},{1,160},{2,96},{3,192},{4,128},{5,32},{6,224},{7,64},{8,16},... | collective-permute-start | bytes 1179656 | tf_op jit(solution)/shard_map/ppermute | solution.py:51
  176.5 16.9 %collective-permute-start.33 = (f32[256,128]{1,0:T(8,128)S(1)}, f32[256,128]{1,0:T(8,128)S(1)}, u32[]{:S(2)}, u32[]{:S(2)}) collective-permute-start(f32[256,128]{1,0:T(8,128)S(1)} %get-tuple-element.53), channel_id=1, source_target_pairs={{0,2},{1,3},{2,4},{3,5},{4,6},{5,7},{6,0},{7,1},{8,10},{9,11},{10,... | collective-permute-start | bytes 393224 | tf_op jit(solution)/shard_map/ppermute | solution.py:51
  176.6 19.1 %collective-permute-start.34 = (f32[256,128]{1,0:T(8,128)S(1)}, f32[256,128]{1,0:T(8,128)S(1)}, u32[]{:S(2)}, u32[]{:S(2)}) collective-permute-start(f32[256,128]{1,0:T(8,128)S(1)} %get-tuple-element.54), channel_id=1, source_target_pairs={{0,6},{1,7},{2,0},{3,1},{4,2},{5,3},{6,4},{7,5},{8,14},{9,15},{10,... | collective-permute-start | bytes 393224 | tf_op jit(solution)/shard_map/ppermute | solution.py:51
  187.5 12.2 %collective-permute-start.35 = (f32[256,128]{1,0:T(8,128)S(1)}, f32[256,128]{1,0:T(8,128)S(1)}, u32[]{:S(2)}, u32[]{:S(2)}) collective-permute-start(f32[256,128]{1,0:T(8,128)S(1)} %get-tuple-element.55), channel_id=1, source_target_pairs={{0,4},{1,5},{2,6},{3,7},{4,0},{5,1},{6,2},{7,3},{8,12},{9,13},{10,... | collective-permute-start | bytes 393224 | tf_op jit(solution)/shard_map/ppermute | solution.py:51
  199.7 8.6 %collective-permute-start.36 = (f32[2,64,128]{2,1,0:T(8,128)S(1)}, f32[2,64,128]{2,1,0:T(8,128)S(1)}, u32[]{:S(2)}, u32[]{:S(2)}) collective-permute-start(f32[2,64,128]{2,1,0:T(8,128)S(1)} %dynamic-slice_bitcast_fusion.5), channel_id=1, source_target_pairs={{0,8},{1,9},{2,10},{3,11},{4,12},{5,13},{6,14},{7,15},{8,0},{9,1},... | collective-permute-start | bytes 196616 | tf_op jit(solution)/shard_map/ppermute | solution.py:51
  209.7 14.4 %collective-permute-start.38 = (f32[128,128]{1,0:T(8,128)S(1)}, f32[128,128]{1,0:T(8,128)S(1)}, u32[]{:S(2)}, u32[]{:S(2)}) collective-permute-start(f32[128,128]{1,0:T(8,128)S(1)} %maximum_select_fusion.1), channel_id=1, source_target_pairs={{0,0},{160,1},{96,2},{192,3},{128,4},{32,5},{224,6},{64,7},{16,8},... | collective-permute-start | bytes 196616 | tf_op jit(solution)/shard_map/ppermute | solution.py:51
  (29 other events, 306.0 us)
where the time goes:
time: 225 us
  starting transfers between devices  97.6 us (43%)
  waiting for transfers between devices  85.5 us (38%)
  Pallas kernels  18.2 us (8%)
  local copies, waits for them, and re-layouts  14.2 us (6%)
  other arithmetic  6.86 us (3%)
  between operations  2.31 us (1%)
    ppermute x39, starting transfers between devices, send(): return lax.ppermute(value, AXES, pairs)  97.6 us
    ppermute x39, waiting for transfers between devices, send(): return lax.ppermute(value, AXES, pairs)  85.5 us
    pallas_call x3, Pallas kernels, product(): pl.pallas_call(functools.partial(product_kernel, rows), out_shape=[jax.Sh...  14.6 us
    unnamed x46, local copies, waits for them, and re-layouts  12.1 us
  transfers between devices with their start and end apart: 39, of which 22 were waited for; matrix products, arithmetic and copies ran while one was open for 5% of the time, Pallas kernels for 5%

commit v1 on v0

--- a/solution.py
+++ b/solution.py
@@ -9,13 +9,14 @@
 
 BS = 768
 AXES = ("prow", "pcol")
-SIZES = (16, 32, 16)
-FROM = (0, 16, 48)
+SIZES = (32, 32)
+FROM = (0, 32)
 STEPS = (0, 1, -1, 2)
 COST = pl.CostEstimate(flops=1000, bytes_accessed=1000, transcendentals=0)
 VMEM = pl.BlockSpec(memory_space=pltpu.VMEM)
 SMEM = pl.BlockSpec(memory_space=pltpu.SMEM)
 ANY = pl.BlockSpec(memory_space=pl.ANY)
+HBM = pl.BlockSpec(memory_space=pltpu.HBM)
 
 
 def places():
@@ -91,7 +92,11 @@
     return jnp.where(step == 3, 2, jnp.where(step == 2, 3, step))
 
 
-def product_kernel(rows, me_ref, c0, c1, c2, c3, h0, l0, h1, l1, o0, o1, o2, o3, high, low):
+def product_kernel(rows, me_ref, c0, c1, c2, c3, h0, l0, h1, l1, *refs):
+    outs, high_out, low_out, high, low, sep, sems = refs[:4], refs[4], refs[5], refs[6], refs[7], refs[8:12], refs[12]
+    loads = [pltpu.make_async_copy(src, dst, sems.at[i]) for i, (src, dst) in enumerate(zip((h0, l0, h1, l1), sep))]
+    for load in loads:
+        load.start()
     x, zh, y = me_ref[0], me_ref[1], me_ref[2]
     for sx, ref in enumerate((c0, c1, c2, c3)):
         for sz in range(4):
@@ -101,14 +106,22 @@
             place = (to * 2 + xs // 2) * 2 + lax.rem(zs, 2)
             at = pl.ds(pl.multiple_of(place * rows, rows), rows)
             store_split(high, low, (at, slice(None)), ref[sz * rows : (sz + 1) * rows, :])
+    stores = [pltpu.make_async_copy(high, high_out, sems.at[4]), pltpu.make_async_copy(low, low_out, sems.at[5])]
+    for store in stores:
+        store.start()
+    for load in loads:
+        load.wait()
+    h0, l0, h1, l1 = sep
     own, other = slice(0, BS), slice(BS, 2 * BS)
     for n in range(0, BS, 256):
         cols = slice(n, n + 256)
         sums = dot_nt(high[:, own], h0[cols, :]) + dot_nt(high[:, other], h1[cols, :])
         sums += dot_nt(low[:, own], h0[cols, :]) + dot_nt(low[:, other], h1[cols, :])
         sums += dot_nt(high[:, own], l0[cols, :]) + dot_nt(high[:, other], l1[cols, :])
-        for i, out in enumerate((o0, o1, o2, o3)):
+        for i, out in enumerate(outs):
             out[:, cols] = sums[4 * rows * i : 4 * rows * (i + 1)]
+    for store in stores:
+        store.wait()
 
 
 def product(me, parts, sep):
@@ -117,38 +130,54 @@
         functools.partial(product_kernel, rows),
         out_shape=[jax.ShapeDtypeStruct((4 * rows, BS), jnp.float32)] * 4
         + [jax.ShapeDtypeStruct((16 * rows, 2 * BS), jnp.bfloat16)] * 2,
-        in_specs=[SMEM] + [VMEM] * 8,
-        out_specs=[VMEM] * 6,
+        in_specs=[SMEM] + [VMEM] * 4 + [HBM] * 4,
+        out_specs=[VMEM] * 4 + [HBM] * 2,
+        scratch_shapes=[pltpu.VMEM((16 * rows, 2 * BS), jnp.bfloat16)] * 2
+        + [pltpu.VMEM((BS, BS), jnp.bfloat16)] * 4
+        + [pltpu.SemaphoreType.DMA((6,))],
         compiler_params=pltpu.CompilerParams(vmem_limit_bytes=18 << 20),
         cost_estimate=COST,
         name="product",
     )(me, *parts, *sep)
-    return outs[:4], outs[4:]
+    return list(outs[:4]), outs[4:]
 
 
 def gram_kernel(*refs):
-    high, low, own, other, outs, chigh, clow = refs[0:3], refs[3:6], refs[6], refs[7], refs[8:12], refs[12], refs[13]
-    store_split(chigh, clow, (slice(None), slice(0, BS)), own[...])
-    store_split(chigh, clow, (slice(None), slice(BS, 2 * BS)), other[...])
+    panels, columns, outs, held, chigh, clow, sems = refs[:4], refs[4:8], refs[8:12], refs[12:16], refs[16], refs[17], refs[18]
+    loads = [pltpu.make_async_copy(src, dst, sems.at[i]) for i, (src, dst) in enumerate(zip(panels, held))]
+    for load in loads:
+        load.start()
+    at = 0
+    for half in range(2):
+        for group, rows in enumerate(SIZES):
+            for i in range(2):
+                value = columns[2 * group + i][rows * half : rows * (half + 1), :]
+                store_split(chigh, clow, (slice(at, at + rows), slice(BS * i, BS * (i + 1))), value)
+            at += rows
     for t, rows in enumerate(SIZES):
-        sums = dot_nt(high[t][...], chigh[...]) + dot_nt(low[t][...], chigh[...]) + dot_nt(high[t][...], clow[...])
+        loads[2 * t].wait()
+        loads[2 * t + 1].wait()
+        high, low = held[2 * t][...], held[2 * t + 1][...]
+        sums = dot_nt(high, chigh[...]) + dot_nt(low, chigh[...]) + dot_nt(high, clow[...])
         for i, out in enumerate(outs):
             for e in range(4):
                 at = 64 * e + FROM[t]
                 out[at : at + rows, :] = sums[(4 * i + e) * rows : (4 * i + e + 1) * rows]
 
 
-def gram_parts(panels, own, other):
+def gram_parts(panels, columns):
     return pl.pallas_call(
         gram_kernel,
         out_shape=[jax.ShapeDtypeStruct((256, 128), jnp.float32)] * 4,
-        in_specs=[VMEM] * 8,
+        in_specs=[HBM] * 4 + [VMEM] * 4,
         out_specs=[VMEM] * 4,
-        scratch_shapes=[pltpu.VMEM((128, 2 * BS), jnp.bfloat16)] * 2,
+        scratch_shapes=[pltpu.VMEM((16 * rows, 2 * BS), jnp.bfloat16) for rows in SIZES for i in range(2)]
+        + [pltpu.VMEM((128, 2 * BS), jnp.bfloat16)] * 2
+        + [pltpu.SemaphoreType.DMA((4,))],
         compiler_params=pltpu.CompilerParams(vmem_limit_bytes=14 << 20),
         cost_estimate=COST,
         name="gram",
-    )(*[p[0] for p in panels], *[p[1] for p in panels], own, other)
+    )(*[p for panel in panels for p in panel], *columns)
 
 
 def join_kernel(sizes, parts, *refs):
@@ -207,6 +236,10 @@
         part = part.reshape(2, 2, -1, BS)
         return keep_r * (pick(part, zl) + send(pick(part, 1 - zl), shift(dzl=1)))
 
+    def whole(value):
+        mine, theirs = pick(value, core), send(pick(value, 1 - core), swap)
+        return jnp.where(first, jnp.concatenate([mine, theirs]), jnp.concatenate([theirs, mine]))
+
     panel_t = (panel * keep_c).T
     low, high = panel_t[:64], panel_t[64:]
     mine = jnp.where(first, low, high)
@@ -218,24 +251,20 @@
     lead, rest = mine[: SIZES[0]], mine[SIZES[0] :]
     rest, col0 = join(ring_gather(lead, "dzh"), SIZES[:1], [rest])
     x0 = ring_gather(col0, "dx")
-    x0[0], col1, col2 = join(ring_forward(rest, "dzh"), SIZES[1:], [col0], [*x0[1:], *sep[2:]])
+    col0, col1 = join(ring_forward(rest, "dzh"), SIZES[1:], [col0], [*x0[1:], *sep])
     x1 = ring_gather(col1, "dx")
+    x0[0] = col0
     out0, panel0 = product(me, x0, sep)
-    own = [from_chips(ring_scatter(out0, "dy"))]
-    x2 = ring_gather(tie(col2, *x1[1:], own[0]), "dx")
     out1, panel1 = product(me, x1, sep)
-    sums1 = ring_scatter(out1, "dy")
-    out2, panel2 = product(me, x2, sep)
-    sums2 = ring_scatter(out2, "dy")
-    own += [from_chips(sums1), from_chips(sums2)]
-
-    def whole(value):
-        mine, theirs = pick(value, core), send(pick(value, 1 - core), swap)
-        return jnp.where(first, jnp.concatenate([mine, theirs]), jnp.concatenate([theirs, mine]))
-
-    kept = whole(jnp.concatenate(own, axis=1))
-    column = send(kept, TO_COLUMN)
-    gram = gram_parts((panel0, panel1, panel2), column, send(column, swap))
+    out0[0] = tie(out0[0], out1[0])
+    kept0 = whole(from_chips(ring_scatter(out0, "dy")))
+    column0 = send(kept0, TO_COLUMN)
+    out1[0] = tie(out1[0], column0)
+    kept1 = whole(from_chips(ring_scatter(out1, "dy")))
+    column1 = send(kept1, TO_COLUMN)
+    columns = [column0, send(column0, swap), column1, send(column1, swap)]
+    gram = gram_parts((panel0, panel1), columns)
+    kept = jnp.concatenate([kept0[:32], kept1[:32], kept0[32:], kept1[32:]])
     off_diagonal = -kept.T
     gram = ring_scatter(gram, "dy").reshape(2, 2, 64, 128)
     gram = whole(pick(gram, zl) + send(pick(gram, 1 - zl), shift(dzl=1)))

time: 225 us -> 230 us (1.022)
  waiting for transfers between devices: 85.5 us -> 112 us
  starting transfers between devices: 97.6 us -> 72.1 us
  Pallas kernels: 18.2 us -> 21.4 us
    ppermute x39 -> x35, waiting for transfers between devices: 85.5 us -> 112 us  [send(): return lax.ppermute(value, AXES, pairs)]
    ppermute x39 -> x35, starting transfers between devices: 97.6 us -> 72.1 us  [send(): return lax.ppermute(value, AXES, pairs)]
    pallas_call x1, Pallas kernels: 2.58 us -> 5.69 us  [gram_parts(): pl.pallas_call(gram_kernel, out_shape=[jax.ShapeDtypeStruct((256, 128), j...]
    unnamed x46 -> x58, local copies, waits for them, and re-layouts: 12.1 us -> 14.8 us
    pallas_call x3 -> x2, Pallas kernels: 14.6 us -> 14.7 us  [product(): pl.pallas_call(functools.partial(product_kernel, rows), out_shape=[jax.Sh...]
  transfers between devices with their start and end apart: 39 -> 35, of which waited for: 22 -> 21; matrix products, arithmetic and copies ran while one was open for 5% -> 3% of each run, Pallas kernels for 5% -> 6%
where the time goes in v1:
time: 230 us
  waiting for transfers between devices  112 us (49%)
  starting transfers between devices  72.1 us (31%)
  Pallas kernels  21.4 us (9%)
  local copies, waits for them, and re-layouts  16.3 us (7%)
  other arithmetic  5.73 us (2%)
  between operations  2.42 us (1%)
    ppermute x35, waiting for transfers between devices, send(): return lax.ppermute(value, AXES, pairs)  112 us
    ppermute x35, starting transfers between devices, send(): return lax.ppermute(value, AXES, pairs)  72.1 us
    unnamed x58, local copies, waits for them, and re-layouts  14.8 us
    pallas_call x2, Pallas kernels, product(): pl.pallas_call(functools.partial(product_kernel, rows), out_shape=[jax.Sh...  14.7 us
    pallas_call x1, Pallas kernels, gram_parts(): pl.pallas_call(gram_kernel, out_shape=[jax.ShapeDtypeStruct((256, 128), j...  5.69 us
  transfers between devices with their start and end apart: 35, of which 21 were waited for; matrix products, arithmetic and copies ran while one was open for 3% of the time, Pallas kernels for 6%

profile of v1, /device:TPU:24, one launch (start us, length us, event | category | flops | bytes accessed | tf_op | source)
XLA Modules:
  0.0 229.8 jit_solution(13509410550666830629)
XLA Ops:
  5.7 7.3 %collective-permute-start.3 = (f32[32,1536]{1,0:T(8,128)S(1)}, f32[32,1536]{1,0:T(8,128)S(1)}, u32[]{:S(2)}, u32[]{:S(2)}) collective-permute-start(f32[32,1536]{1,0:T(8,128)S(1)} %get-tuple-element.49.refs_0_), channel_id=1, source_target_pairs={{0,32},{1,33},{2,34},{3,35},{4,36},{5,37},{6,38},{7,39},{8,40},{9,... | collective-permute-start | bytes 589832 | tf_op jit(solution)/shard_map/ppermute | solution.py:52
  12.9 2.9 %collective-permute-start.1 = (f32[32,1536]{1,0:T(8,128)S(1)}, f32[32,1536]{1,0:T(8,128)S(1)}, u32[]{:S(2)}, u32[]{:S(2)}) collective-permute-start(f32[32,1536]{1,0:T(8,128)S(1)} %get-tuple-element.49.refs_0_), channel_id=1, source_target_pairs={{0,16},{1,17},{2,18},{3,19},{4,20},{5,21},{6,22},{7,23},{8,24},{9,... | collective-permute-start | bytes 589832 | tf_op jit(solution)/shard_map/ppermute | solution.py:52
  15.9 5.6 %collective-permute-done.3.refs_3_ = f32[32,1536]{1,0:T(8,128)S(1)} collective-permute-done((f32[32,1536]{1,0:T(8,128)S(1)}, f32[32,1536]{1,0:T(8,128)S(1)}, u32[]{:S(2)}, u32[]{:S(2)}) %collective-permute-start.3) | collective-permute-done | bytes 196640 | tf_op jit(solution)/shard_map/ppermute | solution.py:52
  21.4 10.2 %collective-permute-done.2.refs_2_ = f32[32,1536]{1,0:T(8,128)S(1)} collective-permute-done((f32[32,1536]{1,0:T(8,128)S(1)}, f32[32,1536]{1,0:T(8,128)S(1)}, u32[]{:S(2)}, u32[]{:S(2)}) %collective-permute-start.2) | collective-permute-done | bytes 196640 | tf_op jit(solution)/shard_map/ppermute | solution.py:52
  31.7 3.1 %collective-permute-start.5 = (f32[32,1536]{1,0:T(8,128)S(1)}, f32[32,1536]{1,0:T(8,128)S(1)}, u32[]{:S(2)}, u32[]{:S(2)}) collective-permute-start(f32[32,1536]{1,0:T(8,128)S(1)} %get-tuple-element.22.refs_0_), channel_id=1, source_target_pairs={{0,48},{1,49},{2,50},{3,51},{4,52},{5,53},{6,54},{7,55},{8,56},{9,... | collective-permute-start | bytes 589832 | tf_op jit(solution)/shard_map/ppermute | solution.py:52
  34.8 3.0 %collective-permute-start.10 = (f32[128,1536]{1,0:T(8,128)S(1)}, f32[128,1536]{1,0:T(8,128)S(1)}, u32[]{:S(2)}, u32[]{:S(2)}) collective-permute-start(f32[128,1536]{1,0:T(8,128)S(1)} %get-tuple-element.23.refs_5_), channel_id=1, source_target_pairs={{0,128},{1,129},{2,130},{3,131},{4,132},{5,133},{6,134},{7,135},{8... | collective-permute-start | bytes 2359304 | tf_op jit(solution)/shard_map/ppermute | solution.py:52
  39.9 2.4 %collective-permute-done.5.refs_2_ = f32[32,1536]{1,0:T(8,128)S(1)} collective-permute-done((f32[32,1536]{1,0:T(8,128)S(1)}, f32[32,1536]{1,0:T(8,128)S(1)}, u32[]{:S(2)}, u32[]{:S(2)}) %collective-permute-start.5) | collective-permute-done | bytes 196640 | tf_op jit(solution)/shard_map/ppermute | solution.py:52
  43.2 12.2 %collective-permute-done.4.refs_1_ = f32[32,1536]{1,0:T(8,128)S(1)} collective-permute-done((f32[32,1536]{1,0:T(8,128)S(1)}, f32[32,1536]{1,0:T(8,128)S(1)}, u32[]{:S(2)}, u32[]{:S(2)}) %collective-permute-start.4) | collective-permute-done | bytes 196640 | tf_op jit(solution)/shard_map/ppermute | solution.py:52
  55.5 3.0 %collective-permute-start.6 = (f32[16,1536]{1,0:T(8,128)S(1)}, f32[16,1536]{1,0:T(8,128)S(1)}, u32[]{:S(2)}, u32[]{:S(2)}) collective-permute-start(f32[16,1536]{1,0:T(8,128)S(1)} %slice.44), channel_id=1, source_target_pairs={{0,16},{1,17},{2,18},{3,19},{4,20},{5,21},{6,22},{7,23},{8,24},{9,... | collective-permute-start | bytes 294920 | tf_op jit(solution)/shard_map/ppermute | solution.py:52
  58.5 2.0 fusion.1
  62.8 9.3 %collective-permute-done.9.refs_7_.c2 = f32[128,1536]{1,0:T(8,128)S(1)} collective-permute-done((f32[128,1536]{1,0:T(8,128)S(1)}, f32[128,1536]{1,0:T(8,128)S(1)}, u32[]{:S(2)}, u32[]{:S(2)}) %collective-permute-start.9) | collective-permute-done | bytes 786464 | tf_op jit(solution)/shard_map/ppermute | solution.py:52
  74.4 2.6 %collective-permute-start.14 = (f32[128,1536]{1,0:T(8,128)}, f32[128,1536]{1,0:T(8,128)}, u32[]{:S(2)}, u32[]{:S(2)}) collective-permute-start(f32[128,1536]{1,0:T(8,128)} %get-tuple-element.26.c0), channel_id=1, source_target_pairs={{0,128},{1,129},{2,130},{3,131},{4,132},{5,133},{6,134},{7,135},{8... | collective-permute-start | bytes 2359304 | tf_op jit(solution)/shard_map/ppermute | solution.py:52
  84.9 7.2 %product.2 = (f32[128,768]{1,0:T(8,128)S(1)}, f32[128,768]{1,0:T(8,128)}, f32[128,768]{1,0:T(8,128)}, f32[128,768]{1,0:T(8,128)}, bf16[512,1536]{1,0:T(8,128)(2,1)S(1)}, /*index=5*/bf16[512,1536]{1,0:T(8,128)(2,1)S(1)}) custom-call(s32[3]{0:T(128)S(1)} %pad_add_fusion.me_ref, f32[128,1536]{1,0:T(8,128)S(1)} %copy-done.12, f32[128,1536]{1,0:T(8,128)S(1)} %copy-done.10, ...), custom_call_target="tpu_custom_call" | custom-call | flops 1000 | bytes 1000 | tf_op jit(solution)/shard_map/product/pallas_call | solution.py:129
  98.5 14.0 %collective-permute-done.13.c2 = f32[128,1536]{1,0:T(8,128)} collective-permute-done((f32[128,1536]{1,0:T(8,128)}, f32[128,1536]{1,0:T(8,128)}, u32[]{:S(2)}, u32[]{:S(2)}) %collective-permute-start.13) | collective-permute-done | bytes 786464 | tf_op jit(solution)/shard_map/ppermute | solution.py:52
  113.8 7.5 %product.3 = (f32[128,768]{1,0:T(8,128)S(1)}, f32[128,768]{1,0:T(8,128)S(1)}, f32[128,768]{1,0:T(8,128)S(1)}, f32[128,768]{1,0:T(8,128)S(1)}, bf16[512,1536]{1,0...) custom-call(s32[3]{0:T(128)S(1)} %pad_add_fusion.me_ref, f32[128,1536]{1,0:T(8,128)} %get-tuple-element.26.c0, ...), custom_call_target="tpu_custom_call" | custom-call | flops 1000 | bytes 1000 | tf_op jit(solution)/shard_map/product/pallas_call | solution.py:129
  122.5 2.3 %add_add_fusion.1 = f32[128,768]{1,0:T(8,128)S(1)} fusion(f32[128,768]{1,0:T(8,128)} %collective-permute-done.16, f32[128,768]{1,0:T(8,128)} %collective-permute-done.17, f32[128,768]{1,0:T(8,128)S(1)} %tie.2, f32[128,768]{1,0:T(8,128)} %collective-permute-done.15), kind=kLoop, calls=%fused_computation.11 | loop fusion | flops 294912 | bytes 1966080 | tf_op jit(solution)/shard_map/add | solution.py:68
  125.7 5.7 %collective-permute-done.18 = f32[2,32,768]{2,1,0:T(8,128)S(1)} collective-permute-done((f32[2,32,768]{2,1,0:T(8,128)S(1)}, f32[2,32,768]{2,1,0:T(8,128)S(1)}, u32[]{:S(2)}, u32[]{:S(2)}) %collective-permute-start.18) | collective-permute-done | bytes 196640 | tf_op jit(solution)/shard_map/ppermute | solution.py:52
  135.0 7.9 %collective-permute-start.20 = (f32[64,768]{1,0:T(8,128)S(1)}, f32[64,768]{1,0:T(8,128)S(1)}, u32[]{:S(2)}, u32[]{:S(2)}) collective-permute-start(f32[64,768]{1,0:T(8,128)S(1)} %maximum_select_fusion), channel_id=1, source_target_pairs={{0,0},{1,160},{2,96},{3,192},{4,128},{5,32},{6,224},{7,64},{8,16},... | collective-permute-start | bytes 589832 | tf_op jit(solution)/shard_map/ppermute | solution.py:52
  142.9 9.8 %collective-permute-done.20.refs_1_.refs_4_ = f32[64,768]{1,0:T(8,128)S(1)} collective-permute-done((f32[64,768]{1,0:T(8,128)S(1)}, f32[64,768]{1,0:T(8,128)S(1)}, u32[]{:S(2)}, u32[]{:S(2)}) %collective-permute-start.20) | collective-permute-done | bytes 196640 | tf_op jit(solution)/shard_map/ppermute | solution.py:52
  152.8 4.4 %collective-permute-done.22 = f32[128,768]{1,0:T(8,128)S(1)} collective-permute-done((f32[128,768]{1,0:T(8,128)}, f32[128,768]{1,0:T(8,128)S(1)}, u32[]{:S(2)}, u32[]{:S(2)}) %collective-permute-start.22) | collective-permute-done | bytes 393248 | tf_op jit(solution)/shard_map/ppermute | solution.py:52
  158.3 5.1 %collective-permute-done.24 = f32[2,32,768]{2,1,0:T(8,128)S(1)} collective-permute-done((f32[2,32,768]{2,1,0:T(8,128)S(1)}, f32[2,32,768]{2,1,0:T(8,128)S(1)}, u32[]{:S(2)}, u32[]{:S(2)}) %collective-permute-start.24) | collective-permute-done | bytes 196640 | tf_op jit(solution)/shard_map/ppermute | solution.py:52
  164.8 7.9 %collective-permute-start.27 = (f32[64,768]{1,0:T(8,128)S(1)}, f32[64,768]{1,0:T(8,128)S(1)}, u32[]{:S(2)}, u32[]{:S(2)}) collective-permute-start(f32[64,768]{1,0:T(8,128)S(1)} %maximum_select_fusion.1), channel_id=1, source_target_pairs={{0,0},{1,160},{2,96},{3,192},{4,128},{5,32},{6,224},{7,64},{8,16},... | collective-permute-start | bytes 589832 | tf_op jit(solution)/shard_map/ppermute | solution.py:52
  172.8 8.2 %collective-permute-done.27.refs_6_ = f32[64,768]{1,0:T(8,128)S(1)} collective-permute-done((f32[64,768]{1,0:T(8,128)S(1)}, f32[64,768]{1,0:T(8,128)S(1)}, u32[]{:S(2)}, u32[]{:S(2)}) %collective-permute-start.27) | collective-permute-done | bytes 196640 | tf_op jit(solution)/shard_map/ppermute | solution.py:52
  182.5 5.7 %gram.1 = (f32[256,128]{1,0:T(8,128)S(1)}, f32[256,128]{1,0:T(8,128)S(1)}, f32[256,128]{1,0:T(8,128)S(1)}, f32[256,128]{1,0:T(8,128)S(1)}) custom-call(bf16[512,1536]{1,0:T(8,128)(2,1)S(1)} %copy-done.14, bf16[512,1536]{1,0:T(8,128)(2,1)S(1)} %copy-done.16, bf16[512,1536]{1,0:T(8,128)(2,1)S(1)} %copy-done.18, bf16[512,1536]{1,0:T(8,128)(2,1)S(1)} %copy-done.20, ...), custom_call_target="tpu_custom_call" | custom-call | flops 1000 | bytes 1000 | tf_op jit(solution)/shard_map/gram/pallas_call | solution.py:169
  188.2 5.6 %collective-permute-start.30 = (f32[256,128]{1,0:T(8,128)S(1)}, f32[256,128]{1,0:T(8,128)S(1)}, u32[]{:S(2)}, u32[]{:S(2)}) collective-permute-start(f32[256,128]{1,0:T(8,128)S(1)} %get-tuple-element.40), channel_id=1, source_target_pairs={{0,6},{1,7},{2,0},{3,1},{4,2},{5,3},{6,4},{7,5},{8,14},{9,15},{10,... | collective-permute-start | bytes 393224 | tf_op jit(solution)/shard_map/ppermute | solution.py:52
  193.8 5.8 %collective-permute-start.31 = (f32[256,128]{1,0:T(8,128)S(1)}, f32[256,128]{1,0:T(8,128)S(1)}, u32[]{:S(2)}, u32[]{:S(2)}) collective-permute-start(f32[256,128]{1,0:T(8,128)S(1)} %get-tuple-element.41), channel_id=1, source_target_pairs={{0,4},{1,5},{2,6},{3,7},{4,0},{5,1},{6,2},{7,3},{8,12},{9,13},{10,... | collective-permute-start | bytes 393224 | tf_op jit(solution)/shard_map/ppermute | solution.py:52
  199.6 2.3 collective-permute-done.30
  201.8 4.0 %collective-permute-done.31 = f32[256,128]{1,0:T(8,128)S(1)} collective-permute-done((f32[256,128]{1,0:T(8,128)S(1)}, f32[256,128]{1,0:T(8,128)S(1)}, u32[]{:S(2)}, u32[]{:S(2)}) %collective-permute-start.31) | collective-permute-done | bytes 131104 | tf_op jit(solution)/shard_map/ppermute | solution.py:52
  205.9 5.3 %collective-permute-start.32 = (f32[2,64,128]{2,1,0:T(8,128)S(1)}, f32[2,64,128]{2,1,0:T(8,128)S(1)}, u32[]{:S(2)}, u32[]{:S(2)}) collective-permute-start(f32[2,64,128]{2,1,0:T(8,128)S(1)} %dynamic-slice_bitcast_fusion.6), channel_id=1, source_target_pairs={{0,8},{1,9},{2,10},{3,11},{4,12},{5,13},{6,14},{7,15},{8,0},{9,1},... | collective-permute-start | bytes 196616 | tf_op jit(solution)/shard_map/ppermute | solution.py:52
  211.2 2.2 collective-permute-done.32
  214.8 4.4 %collective-permute-start.34 = (f32[128,128]{1,0:T(8,128)S(1)}, f32[128,128]{1,0:T(8,128)S(1)}, u32[]{:S(2)}, u32[]{:S(2)}) collective-permute-start(f32[128,128]{1,0:T(8,128)S(1)} %maximum_select_fusion.2), channel_id=1, source_target_pairs={{0,0},{160,1},{96,2},{192,3},{128,4},{32,5},{224,6},{64,7},{16,8},... | collective-permute-start | bytes 196616 | tf_op jit(solution)/shard_map/ppermute | solution.py:52
  220.1 9.0 %collective-permute-done.34 = f32[128,128]{1,0:T(8,128)S(1)} collective-permute-done((f32[128,128]{1,0:T(8,128)S(1)}, f32[128,128]{1,0:T(8,128)S(1)}, u32[]{:S(2)}, u32[]{:S(2)}) %collective-permute-start.34) | collective-permute-done | bytes 65568 | tf_op jit(solution)/shard_map/ppermute | solution.py:52
  (131 shorter events, 39.4 us)
Async XLA Ops:
  0.6 54.8 %collective-permute-start.11 = (f32[768,768]{1,0:T(8,128)}, f32[768,768]{1,0:T(8,128)}, u32[]{:S(2)}, u32[]{:S(2)}) collective-permute-start(f32[768,768]{1,0:T(8,128)} %param.4), channel_id=1, source_target_pairs={{0,1},{1,0},{2,3},{3,2},{4,5},{5,4},{6,7},{7,6},{8,9},{9,8},{10,11... | collective-permute-start | bytes 7077896 | tf_op jit(solution)/shard_map/ppermute | solution.py:52
  4.0 1.6 collective-permute-start
  5.7 15.8 %collective-permute-start.3 = (f32[32,1536]{1,0:T(8,128)S(1)}, f32[32,1536]{1,0:T(8,128)S(1)}, u32[]{:S(2)}, u32[]{:S(2)}) collective-permute-start(f32[32,1536]{1,0:T(8,128)S(1)} %get-tuple-element.49.refs_0_), channel_id=1, source_target_pairs={{0,32},{1,33},{2,34},{3,35},{4,36},{5,37},{6,38},{7,39},{8,40},{9,... | collective-permute-start | bytes 589832 | tf_op jit(solution)/shard_map/ppermute | solution.py:52
  12.9 18.7 %collective-permute-start.2 = (f32[32,1536]{1,0:T(8,128)S(1)}, f32[32,1536]{1,0:T(8,128)S(1)}, u32[]{:S(2)}, u32[]{:S(2)}) collective-permute-start(f32[32,1536]{1,0:T(8,128)S(1)} %get-tuple-element.49.refs_0_), channel_id=1, source_target_pairs={{0,48},{1,49},{2,50},{3,51},{4,52},{5,53},{6,54},{7,55},{8,56},{9,... | collective-permute-start | bytes 589832 | tf_op jit(solution)/shard_map/ppermute | solution.py:52
  12.9 18.7 %collective-permute-start.1 = (f32[32,1536]{1,0:T(8,128)S(1)}, f32[32,1536]{1,0:T(8,128)S(1)}, u32[]{:S(2)}, u32[]{:S(2)}) collective-permute-start(f32[32,1536]{1,0:T(8,128)S(1)} %get-tuple-element.49.refs_0_), channel_id=1, source_target_pairs={{0,16},{1,17},{2,18},{3,19},{4,20},{5,21},{6,22},{7,23},{8,24},{9,... | collective-permute-start | bytes 589832 | tf_op jit(solution)/shard_map/ppermute | solution.py:52
  31.7 10.6 %collective-permute-start.5 = (f32[32,1536]{1,0:T(8,128)S(1)}, f32[32,1536]{1,0:T(8,128)S(1)}, u32[]{:S(2)}, u32[]{:S(2)}) collective-permute-start(f32[32,1536]{1,0:T(8,128)S(1)} %get-tuple-element.22.refs_0_), channel_id=1, source_target_pairs={{0,48},{1,49},{2,50},{3,51},{4,52},{5,53},{6,54},{7,55},{8,56},{9,... | collective-permute-start | bytes 589832 | tf_op jit(solution)/shard_map/ppermute | solution.py:52
  34.8 27.9 %collective-permute-start.10 = (f32[128,1536]{1,0:T(8,128)S(1)}, f32[128,1536]{1,0:T(8,128)S(1)}, u32[]{:S(2)}, u32[]{:S(2)}) collective-permute-start(f32[128,1536]{1,0:T(8,128)S(1)} %get-tuple-element.23.refs_5_), channel_id=1, source_target_pairs={{0,128},{1,129},{2,130},{3,131},{4,132},{5,133},{6,134},{7,135},{8... | collective-permute-start | bytes 2359304 | tf_op jit(solution)/shard_map/ppermute | solution.py:52
  37.8 34.2 %collective-permute-start.9 = (f32[128,1536]{1,0:T(8,128)S(1)}, f32[128,1536]{1,0:T(8,128)S(1)}, u32[]{:S(2)}, u32[]{:S(2)}) collective-permute-start(f32[128,1536]{1,0:T(8,128)S(1)} %get-tuple-element.23.refs_5_), channel_id=1, source_target_pairs={{0,192},{1,193},{2,194},{3,195},{4,196},{5,197},{6,198},{7,199},{8... | collective-permute-start | bytes 2359304 | tf_op jit(solution)/shard_map/ppermute | solution.py:52
  39.0 33.1 %collective-permute-start.8 = (f32[128,1536]{1,0:T(8,128)S(1)}, f32[128,1536]{1,0:T(8,128)S(1)}, u32[]{:S(2)}, u32[]{:S(2)}) collective-permute-start(f32[128,1536]{1,0:T(8,128)S(1)} %get-tuple-element.23.refs_5_), channel_id=1, source_target_pairs={{0,64},{1,65},{2,66},{3,67},{4,68},{5,69},{6,70},{7,71},{8,72},{9,... | collective-permute-start | bytes 2359304 | tf_op jit(solution)/shard_map/ppermute | solution.py:52
  42.3 13.1 %collective-permute-start.4 = (f32[32,1536]{1,0:T(8,128)S(1)}, f32[32,1536]{1,0:T(8,128)S(1)}, u32[]{:S(2)}, u32[]{:S(2)}) collective-permute-start(f32[32,1536]{1,0:T(8,128)S(1)} %get-tuple-element.22.refs_0_), channel_id=1, source_target_pairs={{0,16},{1,17},{2,18},{3,19},{4,20},{5,21},{6,22},{7,23},{8,24},{9,... | collective-permute-start | bytes 589832 | tf_op jit(solution)/shard_map/ppermute | solution.py:52
  55.4 6.8 %collective-permute-start.7 = (f32[16,1536]{1,0:T(8,128)S(1)}, f32[16,1536]{1,0:T(8,128)S(1)}, u32[]{:S(2)}, u32[]{:S(2)}) collective-permute-start(f32[16,1536]{1,0:T(8,128)S(1)} %slice.45), channel_id=1, source_target_pairs={{0,48},{1,49},{2,50},{3,51},{4,52},{5,53},{6,54},{7,55},{8,56},{9,... | collective-permute-start | bytes 294920 | tf_op jit(solution)/shard_map/ppermute | solution.py:52
  55.5 7.3 %collective-permute-start.6 = (f32[16,1536]{1,0:T(8,128)S(1)}, f32[16,1536]{1,0:T(8,128)S(1)}, u32[]{:S(2)}, u32[]{:S(2)}) collective-permute-start(f32[16,1536]{1,0:T(8,128)S(1)} %slice.44), channel_id=1, source_target_pairs={{0,16},{1,17},{2,18},{3,19},{4,20},{5,21},{6,22},{7,23},{8,24},{9,... | collective-permute-start | bytes 294920 | tf_op jit(solution)/shard_map/ppermute | solution.py:52
  74.4 22.9 %collective-permute-start.14 = (f32[128,1536]{1,0:T(8,128)}, f32[128,1536]{1,0:T(8,128)}, u32[]{:S(2)}, u32[]{:S(2)}) collective-permute-start(f32[128,1536]{1,0:T(8,128)} %get-tuple-element.26.c0), channel_id=1, source_target_pairs={{0,128},{1,129},{2,130},{3,131},{4,132},{5,133},{6,134},{7,135},{8... | collective-permute-start | bytes 2359304 | tf_op jit(solution)/shard_map/ppermute | solution.py:52
  77.0 35.5 %collective-permute-start.13 = (f32[128,1536]{1,0:T(8,128)}, f32[128,1536]{1,0:T(8,128)}, u32[]{:S(2)}, u32[]{:S(2)}) collective-permute-start(f32[128,1536]{1,0:T(8,128)} %get-tuple-element.26.c0), channel_id=1, source_target_pairs={{0,192},{1,193},{2,194},{3,195},{4,196},{5,197},{6,198},{7,199},{8... | collective-permute-start | bytes 2359304 | tf_op jit(solution)/shard_map/ppermute | solution.py:52
  78.4 34.1 %collective-permute-start.12 = (f32[128,1536]{1,0:T(8,128)}, f32[128,1536]{1,0:T(8,128)}, u32[]{:S(2)}, u32[]{:S(2)}) collective-permute-start(f32[128,1536]{1,0:T(8,128)} %get-tuple-element.26.c0), channel_id=1, source_target_pairs={{0,64},{1,65},{2,66},{3,67},{4,68},{5,69},{6,70},{7,71},{8,72},{9,... | collective-permute-start | bytes 2359304 | tf_op jit(solution)/shard_map/ppermute | solution.py:52
  95.2 27.3 %collective-permute-start.15 = (f32[128,768]{1,0:T(8,128)}, f32[128,768]{1,0:T(8,128)}, u32[]{:S(2)}, u32[]{:S(2)}) collective-permute-start(f32[128,768]{1,0:T(8,128)} %get-tuple-element.28), channel_id=1, source_target_pairs={{0,2},{1,3},{2,4},{3,5},{4,6},{5,7},{6,0},{7,1},{8,10},{9,11},{10,... | collective-permute-start | bytes 1179656 | tf_op jit(solution)/shard_map/ppermute | solution.py:52
  95.4 27.1 %collective-permute-start.16 = (f32[128,768]{1,0:T(8,128)}, f32[128,768]{1,0:T(8,128)}, u32[]{:S(2)}, u32[]{:S(2)}) collective-permute-start(f32[128,768]{1,0:T(8,128)} %get-tuple-element.29), channel_id=1, source_target_pairs={{0,6},{1,7},{2,0},{3,1},{4,2},{5,3},{6,4},{7,5},{8,14},{9,15},{10,... | collective-permute-start | bytes 1179656 | tf_op jit(solution)/shard_map/ppermute | solution.py:52
  97.3 25.3 %collective-permute-start.17 = (f32[128,768]{1,0:T(8,128)}, f32[128,768]{1,0:T(8,128)}, u32[]{:S(2)}, u32[]{:S(2)}) collective-permute-start(f32[128,768]{1,0:T(8,128)} %get-tuple-element.30), channel_id=1, source_target_pairs={{0,4},{1,5},{2,6},{3,7},{4,0},{5,1},{6,2},{7,3},{8,12},{9,13},{10,... | collective-permute-start | bytes 1179656 | tf_op jit(solution)/shard_map/ppermute | solution.py:52
  125.0 6.5 %collective-permute-start.18 = (f32[2,32,768]{2,1,0:T(8,128)S(1)}, f32[2,32,768]{2,1,0:T(8,128)S(1)}, u32[]{:S(2)}, u32[]{:S(2)}) collective-permute-start(f32[2,32,768]{2,1,0:T(8,128)S(1)} %dynamic-slice_bitcast_fusion.1), channel_id=1, source_target_pairs={{0,8},{1,9},{2,10},{3,11},{4,12},{5,13},{6,14},{7,15},{8,0},{9,1},... | collective-permute-start | bytes 589832 | tf_op jit(solution)/shard_map/ppermute | solution.py:52
  131.5 3.4 %collective-permute-start.19 = (f32[32,768]{1,0:T(8,128)S(1)}, f32[32,768]{1,0:T(8,128)S(1)}, u32[]{:S(2)}, u32[]{:S(2)}) collective-permute-start(f32[32,768]{1,0:T(8,128)S(1)} %get-tuple-element.59), channel_id=1, source_target_pairs={{0,1},{1,0},{2,3},{3,2},{4,5},{5,4},{6,7},{7,6},{8,9},{9,8},{10,11... | collective-permute-start | bytes 294920 | tf_op jit(solution)/shard_map/ppermute | solution.py:52
  131.6 21.2 %collective-permute-start.21 = (f32[128,768]{1,0:T(8,128)}, f32[128,768]{1,0:T(8,128)S(1)}, u32[]{:S(2)}, u32[]{:S(2)}) collective-permute-start(f32[128,768]{1,0:T(8,128)} %copy-done.25), channel_id=1, source_target_pairs={{0,2},{1,3},{2,4},{3,5},{4,6},{5,7},{6,0},{7,1},{8,10},{9,11},{10,... | collective-permute-start | bytes 1179656 | tf_op jit(solution)/shard_map/ppermute | solution.py:52
  131.9 25.3 %collective-permute-start.22 = (f32[128,768]{1,0:T(8,128)}, f32[128,768]{1,0:T(8,128)S(1)}, u32[]{:S(2)}, u32[]{:S(2)}) collective-permute-start(f32[128,768]{1,0:T(8,128)} %copy-done.24), channel_id=1, source_target_pairs={{0,6},{1,7},{2,0},{3,1},{4,2},{5,3},{6,4},{7,5},{8,14},{9,15},{10,... | collective-permute-start | bytes 1179656 | tf_op jit(solution)/shard_map/ppermute | solution.py:52
  133.7 23.5 %collective-permute-start.23 = (f32[128,768]{1,0:T(8,128)}, f32[128,768]{1,0:T(8,128)S(1)}, u32[]{:S(2)}, u32[]{:S(2)}) collective-permute-start(f32[128,768]{1,0:T(8,128)} %copy-done.23), channel_id=1, source_target_pairs={{0,4},{1,5},{2,6},{3,7},{4,0},{5,1},{6,2},{7,3},{8,12},{9,13},{10,... | collective-permute-start | bytes 1179656 | tf_op jit(solution)/shard_map/ppermute | solution.py:52
  135.0 17.8 %collective-permute-start.20 = (f32[64,768]{1,0:T(8,128)S(1)}, f32[64,768]{1,0:T(8,128)S(1)}, u32[]{:S(2)}, u32[]{:S(2)}) collective-permute-start(f32[64,768]{1,0:T(8,128)S(1)} %maximum_select_fusion), channel_id=1, source_target_pairs={{0,0},{1,160},{2,96},{3,192},{4,128},{5,32},{6,224},{7,64},{8,16},... | collective-permute-start | bytes 589832 | tf_op jit(solution)/shard_map/ppermute | solution.py:52
  157.3 6.1 %collective-permute-start.24 = (f32[2,32,768]{2,1,0:T(8,128)S(1)}, f32[2,32,768]{2,1,0:T(8,128)S(1)}, u32[]{:S(2)}, u32[]{:S(2)}) collective-permute-start(f32[2,32,768]{2,1,0:T(8,128)S(1)} %dynamic-slice_bitcast_fusion), channel_id=1, source_target_pairs={{0,8},{1,9},{2,10},{3,11},{4,12},{5,13},{6,14},{7,15},{8,0},{9,1},... | collective-permute-start | bytes 589832 | tf_op jit(solution)/shard_map/ppermute | solution.py:52
  164.8 16.2 %collective-permute-start.27 = (f32[64,768]{1,0:T(8,128)S(1)}, f32[64,768]{1,0:T(8,128)S(1)}, u32[]{:S(2)}, u32[]{:S(2)}) collective-permute-start(f32[64,768]{1,0:T(8,128)S(1)} %maximum_select_fusion.1), channel_id=1, source_target_pairs={{0,0},{1,160},{2,96},{3,192},{4,128},{5,32},{6,224},{7,64},{8,16},... | collective-permute-start | bytes 589832 | tf_op jit(solution)/shard_map/ppermute | solution.py:52
  172.7 8.3 %collective-permute-start.26 = (f32[64,768]{1,0:T(8,128)S(1)}, f32[64,768]{1,0:T(8,128)S(1)}, u32[]{:S(2)}, u32[]{:S(2)}) collective-permute-start(f32[64,768]{1,0:T(8,128)S(1)} %collective-permute-done.20.refs_1_.refs_4_), channel_id=1, source_target_pairs={{0,1},{1,0},{2,3},{3,2},{4,5},{5,4},{6,7},{7,6},{8,9},{9,8},{10,11... | collective-permute-start | bytes 589832 | tf_op jit(solution)/shard_map/ppermute | solution.py:52
  188.2 11.4 %collective-permute-start.29 = (f32[256,128]{1,0:T(8,128)S(1)}, f32[256,128]{1,0:T(8,128)S(1)}, u32[]{:S(2)}, u32[]{:S(2)}) collective-permute-start(f32[256,128]{1,0:T(8,128)S(1)} %get-tuple-element.39), channel_id=1, source_target_pairs={{0,2},{1,3},{2,4},{3,5},{4,6},{5,7},{6,0},{7,1},{8,10},{9,11},{10,... | collective-permute-start | bytes 393224 | tf_op jit(solution)/shard_map/ppermute | solution.py:52
  188.2 13.6 %collective-permute-start.30 = (f32[256,128]{1,0:T(8,128)S(1)}, f32[256,128]{1,0:T(8,128)S(1)}, u32[]{:S(2)}, u32[]{:S(2)}) collective-permute-start(f32[256,128]{1,0:T(8,128)S(1)} %get-tuple-element.40), channel_id=1, source_target_pairs={{0,6},{1,7},{2,0},{3,1},{4,2},{5,3},{6,4},{7,5},{8,14},{9,15},{10,... | collective-permute-start | bytes 393224 | tf_op jit(solution)/shard_map/ppermute | solution.py:52
  193.8 12.0 %collective-permute-start.31 = (f32[256,128]{1,0:T(8,128)S(1)}, f32[256,128]{1,0:T(8,128)S(1)}, u32[]{:S(2)}, u32[]{:S(2)}) collective-permute-start(f32[256,128]{1,0:T(8,128)S(1)} %get-tuple-element.41), channel_id=1, source_target_pairs={{0,4},{1,5},{2,6},{3,7},{4,0},{5,1},{6,2},{7,3},{8,12},{9,13},{10,... | collective-permute-start | bytes 393224 | tf_op jit(solution)/shard_map/ppermute | solution.py:52
  205.9 7.5 %collective-permute-start.32 = (f32[2,64,128]{2,1,0:T(8,128)S(1)}, f32[2,64,128]{2,1,0:T(8,128)S(1)}, u32[]{:S(2)}, u32[]{:S(2)}) collective-permute-start(f32[2,64,128]{2,1,0:T(8,128)S(1)} %dynamic-slice_bitcast_fusion.6), channel_id=1, source_target_pairs={{0,8},{1,9},{2,10},{3,11},{4,12},{5,13},{6,14},{7,15},{8,0},{9,1},... | collective-permute-start | bytes 196616 | tf_op jit(solution)/shard_map/ppermute | solution.py:52
  214.8 14.4 %collective-permute-start.34 = (f32[128,128]{1,0:T(8,128)S(1)}, f32[128,128]{1,0:T(8,128)S(1)}, u32[]{:S(2)}, u32[]{:S(2)}) collective-permute-start(f32[128,128]{1,0:T(8,128)S(1)} %maximum_select_fusion.2), channel_id=1, source_target_pairs={{0,0},{160,1},{96,2},{192,3},{128,4},{32,5},{224,6},{64,7},{16,8},... | collective-permute-start | bytes 196616 | tf_op jit(solution)/shard_map/ppermute | solution.py:52
  (31 other events, 301.8 us)

commit v2 on v1

--- a/solution.py
+++ b/solution.py
@@ -56,15 +56,24 @@
     return [value] + [send(value, shift(**{axis: step})) for step in STEPS[1:]]
 
 
-def ring_forward(value, axis):
+def ring_forward(value, axis, work=None):
     half = value.shape[0] // 2
     up, down = (send(value, shift(**{axis: step})) for step in STEPS[1:3])
+    if work is not None:
+        up = tie(up, work())
     far = [send(up[:half], shift(**{axis: 1})), send(down[half:], shift(**{axis: -1}))]
     return [value, up, down, *far]
 
 
 def ring_scatter(values, axis):
-    got = [send(value, shift(**{axis: step})) for step, value in zip(STEPS[1:], values[1:])]
+    return ring_sum(values, ring_send(values, axis))
+
+
+def ring_send(values, axis):
+    return [send(value, shift(**{axis: step})) for step, value in zip(STEPS[1:], values[1:])]
+
+
+def ring_sum(values, got):
     return (values[0] + got[0]) + (got[1] + got[2])
 
 
@@ -92,20 +101,23 @@
     return jnp.where(step == 3, 2, jnp.where(step == 2, 3, step))
 
 
-def product_kernel(rows, me_ref, c0, c1, c2, c3, h0, l0, h1, l1, *refs):
+def product_kernel(rows, me_ref, c0, c1, c2, c3, c4, h0, l0, h1, l1, *refs):
     outs, high_out, low_out, high, low, sep, sems = refs[:4], refs[4], refs[5], refs[6], refs[7], refs[8:12], refs[12]
     loads = [pltpu.make_async_copy(src, dst, sems.at[i]) for i, (src, dst) in enumerate(zip((h0, l0, h1, l1), sep))]
     for load in loads:
         load.start()
     x, zh, y = me_ref[0], me_ref[1], me_ref[2]
-    for sx, ref in enumerate((c0, c1, c2, c3)):
+    for sx in range(4):
         for sz in range(4):
+            ref, start = (c0, c1, c2, c3)[sx], sz * rows
+            if sx == 3 and sz >= 2:
+                ref, start = c4, start - 2 * rows
             xs = lax.rem(x - STEPS[sx] + 4, 4)
             zs = lax.rem(zh - STEPS[sz] + 4, 4)
             to = ring_slot(2 * lax.rem(xs, 2) + zs // 2 - y)
             place = (to * 2 + xs // 2) * 2 + lax.rem(zs, 2)
             at = pl.ds(pl.multiple_of(place * rows, rows), rows)
-            store_split(high, low, (at, slice(None)), ref[sz * rows : (sz + 1) * rows, :])
+            store_split(high, low, (at, slice(None)), ref[start : start + rows, :])
     stores = [pltpu.make_async_copy(high, high_out, sems.at[4]), pltpu.make_async_copy(low, low_out, sems.at[5])]
     for store in stores:
         store.start()
@@ -130,7 +142,7 @@
         functools.partial(product_kernel, rows),
         out_shape=[jax.ShapeDtypeStruct((4 * rows, BS), jnp.float32)] * 4
         + [jax.ShapeDtypeStruct((16 * rows, 2 * BS), jnp.bfloat16)] * 2,
-        in_specs=[SMEM] + [VMEM] * 4 + [HBM] * 4,
+        in_specs=[SMEM] + [VMEM] * 5 + [HBM] * 4,
         out_specs=[VMEM] * 4 + [HBM] * 2,
         scratch_shapes=[pltpu.VMEM((16 * rows, 2 * BS), jnp.bfloat16)] * 2
         + [pltpu.VMEM((BS, BS), jnp.bfloat16)] * 4
@@ -143,10 +155,7 @@
 
 
 def gram_kernel(*refs):
-    panels, columns, outs, held, chigh, clow, sems = refs[:4], refs[4:8], refs[8:12], refs[12:16], refs[16], refs[17], refs[18]
-    loads = [pltpu.make_async_copy(src, dst, sems.at[i]) for i, (src, dst) in enumerate(zip(panels, held))]
-    for load in loads:
-        load.start()
+    panels, columns, outs, chigh, clow = refs[:4], refs[4:8], refs[8:12], refs[12], refs[13]
     at = 0
     for half in range(2):
         for group, rows in enumerate(SIZES):
@@ -155,9 +164,7 @@
                 store_split(chigh, clow, (slice(at, at + rows), slice(BS * i, BS * (i + 1))), value)
             at += rows
     for t, rows in enumerate(SIZES):
-        loads[2 * t].wait()
-        loads[2 * t + 1].wait()
-        high, low = held[2 * t][...], held[2 * t + 1][...]
+        high, low = panels[2 * t][...], panels[2 * t + 1][...]
         sums = dot_nt(high, chigh[...]) + dot_nt(low, chigh[...]) + dot_nt(high, clow[...])
         for i, out in enumerate(outs):
             for e in range(4):
@@ -169,11 +176,9 @@
     return pl.pallas_call(
         gram_kernel,
         out_shape=[jax.ShapeDtypeStruct((256, 128), jnp.float32)] * 4,
-        in_specs=[HBM] * 4 + [VMEM] * 4,
+        in_specs=[VMEM] * 8,
         out_specs=[VMEM] * 4,
-        scratch_shapes=[pltpu.VMEM((16 * rows, 2 * BS), jnp.bfloat16) for rows in SIZES for i in range(2)]
-        + [pltpu.VMEM((128, 2 * BS), jnp.bfloat16)] * 2
-        + [pltpu.SemaphoreType.DMA((4,))],
+        scratch_shapes=[pltpu.VMEM((128, 2 * BS), jnp.bfloat16)] * 2,
         compiler_params=pltpu.CompilerParams(vmem_limit_bytes=14 << 20),
         cost_estimate=COST,
         name="gram",
@@ -249,17 +254,15 @@
     sep = split(separator_inverse) + split(sep_other)
 
     lead, rest = mine[: SIZES[0]], mine[SIZES[0] :]
-    rest, col0 = join(ring_gather(lead, "dzh"), SIZES[:1], [rest])
-    x0 = ring_gather(col0, "dx")
+    rest, col0 = join(ring_forward(lead, "dzh"), SIZES[:1], [rest])
+    x0 = ring_forward(col0, "dx")
     col0, col1 = join(ring_forward(rest, "dzh"), SIZES[1:], [col0], [*x0[1:], *sep])
-    x1 = ring_gather(col1, "dx")
     x0[0] = col0
     out0, panel0 = product(me, x0, sep)
+    x1 = ring_forward(col1, "dx", lambda: out0[1])
     out1, panel1 = product(me, x1, sep)
-    out0[0] = tie(out0[0], out1[0])
     kept0 = whole(from_chips(ring_scatter(out0, "dy")))
     column0 = send(kept0, TO_COLUMN)
-    out1[0] = tie(out1[0], column0)
     kept1 = whole(from_chips(ring_scatter(out1, "dy")))
     column1 = send(kept1, TO_COLUMN)
     columns = [column0, send(column0, swap), column1, send(column1, swap)]

time: 230 us -> 205 us (0.89)
  waiting for transfers between devices: 112 us -> 77.4 us
  starting transfers between devices: 72.1 us -> 82.3 us
  Pallas kernels: 21.4 us -> 19 us
    ppermute x35 -> x38, waiting for transfers between devices: 112 us -> 77.4 us  [send(): return lax.ppermute(value, AXES, pairs)]
    ppermute x35 -> x38, starting transfers between devices: 72.1 us -> 82.3 us  [send(): return lax.ppermute(value, AXES, pairs)]
    pallas_call x1, Pallas kernels: 5.69 us -> 2.58 us  [gram_parts(): pl.pallas_call(gram_kernel, out_shape=[jax.ShapeDtypeStruct((256, 128), j...]
    unnamed x58 -> x54, local copies, waits for them, and re-layouts: 14.8 us -> 13.6 us
  transfers between devices with their start and end apart: 35 -> 38, of which waited for: 21 -> 22; matrix products, arithmetic and copies ran while one was open for 3% -> 5% of each run, Pallas kernels for 6% -> 8%
where the time goes in v2:
time: 205 us; the launch traced here: 203 us
  starting transfers between devices  82.3 us (40%)
  waiting for transfers between devices  77.4 us (38%)
  Pallas kernels  19 us (9%)
  local copies, waits for them, and re-layouts  17.3 us (8%)
  other arithmetic  4.97 us (2%)
  between operations  2.45 us (1%)
    ppermute x38, starting transfers between devices, send(): return lax.ppermute(value, AXES, pairs)  82.3 us
    ppermute x38, waiting for transfers between devices, send(): return lax.ppermute(value, AXES, pairs)  77.4 us
    pallas_call x2, Pallas kernels, product(): pl.pallas_call(functools.partial(product_kernel, rows), out_shape=[jax.Sh...  15.3 us
    unnamed x54, local copies, waits for them, and re-layouts  13.6 us
  transfers between devices with their start and end apart: 38, of which 22 were waited for; matrix products, arithmetic and copies ran while one was open for 5% of the time, Pallas kernels for 8%

profile of v2, /device:TPU:24, one launch (start us, length us, event | category | flops | bytes accessed | tf_op | source)
XLA Modules:
  0.0 203.4 jit_solution(7988674461012185687)
XLA Ops:
  5.7 3.4 %collective-permute-start.1 = (f32[32,1536]{1,0:T(8,128)S(1)}, f32[32,1536]{1,0:T(8,128)S(1)}, u32[]{:S(2)}, u32[]{:S(2)}) collective-permute-start(f32[32,1536]{1,0:T(8,128)S(1)} %get-tuple-element.49.refs_0_), channel_id=1, source_target_pairs={{0,16},{1,17},{2,18},{3,19},{4,20},{5,21},{6,22},{7,23},{8,24},{9,... | collective-permute-start | bytes 589832 | tf_op jit(solution)/shard_map/ppermute | solution.py:52
  9.0 3.1 %collective-permute-start.2 = (f32[32,1536]{1,0:T(8,128)S(1)}, f32[32,1536]{1,0:T(8,128)S(1)}, u32[]{:S(2)}, u32[]{:S(2)}) collective-permute-start(f32[32,1536]{1,0:T(8,128)S(1)} %get-tuple-element.49.refs_0_), channel_id=1, source_target_pairs={{0,48},{1,49},{2,50},{3,51},{4,52},{5,53},{6,54},{7,55},{8,56},{9,... | collective-permute-start | bytes 589832 | tf_op jit(solution)/shard_map/ppermute | solution.py:52
  12.1 6.9 %collective-permute-done.1.refs_1_ = f32[32,1536]{1,0:T(8,128)S(1)} collective-permute-done((f32[32,1536]{1,0:T(8,128)S(1)}, f32[32,1536]{1,0:T(8,128)S(1)}, u32[]{:S(2)}, u32[]{:S(2)}) %collective-permute-start.1) | collective-permute-done | bytes 196640 | tf_op jit(solution)/shard_map/ppermute | solution.py:52
  19.1 3.2 %collective-permute-start.3 = (f32[16,1536]{1,0:T(8,128)S(1)}, f32[16,1536]{1,0:T(8,128)S(1)}, u32[]{:S(2)}, u32[]{:S(2)}) collective-permute-start(f32[16,1536]{1,0:T(8,128)S(1)} %slice.68), channel_id=1, source_target_pairs={{0,16},{1,17},{2,18},{3,19},{4,20},{5,21},{6,22},{7,23},{8,24},{9,... | collective-permute-start | bytes 294920 | tf_op jit(solution)/shard_map/ppermute | solution.py:52
  22.9 2.8 %collective-permute-start.4 = (f32[16,1536]{1,0:T(8,128)S(1)}, f32[16,1536]{1,0:T(8,128)S(1)}, u32[]{:S(2)}, u32[]{:S(2)}) collective-permute-start(f32[16,1536]{1,0:T(8,128)S(1)} %slice.69), channel_id=1, source_target_pairs={{0,48},{1,49},{2,50},{3,51},{4,52},{5,53},{6,54},{7,55},{8,56},{9,... | collective-permute-start | bytes 294920 | tf_op jit(solution)/shard_map/ppermute | solution.py:52
  25.7 2.3 %collective-permute-done.3.refs_3_ = f32[16,1536]{1,0:T(8,128)S(1)} collective-permute-done((f32[16,1536]{1,0:T(8,128)S(1)}, f32[16,1536]{1,0:T(8,128)S(1)}, u32[]{:S(2)}, u32[]{:S(2)}) %collective-permute-start.3) | collective-permute-done | bytes 98336 | tf_op jit(solution)/shard_map/ppermute | solution.py:52
  28.1 2.6 %collective-permute-done.4.refs_4_ = f32[16,1536]{1,0:T(8,128)S(1)} collective-permute-done((f32[16,1536]{1,0:T(8,128)S(1)}, f32[16,1536]{1,0:T(8,128)S(1)}, u32[]{:S(2)}, u32[]{:S(2)}) %collective-permute-start.4) | collective-permute-done | bytes 98336 | tf_op jit(solution)/shard_map/ppermute | solution.py:52
  34.0 4.2 %collective-permute-start.5 = (f32[32,1536]{1,0:T(8,128)S(1)}, f32[32,1536]{1,0:T(8,128)S(1)}, u32[]{:S(2)}, u32[]{:S(2)}) collective-permute-start(f32[32,1536]{1,0:T(8,128)S(1)} %get-tuple-element.22.refs_0_), channel_id=1, source_target_pairs={{0,16},{1,17},{2,18},{3,19},{4,20},{5,21},{6,22},{7,23},{8,24},{9,... | collective-permute-start | bytes 589832 | tf_op jit(solution)/shard_map/ppermute | solution.py:52
  38.2 10.9 %collective-permute-done.9.refs_6_.c1 = f32[128,1536]{1,0:T(8,128)S(1)} collective-permute-done((f32[128,1536]{1,0:T(8,128)S(1)}, f32[128,1536]{1,0:T(8,128)S(1)}, u32[]{:S(2)}, u32[]{:S(2)}) %collective-permute-start.9) | collective-permute-done | bytes 786464 | tf_op jit(solution)/shard_map/ppermute | solution.py:52
  50.0 2.6 %collective-permute-start.12 = (f32[64,1536]{1,0:T(8,128)S(1)}, f32[64,1536]{1,0:T(8,128)S(1)}, u32[]{:S(2)}, u32[]{:S(2)}) collective-permute-start(f32[64,1536]{1,0:T(8,128)S(1)} %slice.73), channel_id=1, source_target_pairs={{0,192},{1,193},{2,194},{3,195},{4,196},{5,197},{6,198},{7,199},{8... | collective-permute-start | bytes 1179656 | tf_op jit(solution)/shard_map/ppermute | solution.py:52
  53.0 3.8 %collective-permute-start.7 = (f32[16,1536]{1,0:T(8,128)S(1)}, f32[16,1536]{1,0:T(8,128)S(1)}, u32[]{:S(2)}, u32[]{:S(2)}) collective-permute-start(f32[16,1536]{1,0:T(8,128)S(1)} %slice.70), channel_id=1, source_target_pairs={{0,16},{1,17},{2,18},{3,19},{4,20},{5,21},{6,22},{7,23},{8,24},{9,... | collective-permute-start | bytes 294920 | tf_op jit(solution)/shard_map/ppermute | solution.py:52
  61.0 2.0 collective-permute-done.8.refs_4_
  65.2 3.1 %collective-permute-start.20 = (f32[128,1536]{1,0:T(8,128)}, f32[128,1536]{1,0:T(8,128)}, u32[]{:S(2)}, u32[]{:S(2)}) collective-permute-start(f32[128,1536]{1,0:T(8,128)} %get-tuple-element.29.c0), channel_id=1, source_target_pairs={{0,192},{1,193},{2,194},{3,195},{4,196},{5,197},{6,198},{7,199},{8... | collective-permute-start | bytes 2359304 | tf_op jit(solution)/shard_map/ppermute | solution.py:52
  74.9 7.0 %product.2 = (f32[128,768]{1,0:T(8,128)S(1)}, f32[128,768]{1,0:T(8,128)S(1)}, f32[128,768]{1,0:T(8,128)}, f32[128,768]{1,0:T(8,128)}, bf16[512,1536]{1,0:T(8,128)(2,1)S(1)}, /*index=5*/bf16[512,1536]{1,0:T(8,128)(2,1)S(1)}) custom-call(s32[3]{0:T(128)S(1)} %pad_add_fusion.me_ref, f32[128,1536]{1,0:T(8,128)S(1)} %copy-done.7, f32[128,1536]{1,0:T(8,128)S(1)} %copy-done.3, ...), custom_call_target="tpu_custom_call" | custom-call | flops 1000 | bytes 1000 | tf_op jit(solution)/shard_map/product/pallas_call | solution.py:141
  85.3 3.3 %collective-permute-start.22 = (f32[64,1536]{1,0:T(8,128)S(1)}, f32[64,1536]{1,0:T(8,128)S(1)}, u32[]{:S(2)}, u32[]{:S(2)}) collective-permute-start(f32[64,1536]{1,0:T(8,128)S(1)} %slice.76), channel_id=1, source_target_pairs={{0,192},{1,193},{2,194},{3,195},{4,196},{5,197},{6,198},{7,199},{8... | collective-permute-start | bytes 1179656 | tf_op jit(solution)/shard_map/ppermute | solution.py:52
  93.9 8.3 %product.3 = (f32[128,768]{1,0:T(8,128)S(1)}, f32[128,768]{1,0:T(8,128)}, f32[128,768]{1,0:T(8,128)}, f32[128,768]{1,0:T(8,128)}, bf16[512,1536]{1,0:T(8,128)(2,1)S(1)}, /*index=5*/bf16[512,1536]{1,0:T(8,128)(2,1)S(1)}) custom-call(s32[3]{0:T(128)S(1)} %pad_add_fusion.me_ref, f32[128,1536]{1,0:T(8,128)} %get-tuple-element.29.c0, f32[128,1536]{1,0:T(8,128)} %tie.1.c1, ...), custom_call_target="tpu_custom_call" | custom-call | flops 1000 | bytes 1000 | tf_op jit(solution)/shard_map/product/pallas_call | solution.py:141
  112.1 4.6 %collective-permute-done.23 = f32[128,768]{1,0:T(8,128)S(1)} collective-permute-done((f32[128,768]{1,0:T(8,128)}, f32[128,768]{1,0:T(8,128)S(1)}, u32[]{:S(2)}, u32[]{:S(2)}) %collective-permute-start.23) | collective-permute-done | bytes 393248 | tf_op jit(solution)/shard_map/ppermute | solution.py:52
  116.6 5.5 %collective-permute-done.24 = f32[128,768]{1,0:T(8,128)S(1)} collective-permute-done((f32[128,768]{1,0:T(8,128)}, f32[128,768]{1,0:T(8,128)S(1)}, u32[]{:S(2)}, u32[]{:S(2)}) %collective-permute-start.24) | collective-permute-done | bytes 393248 | tf_op jit(solution)/shard_map/ppermute | solution.py:52
  123.2 4.9 %collective-permute-done.26 = f32[2,32,768]{2,1,0:T(8,128)S(1)} collective-permute-done((f32[2,32,768]{2,1,0:T(8,128)S(1)}, f32[2,32,768]{2,1,0:T(8,128)S(1)}, u32[]{:S(2)}, u32[]{:S(2)}) %collective-permute-start.26) | collective-permute-done | bytes 196640 | tf_op jit(solution)/shard_map/ppermute | solution.py:52
  128.3 11.0 %collective-permute-start.28 = (f32[64,768]{1,0:T(8,128)S(1)}, f32[64,768]{1,0:T(8,128)S(1)}, u32[]{:S(2)}, u32[]{:S(2)}) collective-permute-start(f32[64,768]{1,0:T(8,128)S(1)} %maximum_select_fusion), channel_id=1, source_target_pairs={{0,0},{1,160},{2,96},{3,192},{4,128},{5,32},{6,224},{7,64},{8,16},... | collective-permute-start | bytes 589832 | tf_op jit(solution)/shard_map/ppermute | solution.py:52
  139.4 2.0 collective-permute-start.30
  141.4 3.5 %collective-permute-done.28.refs_4_ = f32[64,768]{1,0:T(8,128)S(1)} collective-permute-done((f32[64,768]{1,0:T(8,128)S(1)}, f32[64,768]{1,0:T(8,128)S(1)}, u32[]{:S(2)}, u32[]{:S(2)}) %collective-permute-start.28) | collective-permute-done | bytes 196640 | tf_op jit(solution)/shard_map/ppermute | solution.py:52
  145.0 9.5 %collective-permute-done.30.refs_6_ = f32[64,768]{1,0:T(8,128)S(1)} collective-permute-done((f32[64,768]{1,0:T(8,128)S(1)}, f32[64,768]{1,0:T(8,128)S(1)}, u32[]{:S(2)}, u32[]{:S(2)}) %collective-permute-start.30) | collective-permute-done | bytes 196640 | tf_op jit(solution)/shard_map/ppermute | solution.py:52
  155.9 2.6 %gram.1 = (f32[256,128]{1,0:T(8,128)S(1)}, f32[256,128]{1,0:T(8,128)S(1)}, f32[256,128]{1,0:T(8,128)S(1)}, f32[256,128]{1,0:T(8,128)S(1)}) custom-call(bf16[512,1536]{1,0:T(8,128)(2,1)S(1)} %copy-done.13, bf16[512,1536]{1,0:T(8,128)(2,1)S(1)} %copy-done.15, bf16[512,1536]{1,0:T(8,128)(2,1)S(1)} %copy-done.17, bf16[512,1536]{1,0:T(8,128)(2,1)S(1)} %copy-done.19, ...), custom_call_target="tpu_custom_call" | custom-call | flops 1000 | bytes 1000 | tf_op jit(solution)/shard_map/gram/pallas_call | solution.py:176
  158.6 8.2 %collective-permute-start.33 = (f32[256,128]{1,0:T(8,128)S(1)}, f32[256,128]{1,0:T(8,128)S(1)}, u32[]{:S(2)}, u32[]{:S(2)}) collective-permute-start(f32[256,128]{1,0:T(8,128)S(1)} %get-tuple-element.40), channel_id=1, source_target_pairs={{0,6},{1,7},{2,0},{3,1},{4,2},{5,3},{6,4},{7,5},{8,14},{9,15},{10,... | collective-permute-start | bytes 393224 | tf_op jit(solution)/shard_map/ppermute | solution.py:52
  166.8 7.6 %collective-permute-start.34 = (f32[256,128]{1,0:T(8,128)S(1)}, f32[256,128]{1,0:T(8,128)S(1)}, u32[]{:S(2)}, u32[]{:S(2)}) collective-permute-start(f32[256,128]{1,0:T(8,128)S(1)} %get-tuple-element.41), channel_id=1, source_target_pairs={{0,4},{1,5},{2,6},{3,7},{4,0},{5,1},{6,2},{7,3},{8,12},{9,13},{10,... | collective-permute-start | bytes 393224 | tf_op jit(solution)/shard_map/ppermute | solution.py:52
  174.3 2.3 %collective-permute-done.33 = f32[256,128]{1,0:T(8,128)S(1)} collective-permute-done((f32[256,128]{1,0:T(8,128)S(1)}, f32[256,128]{1,0:T(8,128)S(1)}, u32[]{:S(2)}, u32[]{:S(2)}) %collective-permute-start.33) | collective-permute-done | bytes 131104 | tf_op jit(solution)/shard_map/ppermute | solution.py:52
  176.6 4.0 %collective-permute-done.34 = f32[256,128]{1,0:T(8,128)S(1)} collective-permute-done((f32[256,128]{1,0:T(8,128)S(1)}, f32[256,128]{1,0:T(8,128)S(1)}, u32[]{:S(2)}, u32[]{:S(2)}) %collective-permute-start.34) | collective-permute-done | bytes 131104 | tf_op jit(solution)/shard_map/ppermute | solution.py:52
  180.7 4.1 %collective-permute-start.35 = (f32[2,64,128]{2,1,0:T(8,128)S(1)}, f32[2,64,128]{2,1,0:T(8,128)S(1)}, u32[]{:S(2)}, u32[]{:S(2)}) collective-permute-start(f32[2,64,128]{2,1,0:T(8,128)S(1)} %dynamic-slice_bitcast_fusion.6), channel_id=1, source_target_pairs={{0,8},{1,9},{2,10},{3,11},{4,12},{5,13},{6,14},{7,15},{8,0},{9,1},... | collective-permute-start | bytes 196616 | tf_op jit(solution)/shard_map/ppermute | solution.py:52
  184.8 2.2 %collective-permute-done.35 = f32[2,64,128]{2,1,0:T(8,128)S(1)} collective-permute-done((f32[2,64,128]{2,1,0:T(8,128)S(1)}, f32[2,64,128]{2,1,0:T(8,128)S(1)}, u32[]{:S(2)}, u32[]{:S(2)}) %collective-permute-start.35) | collective-permute-done | bytes 65568 | tf_op jit(solution)/shard_map/ppermute | solution.py:52
  188.4 6.4 %collective-permute-start.37 = (f32[128,128]{1,0:T(8,128)S(1)}, f32[128,128]{1,0:T(8,128)S(1)}, u32[]{:S(2)}, u32[]{:S(2)}) collective-permute-start(f32[128,128]{1,0:T(8,128)S(1)} %maximum_select_fusion.2), channel_id=1, source_target_pairs={{0,0},{160,1},{96,2},{192,3},{128,4},{32,5},{224,6},{64,7},{16,8},... | collective-permute-start | bytes 196616 | tf_op jit(solution)/shard_map/ppermute | solution.py:52
  195.7 7.0 %collective-permute-done.37 = f32[128,128]{1,0:T(8,128)S(1)} collective-permute-done((f32[128,128]{1,0:T(8,128)S(1)}, f32[128,128]{1,0:T(8,128)S(1)}, u32[]{:S(2)}, u32[]{:S(2)}) %collective-permute-start.37) | collective-permute-done | bytes 65568 | tf_op jit(solution)/shard_map/ppermute | solution.py:52
  (138 shorter events, 45.9 us)
Async XLA Ops:
  0.6 56.7 %collective-permute-start.13 = (f32[768,768]{1,0:T(8,128)}, f32[768,768]{1,0:T(8,128)}, u32[]{:S(2)}, u32[]{:S(2)}) collective-permute-start(f32[768,768]{1,0:T(8,128)} %param.4), channel_id=1, source_target_pairs={{0,1},{1,0},{2,3},{3,2},{4,5},{5,4},{6,7},{7,6},{8,9},{9,8},{10,11... | collective-permute-start | bytes 7077896 | tf_op jit(solution)/shard_map/ppermute | solution.py:52
  5.7 13.4 %collective-permute-start.1 = (f32[32,1536]{1,0:T(8,128)S(1)}, f32[32,1536]{1,0:T(8,128)S(1)}, u32[]{:S(2)}, u32[]{:S(2)}) collective-permute-start(f32[32,1536]{1,0:T(8,128)S(1)} %get-tuple-element.49.refs_0_), channel_id=1, source_target_pairs={{0,16},{1,17},{2,18},{3,19},{4,20},{5,21},{6,22},{7,23},{8,24},{9,... | collective-permute-start | bytes 589832 | tf_op jit(solution)/shard_map/ppermute | solution.py:52
  9.0 13.8 %collective-permute-start.2 = (f32[32,1536]{1,0:T(8,128)S(1)}, f32[32,1536]{1,0:T(8,128)S(1)}, u32[]{:S(2)}, u32[]{:S(2)}) collective-permute-start(f32[32,1536]{1,0:T(8,128)S(1)} %get-tuple-element.49.refs_0_), channel_id=1, source_target_pairs={{0,48},{1,49},{2,50},{3,51},{4,52},{5,53},{6,54},{7,55},{8,56},{9,... | collective-permute-start | bytes 589832 | tf_op jit(solution)/shard_map/ppermute | solution.py:52
  19.1 9.0 %collective-permute-start.3 = (f32[16,1536]{1,0:T(8,128)S(1)}, f32[16,1536]{1,0:T(8,128)S(1)}, u32[]{:S(2)}, u32[]{:S(2)}) collective-permute-start(f32[16,1536]{1,0:T(8,128)S(1)} %slice.68), channel_id=1, source_target_pairs={{0,16},{1,17},{2,18},{3,19},{4,20},{5,21},{6,22},{7,23},{8,24},{9,... | collective-permute-start | bytes 294920 | tf_op jit(solution)/shard_map/ppermute | solution.py:52
  22.9 7.8 %collective-permute-start.4 = (f32[16,1536]{1,0:T(8,128)S(1)}, f32[16,1536]{1,0:T(8,128)S(1)}, u32[]{:S(2)}, u32[]{:S(2)}) collective-permute-start(f32[16,1536]{1,0:T(8,128)S(1)} %slice.69), channel_id=1, source_target_pairs={{0,48},{1,49},{2,50},{3,51},{4,52},{5,53},{6,54},{7,55},{8,56},{9,... | collective-permute-start | bytes 294920 | tf_op jit(solution)/shard_map/ppermute | solution.py:52
  30.7 18.4 %collective-permute-start.9 = (f32[128,1536]{1,0:T(8,128)S(1)}, f32[128,1536]{1,0:T(8,128)S(1)}, u32[]{:S(2)}, u32[]{:S(2)}) collective-permute-start(f32[128,1536]{1,0:T(8,128)S(1)} %get-tuple-element.23.refs_5_), channel_id=1, source_target_pairs={{0,64},{1,65},{2,66},{3,67},{4,68},{5,69},{6,70},{7,71},{8,72},{9,... | collective-permute-start | bytes 2359304 | tf_op jit(solution)/shard_map/ppermute | solution.py:52
  32.3 17.7 %collective-permute-start.10 = (f32[128,1536]{1,0:T(8,128)S(1)}, f32[128,1536]{1,0:T(8,128)S(1)}, u32[]{:S(2)}, u32[]{:S(2)}) collective-permute-start(f32[128,1536]{1,0:T(8,128)S(1)} %get-tuple-element.23.refs_5_), channel_id=1, source_target_pairs={{0,192},{1,193},{2,194},{3,195},{4,196},{5,197},{6,198},{7,199},{8... | collective-permute-start | bytes 2359304 | tf_op jit(solution)/shard_map/ppermute | solution.py:52
  34.0 19.0 %collective-permute-start.5 = (f32[32,1536]{1,0:T(8,128)S(1)}, f32[32,1536]{1,0:T(8,128)S(1)}, u32[]{:S(2)}, u32[]{:S(2)}) collective-permute-start(f32[32,1536]{1,0:T(8,128)S(1)} %get-tuple-element.22.refs_0_), channel_id=1, source_target_pairs={{0,16},{1,17},{2,18},{3,19},{4,20},{5,21},{6,22},{7,23},{8,24},{9,... | collective-permute-start | bytes 589832 | tf_op jit(solution)/shard_map/ppermute | solution.py:52
  38.2 18.6 %collective-permute-start.6 = (f32[32,1536]{1,0:T(8,128)S(1)}, f32[32,1536]{1,0:T(8,128)S(1)}, u32[]{:S(2)}, u32[]{:S(2)}) collective-permute-start(f32[32,1536]{1,0:T(8,128)S(1)} %get-tuple-element.22.refs_0_), channel_id=1, source_target_pairs={{0,48},{1,49},{2,50},{3,51},{4,52},{5,53},{6,54},{7,55},{8,56},{9,... | collective-permute-start | bytes 589832 | tf_op jit(solution)/shard_map/ppermute | solution.py:52
  49.2 13.8 %collective-permute-start.11 = (f32[64,1536]{1,0:T(8,128)S(1)}, f32[64,1536]{1,0:T(8,128)S(1)}, u32[]{:S(2)}, u32[]{:S(2)}) collective-permute-start(f32[64,1536]{1,0:T(8,128)S(1)} %slice.72), channel_id=1, source_target_pairs={{0,64},{1,65},{2,66},{3,67},{4,68},{5,69},{6,70},{7,71},{8,72},{9,... | collective-permute-start | bytes 1179656 | tf_op jit(solution)/shard_map/ppermute | solution.py:52
  50.0 13.0 %collective-permute-start.12 = (f32[64,1536]{1,0:T(8,128)S(1)}, f32[64,1536]{1,0:T(8,128)S(1)}, u32[]{:S(2)}, u32[]{:S(2)}) collective-permute-start(f32[64,1536]{1,0:T(8,128)S(1)} %slice.73), channel_id=1, source_target_pairs={{0,192},{1,193},{2,194},{3,195},{4,196},{5,197},{6,198},{7,199},{8... | collective-permute-start | bytes 1179656 | tf_op jit(solution)/shard_map/ppermute | solution.py:52
  53.0 8.0 %collective-permute-start.7 = (f32[16,1536]{1,0:T(8,128)S(1)}, f32[16,1536]{1,0:T(8,128)S(1)}, u32[]{:S(2)}, u32[]{:S(2)}) collective-permute-start(f32[16,1536]{1,0:T(8,128)S(1)} %slice.70), channel_id=1, source_target_pairs={{0,16},{1,17},{2,18},{3,19},{4,20},{5,21},{6,22},{7,23},{8,24},{9,... | collective-permute-start | bytes 294920 | tf_op jit(solution)/shard_map/ppermute | solution.py:52
  65.0 18.1 %collective-permute-start.19 = (f32[128,1536]{1,0:T(8,128)}, f32[128,1536]{1,0:T(8,128)}, u32[]{:S(2)}, u32[]{:S(2)}) collective-permute-start(f32[128,1536]{1,0:T(8,128)} %get-tuple-element.29.c0), channel_id=1, source_target_pairs={{0,64},{1,65},{2,66},{3,67},{4,68},{5,69},{6,70},{7,71},{8,72},{9,... | collective-permute-start | bytes 2359304 | tf_op jit(solution)/shard_map/ppermute | solution.py:52
  65.2 19.1 %collective-permute-start.20 = (f32[128,1536]{1,0:T(8,128)}, f32[128,1536]{1,0:T(8,128)}, u32[]{:S(2)}, u32[]{:S(2)}) collective-permute-start(f32[128,1536]{1,0:T(8,128)} %get-tuple-element.29.c0), channel_id=1, source_target_pairs={{0,192},{1,193},{2,194},{3,195},{4,196},{5,197},{6,198},{7,199},{8... | collective-permute-start | bytes 2359304 | tf_op jit(solution)/shard_map/ppermute | solution.py:52
  84.2 9.1 %collective-permute-start.21 = (f32[64,1536]{1,0:T(8,128)S(1)}, f32[64,1536]{1,0:T(8,128)S(1)}, u32[]{:S(2)}, u32[]{:S(2)}) collective-permute-start(f32[64,1536]{1,0:T(8,128)S(1)} %slice.75), channel_id=1, source_target_pairs={{0,64},{1,65},{2,66},{3,67},{4,68},{5,69},{6,70},{7,71},{8,72},{9,... | collective-permute-start | bytes 1179656 | tf_op jit(solution)/shard_map/ppermute | solution.py:52
  85.3 8.6 %collective-permute-start.22 = (f32[64,1536]{1,0:T(8,128)S(1)}, f32[64,1536]{1,0:T(8,128)S(1)}, u32[]{:S(2)}, u32[]{:S(2)}) collective-permute-start(f32[64,1536]{1,0:T(8,128)S(1)} %slice.76), channel_id=1, source_target_pairs={{0,192},{1,193},{2,194},{3,195},{4,196},{5,197},{6,198},{7,199},{8... | collective-permute-start | bytes 1179656 | tf_op jit(solution)/shard_map/ppermute | solution.py:52
  88.6 18.8 %collective-permute-start.14 = (f32[128,768]{1,0:T(8,128)S(1)}, f32[128,768]{1,0:T(8,128)S(1)}, u32[]{:S(2)}, u32[]{:S(2)}) collective-permute-start(f32[128,768]{1,0:T(8,128)S(1)} %get-tuple-element.26.refs_1_), channel_id=1, source_target_pairs={{0,2},{1,3},{2,4},{3,5},{4,6},{5,7},{6,0},{7,1},{8,10},{9,11},{10,... | collective-permute-start | bytes 1179656 | tf_op jit(solution)/shard_map/ppermute | solution.py:52
  88.9 21.2 %collective-permute-start.15 = (f32[128,768]{1,0:T(8,128)}, f32[128,768]{1,0:T(8,128)}, u32[]{:S(2)}, u32[]{:S(2)}) collective-permute-start(f32[128,768]{1,0:T(8,128)} %get-tuple-element.27), channel_id=1, source_target_pairs={{0,6},{1,7},{2,0},{3,1},{4,2},{5,3},{6,4},{7,5},{8,14},{9,15},{10,... | collective-permute-start | bytes 1179656 | tf_op jit(solution)/shard_map/ppermute | solution.py:52
  90.7 19.4 %collective-permute-start.16 = (f32[128,768]{1,0:T(8,128)}, f32[128,768]{1,0:T(8,128)}, u32[]{:S(2)}, u32[]{:S(2)}) collective-permute-start(f32[128,768]{1,0:T(8,128)} %get-tuple-element.28), channel_id=1, source_target_pairs={{0,4},{1,5},{2,6},{3,7},{4,0},{5,1},{6,2},{7,3},{8,12},{9,13},{10,... | collective-permute-start | bytes 1179656 | tf_op jit(solution)/shard_map/ppermute | solution.py:52
  105.4 11.3 %collective-permute-start.23 = (f32[128,768]{1,0:T(8,128)}, f32[128,768]{1,0:T(8,128)S(1)}, u32[]{:S(2)}, u32[]{:S(2)}) collective-permute-start(f32[128,768]{1,0:T(8,128)} %get-tuple-element.31), channel_id=1, source_target_pairs={{0,2},{1,3},{2,4},{3,5},{4,6},{5,7},{6,0},{7,1},{8,10},{9,11},{10,... | collective-permute-start | bytes 1179656 | tf_op jit(solution)/shard_map/ppermute | solution.py:52
  105.6 16.6 %collective-permute-start.24 = (f32[128,768]{1,0:T(8,128)}, f32[128,768]{1,0:T(8,128)S(1)}, u32[]{:S(2)}, u32[]{:S(2)}) collective-permute-start(f32[128,768]{1,0:T(8,128)} %get-tuple-element.32), channel_id=1, source_target_pairs={{0,6},{1,7},{2,0},{3,1},{4,2},{5,3},{6,4},{7,5},{8,14},{9,15},{10,... | collective-permute-start | bytes 1179656 | tf_op jit(solution)/shard_map/ppermute | solution.py:52
  108.2 14.0 %collective-permute-start.25 = (f32[128,768]{1,0:T(8,128)}, f32[128,768]{1,0:T(8,128)S(1)}, u32[]{:S(2)}, u32[]{:S(2)}) collective-permute-start(f32[128,768]{1,0:T(8,128)} %get-tuple-element.33), channel_id=1, source_target_pairs={{0,4},{1,5},{2,6},{3,7},{4,0},{5,1},{6,2},{7,3},{8,12},{9,13},{10,... | collective-permute-start | bytes 1179656 | tf_op jit(solution)/shard_map/ppermute | solution.py:52
  111.7 11.3 %collective-permute-start.17 = (f32[2,32,768]{2,1,0:T(8,128)S(1)}, f32[2,32,768]{2,1,0:T(8,128)S(1)}, u32[]{:S(2)}, u32[]{:S(2)}) collective-permute-start(f32[2,32,768]{2,1,0:T(8,128)S(1)} %dynamic-slice_bitcast_fusion.1), channel_id=1, source_target_pairs={{0,8},{1,9},{2,10},{3,11},{4,12},{5,13},{6,14},{7,15},{8,0},{9,1},... | collective-permute-start | bytes 589832 | tf_op jit(solution)/shard_map/ppermute | solution.py:52
  128.2 11.2 %collective-permute-start.27 = (f32[32,768]{1,0:T(8,128)S(1)}, f32[32,768]{1,0:T(8,128)S(1)}, u32[]{:S(2)}, u32[]{:S(2)}) collective-permute-start(f32[32,768]{1,0:T(8,128)S(1)} %get-tuple-element.59), channel_id=1, source_target_pairs={{0,1},{1,0},{2,3},{3,2},{4,5},{5,4},{6,7},{7,6},{8,9},{9,8},{10,11... | collective-permute-start | bytes 294920 | tf_op jit(solution)/shard_map/ppermute | solution.py:52
  128.3 16.6 %collective-permute-start.28 = (f32[64,768]{1,0:T(8,128)S(1)}, f32[64,768]{1,0:T(8,128)S(1)}, u32[]{:S(2)}, u32[]{:S(2)}) collective-permute-start(f32[64,768]{1,0:T(8,128)S(1)} %maximum_select_fusion), channel_id=1, source_target_pairs={{0,0},{1,160},{2,96},{3,192},{4,128},{5,32},{6,224},{7,64},{8,16},... | collective-permute-start | bytes 589832 | tf_op jit(solution)/shard_map/ppermute | solution.py:52
  139.4 15.0 %collective-permute-start.30 = (f32[64,768]{1,0:T(8,128)S(1)}, f32[64,768]{1,0:T(8,128)S(1)}, u32[]{:S(2)}, u32[]{:S(2)}) collective-permute-start(f32[64,768]{1,0:T(8,128)S(1)} %maximum_select_fusion.1), channel_id=1, source_target_pairs={{0,0},{1,160},{2,96},{3,192},{4,128},{5,32},{6,224},{7,64},{8,16},... | collective-permute-start | bytes 589832 | tf_op jit(solution)/shard_map/ppermute | solution.py:52
  145.0 9.5 %collective-permute-start.29 = (f32[64,768]{1,0:T(8,128)S(1)}, f32[64,768]{1,0:T(8,128)S(1)}, u32[]{:S(2)}, u32[]{:S(2)}) collective-permute-start(f32[64,768]{1,0:T(8,128)S(1)} %collective-permute-done.28.refs_4_), channel_id=1, source_target_pairs={{0,1},{1,0},{2,3},{3,2},{4,5},{5,4},{6,7},{7,6},{8,9},{9,8},{10,11... | collective-permute-start | bytes 589832 | tf_op jit(solution)/shard_map/ppermute | solution.py:52
  158.5 15.9 %collective-permute-start.32 = (f32[256,128]{1,0:T(8,128)S(1)}, f32[256,128]{1,0:T(8,128)S(1)}, u32[]{:S(2)}, u32[]{:S(2)}) collective-permute-start(f32[256,128]{1,0:T(8,128)S(1)} %get-tuple-element.39), channel_id=1, source_target_pairs={{0,2},{1,3},{2,4},{3,5},{4,6},{5,7},{6,0},{7,1},{8,10},{9,11},{10,... | collective-permute-start | bytes 393224 | tf_op jit(solution)/shard_map/ppermute | solution.py:52
  158.6 18.0 %collective-permute-start.33 = (f32[256,128]{1,0:T(8,128)S(1)}, f32[256,128]{1,0:T(8,128)S(1)}, u32[]{:S(2)}, u32[]{:S(2)}) collective-permute-start(f32[256,128]{1,0:T(8,128)S(1)} %get-tuple-element.40), channel_id=1, source_target_pairs={{0,6},{1,7},{2,0},{3,1},{4,2},{5,3},{6,4},{7,5},{8,14},{9,15},{10,... | collective-permute-start | bytes 393224 | tf_op jit(solution)/shard_map/ppermute | solution.py:52
  166.8 13.8 %collective-permute-start.34 = (f32[256,128]{1,0:T(8,128)S(1)}, f32[256,128]{1,0:T(8,128)S(1)}, u32[]{:S(2)}, u32[]{:S(2)}) collective-permute-start(f32[256,128]{1,0:T(8,128)S(1)} %get-tuple-element.41), channel_id=1, source_target_pairs={{0,4},{1,5},{2,6},{3,7},{4,0},{5,1},{6,2},{7,3},{8,12},{9,13},{10,... | collective-permute-start | bytes 393224 | tf_op jit(solution)/shard_map/ppermute | solution.py:52
  180.7 6.4 %collective-permute-start.35 = (f32[2,64,128]{2,1,0:T(8,128)S(1)}, f32[2,64,128]{2,1,0:T(8,128)S(1)}, u32[]{:S(2)}, u32[]{:S(2)}) collective-permute-start(f32[2,64,128]{2,1,0:T(8,128)S(1)} %dynamic-slice_bitcast_fusion.6), channel_id=1, source_target_pairs={{0,8},{1,9},{2,10},{3,11},{4,12},{5,13},{6,14},{7,15},{8,0},{9,1},... | collective-permute-start | bytes 196616 | tf_op jit(solution)/shard_map/ppermute | solution.py:52
  188.4 14.4 %collective-permute-start.37 = (f32[128,128]{1,0:T(8,128)S(1)}, f32[128,128]{1,0:T(8,128)S(1)}, u32[]{:S(2)}, u32[]{:S(2)}) collective-permute-start(f32[128,128]{1,0:T(8,128)S(1)} %maximum_select_fusion.2), channel_id=1, source_target_pairs={{0,0},{160,1},{96,2},{192,3},{128,4},{32,5},{224,6},{64,7},{16,8},... | collective-permute-start | bytes 196616 | tf_op jit(solution)/shard_map/ppermute | solution.py:52
  (32 other events, 309.4 us)

commit v3 on v2

--- a/solution.py
+++ b/solution.py
@@ -101,37 +101,45 @@
     return jnp.where(step == 3, 2, jnp.where(step == 2, 3, step))
 
 
-def product_kernel(rows, me_ref, c0, c1, c2, c3, c4, h0, l0, h1, l1, *refs):
-    outs, high_out, low_out, high, low, sep, sems = refs[:4], refs[4], refs[5], refs[6], refs[7], refs[8:12], refs[12]
-    loads = [pltpu.make_async_copy(src, dst, sems.at[i]) for i, (src, dst) in enumerate(zip((h0, l0, h1, l1), sep))]
+def product_kernel(rows, me_ref, *refs):
+    parts, sep, outs, high_out, low_out = refs[:5], refs[5:9], refs[9:13], refs[13], refs[14]
+    held, matrix, total, high, low, sems = refs[15:20], refs[20:24], refs[24], refs[25], refs[26], refs[27]
+    loads = [pltpu.make_async_copy(src, dst, sems.at[i]) for i, (src, dst) in enumerate(zip(parts + sep, held + matrix))]
     for load in loads:
         load.start()
     x, zh, y = me_ref[0], me_ref[1], me_ref[2]
     for sx in range(4):
+        loads[sx].wait()
+        if sx == 3:
+            loads[4].wait()
         for sz in range(4):
-            ref, start = (c0, c1, c2, c3)[sx], sz * rows
+            ref, start = held[sx], sz * rows
             if sx == 3 and sz >= 2:
-                ref, start = c4, start - 2 * rows
+                ref, start = held[4], start - 2 * rows
             xs = lax.rem(x - STEPS[sx] + 4, 4)
             zs = lax.rem(zh - STEPS[sz] + 4, 4)
             to = ring_slot(2 * lax.rem(xs, 2) + zs // 2 - y)
             place = (to * 2 + xs // 2) * 2 + lax.rem(zs, 2)
             at = pl.ds(pl.multiple_of(place * rows, rows), rows)
             store_split(high, low, (at, slice(None)), ref[start : start + rows, :])
-    stores = [pltpu.make_async_copy(high, high_out, sems.at[4]), pltpu.make_async_copy(low, low_out, sems.at[5])]
+    stores = [pltpu.make_async_copy(high, high_out, sems.at[9]), pltpu.make_async_copy(low, low_out, sems.at[10])]
     for store in stores:
         store.start()
-    for load in loads:
+    for load in loads[5:]:
         load.wait()
-    h0, l0, h1, l1 = sep
+    h0, l0, h1, l1 = matrix
     own, other = slice(0, BS), slice(BS, 2 * BS)
-    for n in range(0, BS, 256):
-        cols = slice(n, n + 256)
+    for n in range(3):
+        cols = slice(256 * n, 256 * (n + 1))
         sums = dot_nt(high[:, own], h0[cols, :]) + dot_nt(high[:, other], h1[cols, :])
         sums += dot_nt(low[:, own], h0[cols, :]) + dot_nt(low[:, other], h1[cols, :])
         sums += dot_nt(high[:, own], l0[cols, :]) + dot_nt(high[:, other], l1[cols, :])
+        total[:, cols] = sums
         for i, out in enumerate(outs):
-            out[:, cols] = sums[4 * rows * i : 4 * rows * (i + 1)]
+            piece = total.at[pl.ds(4 * rows * i, 4 * rows), pl.ds(256 * n, 256)]
+            store = pltpu.make_async_copy(piece, out.at[:, pl.ds(256 * n, 256)], sems.at[11 + 4 * n + i])
+            store.start()
+            stores.append(store)
     for store in stores:
         store.wait()
 
@@ -142,12 +150,14 @@
         functools.partial(product_kernel, rows),
         out_shape=[jax.ShapeDtypeStruct((4 * rows, BS), jnp.float32)] * 4
         + [jax.ShapeDtypeStruct((16 * rows, 2 * BS), jnp.bfloat16)] * 2,
-        in_specs=[SMEM] + [VMEM] * 5 + [HBM] * 4,
-        out_specs=[VMEM] * 4 + [HBM] * 2,
-        scratch_shapes=[pltpu.VMEM((16 * rows, 2 * BS), jnp.bfloat16)] * 2
+        in_specs=[SMEM] + [HBM] * 9,
+        out_specs=[HBM] * 6,
+        scratch_shapes=[pltpu.VMEM(part.shape, jnp.float32) for part in parts]
         + [pltpu.VMEM((BS, BS), jnp.bfloat16)] * 4
-        + [pltpu.SemaphoreType.DMA((6,))],
-        compiler_params=pltpu.CompilerParams(vmem_limit_bytes=18 << 20),
+        + [pltpu.VMEM((16 * rows, BS), jnp.float32)]
+        + [pltpu.VMEM((16 * rows, 2 * BS), jnp.bfloat16)] * 2
+        + [pltpu.SemaphoreType.DMA((23,))],
+        compiler_params=pltpu.CompilerParams(vmem_limit_bytes=56 << 20),
         cost_estimate=COST,
         name="product",
     )(me, *parts, *sep)

time: 205 us -> 203 us (level)
  local copies, waits for them, and re-layouts: 17.3 us -> 7.15 us
  Pallas kernels: 19 us -> 23.6 us
  starting transfers between devices: 82.3 us -> 84.9 us
  waiting for transfers between devices: 77.4 us -> 80 us
    unnamed x54 -> x50, local copies, waits for them, and re-layouts: 13.6 us -> 5.54 us
    pallas_call x2, Pallas kernels: 15.3 us -> 19.9 us  [product(): pl.pallas_call(functools.partial(product_kernel, rows), out_shape=[jax.Sh...]
    ppermute x38, waiting for transfers between devices: 77.4 us -> 80 us  [send(): return lax.ppermute(value, AXES, pairs)]
    ppermute x38, starting transfers between devices: 82.3 us -> 84.9 us  [send(): return lax.ppermute(value, AXES, pairs)]
  transfers between devices with their start and end apart: 38 -> 38, of which waited for: 22 -> 21; matrix products, arithmetic and copies ran while one was open for 5% -> 3% of each run, Pallas kernels for 8% -> 10%
where the time goes in v3:
time: 203 us; the launch traced here: 202 us
  starting transfers between devices  84.9 us (42%)
  waiting for transfers between devices  80 us (39%)
  Pallas kernels  23.6 us (12%)
  local copies, waits for them, and re-layouts  7.15 us (4%)
  other arithmetic  4 us (2%)
  between operations  2.4 us (1%)
    ppermute x38, starting transfers between devices, send(): return lax.ppermute(value, AXES, pairs)  84.9 us
    ppermute x38, waiting for transfers between devices, send(): return lax.ppermute(value, AXES, pairs)  80 us
    pallas_call x2, Pallas kernels, product(): pl.pallas_call(functools.partial(product_kernel, rows), out_shape=[jax.Sh...  19.9 us
    unnamed x50, local copies, waits for them, and re-layouts  5.54 us
  transfers between devices with their start and end apart: 38, of which 21 were waited for; matrix products, arithmetic and copies ran while one was open for 3% of the time, Pallas kernels for 10%

profile of v3, /device:TPU:24, one launch (start us, length us, event | category | flops | bytes accessed | tf_op | source)
XLA Modules:
  0.0 202.1 jit_solution(6503764473625934369)
XLA Ops:
  5.6 3.4 %collective-permute-start.1 = (f32[32,1536]{1,0:T(8,128)S(1)}, f32[32,1536]{1,0:T(8,128)S(1)}, u32[]{:S(2)}, u32[]{:S(2)}) collective-permute-start(f32[32,1536]{1,0:T(8,128)S(1)} %get-tuple-element.49.refs_0_), channel_id=1, source_target_pairs={{0,16},{1,17},{2,18},{3,19},{4,20},{5,21},{6,22},{7,23},{8,24},{9,... | collective-permute-start | bytes 589832 | tf_op jit(solution)/shard_map/ppermute | solution.py:52
  9.0 3.1 %collective-permute-start.2 = (f32[32,1536]{1,0:T(8,128)S(1)}, f32[32,1536]{1,0:T(8,128)S(1)}, u32[]{:S(2)}, u32[]{:S(2)}) collective-permute-start(f32[32,1536]{1,0:T(8,128)S(1)} %get-tuple-element.49.refs_0_), channel_id=1, source_target_pairs={{0,48},{1,49},{2,50},{3,51},{4,52},{5,53},{6,54},{7,55},{8,56},{9,... | collective-permute-start | bytes 589832 | tf_op jit(solution)/shard_map/ppermute | solution.py:52
  12.1 6.9 %collective-permute-done.1.refs_1_ = f32[32,1536]{1,0:T(8,128)S(1)} collective-permute-done((f32[32,1536]{1,0:T(8,128)S(1)}, f32[32,1536]{1,0:T(8,128)S(1)}, u32[]{:S(2)}, u32[]{:S(2)}) %collective-permute-start.1) | collective-permute-done | bytes 196640 | tf_op jit(solution)/shard_map/ppermute | solution.py:52
  19.0 3.2 %collective-permute-start.3 = (f32[16,1536]{1,0:T(8,128)S(1)}, f32[16,1536]{1,0:T(8,128)S(1)}, u32[]{:S(2)}, u32[]{:S(2)}) collective-permute-start(f32[16,1536]{1,0:T(8,128)S(1)} %slice.68), channel_id=1, source_target_pairs={{0,16},{1,17},{2,18},{3,19},{4,20},{5,21},{6,22},{7,23},{8,24},{9,... | collective-permute-start | bytes 294920 | tf_op jit(solution)/shard_map/ppermute | solution.py:52
  22.9 2.8 %collective-permute-start.4 = (f32[16,1536]{1,0:T(8,128)S(1)}, f32[16,1536]{1,0:T(8,128)S(1)}, u32[]{:S(2)}, u32[]{:S(2)}) collective-permute-start(f32[16,1536]{1,0:T(8,128)S(1)} %slice.69), channel_id=1, source_target_pairs={{0,48},{1,49},{2,50},{3,51},{4,52},{5,53},{6,54},{7,55},{8,56},{9,... | collective-permute-start | bytes 294920 | tf_op jit(solution)/shard_map/ppermute | solution.py:52
  25.7 2.3 %collective-permute-done.3.refs_3_ = f32[16,1536]{1,0:T(8,128)S(1)} collective-permute-done((f32[16,1536]{1,0:T(8,128)S(1)}, f32[16,1536]{1,0:T(8,128)S(1)}, u32[]{:S(2)}, u32[]{:S(2)}) %collective-permute-start.3) | collective-permute-done | bytes 98336 | tf_op jit(solution)/shard_map/ppermute | solution.py:52
  28.0 2.6 %collective-permute-done.4.refs_4_ = f32[16,1536]{1,0:T(8,128)S(1)} collective-permute-done((f32[16,1536]{1,0:T(8,128)S(1)}, f32[16,1536]{1,0:T(8,128)S(1)}, u32[]{:S(2)}, u32[]{:S(2)}) %collective-permute-start.4) | collective-permute-done | bytes 98336 | tf_op jit(solution)/shard_map/ppermute | solution.py:52
  34.0 4.2 %collective-permute-start.5 = (f32[32,1536]{1,0:T(8,128)S(1)}, f32[32,1536]{1,0:T(8,128)S(1)}, u32[]{:S(2)}, u32[]{:S(2)}) collective-permute-start(f32[32,1536]{1,0:T(8,128)S(1)} %get-tuple-element.22.refs_0_), channel_id=1, source_target_pairs={{0,16},{1,17},{2,18},{3,19},{4,20},{5,21},{6,22},{7,23},{8,24},{9,... | collective-permute-start | bytes 589832 | tf_op jit(solution)/shard_map/ppermute | solution.py:52
  38.2 10.9 %collective-permute-done.9.refs_6_.refs_1_ = f32[128,1536]{1,0:T(8,128)S(1)} collective-permute-done((f32[128,1536]{1,0:T(8,128)S(1)}, f32[128,1536]{1,0:T(8,128)S(1)}, u32[]{:S(2)}, u32[]{:S(2)}) %collective-permute-start.9) | collective-permute-done | bytes 786464 | tf_op jit(solution)/shard_map/ppermute | solution.py:52
  50.0 2.6 %collective-permute-start.12 = (f32[64,1536]{1,0:T(8,128)S(1)}, f32[64,1536]{1,0:T(8,128)S(1)}, u32[]{:S(2)}, u32[]{:S(2)}) collective-permute-start(f32[64,1536]{1,0:T(8,128)S(1)} %slice.73), channel_id=1, source_target_pairs={{0,192},{1,193},{2,194},{3,195},{4,196},{5,197},{6,198},{7,199},{8... | collective-permute-start | bytes 1179656 | tf_op jit(solution)/shard_map/ppermute | solution.py:52
  53.0 3.8 %collective-permute-start.7 = (f32[16,1536]{1,0:T(8,128)S(1)}, f32[16,1536]{1,0:T(8,128)S(1)}, u32[]{:S(2)}, u32[]{:S(2)}) collective-permute-start(f32[16,1536]{1,0:T(8,128)S(1)} %slice.70), channel_id=1, source_target_pairs={{0,16},{1,17},{2,18},{3,19},{4,20},{5,21},{6,22},{7,23},{8,24},{9,... | collective-permute-start | bytes 294920 | tf_op jit(solution)/shard_map/ppermute | solution.py:52
  65.2 3.1 %collective-permute-start.20 = (f32[128,1536]{1,0:T(8,128)}, f32[128,1536]{1,0:T(8,128)S(1)}, u32[]{:S(2)}, u32[]{:S(2)}) collective-permute-start(f32[128,1536]{1,0:T(8,128)} %get-tuple-element.29.refs_0_), channel_id=1, source_target_pairs={{0,192},{1,193},{2,194},{3,195},{4,196},{5,197},{6,198},{7,199},{8... | collective-permute-start | bytes 2359304 | tf_op jit(solution)/shard_map/ppermute | solution.py:52
  68.8 10.0 %product.2 = (f32[128,768]{1,0:T(8,128)}, f32[128,768]{1,0:T(8,128)}, f32[128,768]{1,0:T(8,128)}, f32[128,768]{1,0:T(8,128)}, bf16[512,1536]{1,0:T(8,128)(2,1)}, /*index=5*/bf16[512,1536]{1,0:T(8,128)(2,1)}) custom-call(s32[3]{0:T(128)} %pad_add_fusion.me_ref, f32[128,1536]{1,0:T(8,128)} %copy-done.7, f32[128,1536]{1,0:T(8,128)} %copy-done.4, ...), custom_call_target="tpu_custom_call" | custom-call | flops 1000 | bytes 1000 | tf_op jit(solution)/shard_map/product/pallas_call | solution.py:149
  78.8 4.2 %collective-permute-done.19.refs_0_ = f32[128,1536]{1,0:T(8,128)S(1)} collective-permute-done((f32[128,1536]{1,0:T(8,128)}, f32[128,1536]{1,0:T(8,128)S(1)}, u32[]{:S(2)}, u32[]{:S(2)}) %collective-permute-start.19) | collective-permute-done | bytes 786464 | tf_op jit(solution)/shard_map/ppermute | solution.py:52
  84.1 3.3 %collective-permute-start.22 = (f32[64,1536]{1,0:T(8,128)S(1)}, f32[64,1536]{1,0:T(8,128)S(1)}, u32[]{:S(2)}, u32[]{:S(2)}) collective-permute-start(f32[64,1536]{1,0:T(8,128)S(1)} %slice.76), channel_id=1, source_target_pairs={{0,192},{1,193},{2,194},{3,195},{4,196},{5,197},{6,198},{7,199},{8... | collective-permute-start | bytes 1179656 | tf_op jit(solution)/shard_map/ppermute | solution.py:52
  90.7 2.4 %collective-permute-done.21.refs_3_ = f32[64,1536]{1,0:T(8,128)S(1)} collective-permute-done((f32[64,1536]{1,0:T(8,128)S(1)}, f32[64,1536]{1,0:T(8,128)S(1)}, u32[]{:S(2)}, u32[]{:S(2)}) %collective-permute-start.21) | collective-permute-done | bytes 393248 | tf_op jit(solution)/shard_map/ppermute | solution.py:52
  94.6 9.9 %product.3 = (f32[128,768]{1,0:T(8,128)}, f32[128,768]{1,0:T(8,128)}, f32[128,768]{1,0:T(8,128)}, f32[128,768]{1,0:T(8,128)}, bf16[512,1536]{1,0:T(8,128)(2,1)}, /*index=5*/bf16[512,1536]{1,0:T(8,128)(2,1)}) custom-call(s32[3]{0:T(128)} %pad_add_fusion.me_ref, f32[128,1536]{1,0:T(8,128)} %get-tuple-element.29.refs_0_, f32[128,1536]{1,0:T(8,128)} %copy-done.6, ...), custom_call_target="tpu_custom_call" | custom-call | flops 1000 | bytes 1000 | tf_op jit(solution)/shard_map/product/pallas_call | solution.py:149
  109.2 6.0 %collective-permute-done.23 = f32[128,768]{1,0:T(8,128)S(1)} collective-permute-done((f32[128,768]{1,0:T(8,128)}, f32[128,768]{1,0:T(8,128)S(1)}, u32[]{:S(2)}, u32[]{:S(2)}) %collective-permute-start.23) | collective-permute-done | bytes 393248 | tf_op jit(solution)/shard_map/ppermute | solution.py:52
  115.2 5.6 %collective-permute-done.24 = f32[128,768]{1,0:T(8,128)S(1)} collective-permute-done((f32[128,768]{1,0:T(8,128)}, f32[128,768]{1,0:T(8,128)S(1)}, u32[]{:S(2)}, u32[]{:S(2)}) %collective-permute-start.24) | collective-permute-done | bytes 393248 | tf_op jit(solution)/shard_map/ppermute | solution.py:52
  122.1 4.6 %collective-permute-done.26 = f32[2,32,768]{2,1,0:T(8,128)S(1)} collective-permute-done((f32[2,32,768]{2,1,0:T(8,128)S(1)}, f32[2,32,768]{2,1,0:T(8,128)S(1)}, u32[]{:S(2)}, u32[]{:S(2)}) %collective-permute-start.26) | collective-permute-done | bytes 196640 | tf_op jit(solution)/shard_map/ppermute | solution.py:52
  126.9 10.7 %collective-permute-start.28 = (f32[64,768]{1,0:T(8,128)S(1)}, f32[64,768]{1,0:T(8,128)S(1)}, u32[]{:S(2)}, u32[]{:S(2)}) collective-permute-start(f32[64,768]{1,0:T(8,128)S(1)} %maximum_select_fusion), channel_id=1, source_target_pairs={{0,0},{1,160},{2,96},{3,192},{4,128},{5,32},{6,224},{7,64},{8,16},... | collective-permute-start | bytes 589832 | tf_op jit(solution)/shard_map/ppermute | solution.py:52
  137.6 2.8 %collective-permute-start.30 = (f32[64,768]{1,0:T(8,128)S(1)}, f32[64,768]{1,0:T(8,128)S(1)}, u32[]{:S(2)}, u32[]{:S(2)}) collective-permute-start(f32[64,768]{1,0:T(8,128)S(1)} %maximum_select_fusion.1), channel_id=1, source_target_pairs={{0,0},{1,160},{2,96},{3,192},{4,128},{5,32},{6,224},{7,64},{8,16},... | collective-permute-start | bytes 589832 | tf_op jit(solution)/shard_map/ppermute | solution.py:52
  140.4 8.5 %collective-permute-done.28.refs_4_ = f32[64,768]{1,0:T(8,128)S(1)} collective-permute-done((f32[64,768]{1,0:T(8,128)S(1)}, f32[64,768]{1,0:T(8,128)S(1)}, u32[]{:S(2)}, u32[]{:S(2)}) %collective-permute-start.28) | collective-permute-done | bytes 196640 | tf_op jit(solution)/shard_map/ppermute | solution.py:52
  148.9 3.3 %collective-permute-done.30.refs_6_ = f32[64,768]{1,0:T(8,128)S(1)} collective-permute-done((f32[64,768]{1,0:T(8,128)S(1)}, f32[64,768]{1,0:T(8,128)S(1)}, u32[]{:S(2)}, u32[]{:S(2)}) %collective-permute-start.30) | collective-permute-done | bytes 196640 | tf_op jit(solution)/shard_map/ppermute | solution.py:52
  153.7 2.6 %gram.1 = (f32[256,128]{1,0:T(8,128)S(1)}, f32[256,128]{1,0:T(8,128)S(1)}, f32[256,128]{1,0:T(8,128)S(1)}, f32[256,128]{1,0:T(8,128)S(1)}) custom-call(bf16[512,1536]{1,0:T(8,128)(2,1)S(1)} %copy-done.10, bf16[512,1536]{1,0:T(8,128)(2,1)S(1)} %copy-done.11, bf16[512,1536]{1,0:T(8,128)(2,1)S(1)} %copy-done.12, bf16[512,1536]{1,0:T(8,128)(2,1)S(1)} %copy-done.13, ...), custom_call_target="tpu_custom_call" | custom-call | flops 1000 | bytes 1000 | tf_op jit(solution)/shard_map/gram/pallas_call | solution.py:186
  156.4 9.1 %collective-permute-start.33 = (f32[256,128]{1,0:T(8,128)S(1)}, f32[256,128]{1,0:T(8,128)S(1)}, u32[]{:S(2)}, u32[]{:S(2)}) collective-permute-start(f32[256,128]{1,0:T(8,128)S(1)} %get-tuple-element.40), channel_id=1, source_target_pairs={{0,6},{1,7},{2,0},{3,1},{4,2},{5,3},{6,4},{7,5},{8,14},{9,15},{10,... | collective-permute-start | bytes 393224 | tf_op jit(solution)/shard_map/ppermute | solution.py:52
  165.5 6.8 %collective-permute-start.34 = (f32[256,128]{1,0:T(8,128)S(1)}, f32[256,128]{1,0:T(8,128)S(1)}, u32[]{:S(2)}, u32[]{:S(2)}) collective-permute-start(f32[256,128]{1,0:T(8,128)S(1)} %get-tuple-element.41), channel_id=1, source_target_pairs={{0,4},{1,5},{2,6},{3,7},{4,0},{5,1},{6,2},{7,3},{8,12},{9,13},{10,... | collective-permute-start | bytes 393224 | tf_op jit(solution)/shard_map/ppermute | solution.py:52
  172.3 2.3 %collective-permute-done.33 = f32[256,128]{1,0:T(8,128)S(1)} collective-permute-done((f32[256,128]{1,0:T(8,128)S(1)}, f32[256,128]{1,0:T(8,128)S(1)}, u32[]{:S(2)}, u32[]{:S(2)}) %collective-permute-start.33) | collective-permute-done | bytes 131104 | tf_op jit(solution)/shard_map/ppermute | solution.py:52
  174.6 4.0 %collective-permute-done.34 = f32[256,128]{1,0:T(8,128)S(1)} collective-permute-done((f32[256,128]{1,0:T(8,128)S(1)}, f32[256,128]{1,0:T(8,128)S(1)}, u32[]{:S(2)}, u32[]{:S(2)}) %collective-permute-start.34) | collective-permute-done | bytes 131104 | tf_op jit(solution)/shard_map/ppermute | solution.py:52
  178.6 4.9 %collective-permute-start.35 = (f32[2,64,128]{2,1,0:T(8,128)S(1)}, f32[2,64,128]{2,1,0:T(8,128)S(1)}, u32[]{:S(2)}, u32[]{:S(2)}) collective-permute-start(f32[2,64,128]{2,1,0:T(8,128)S(1)} %dynamic-slice_bitcast_fusion.6), channel_id=1, source_target_pairs={{0,8},{1,9},{2,10},{3,11},{4,12},{5,13},{6,14},{7,15},{8,0},{9,1},... | collective-permute-start | bytes 196616 | tf_op jit(solution)/shard_map/ppermute | solution.py:52
  187.1 7.0 %collective-permute-start.37 = (f32[128,128]{1,0:T(8,128)S(1)}, f32[128,128]{1,0:T(8,128)S(1)}, u32[]{:S(2)}, u32[]{:S(2)}) collective-permute-start(f32[128,128]{1,0:T(8,128)S(1)} %maximum_select_fusion.2), channel_id=1, source_target_pairs={{0,0},{160,1},{96,2},{192,3},{128,4},{32,5},{224,6},{64,7},{16,8},... | collective-permute-start | bytes 196616 | tf_op jit(solution)/shard_map/ppermute | solution.py:52
  195.0 6.4 %collective-permute-done.37 = f32[128,128]{1,0:T(8,128)S(1)} collective-permute-done((f32[128,128]{1,0:T(8,128)S(1)}, f32[128,128]{1,0:T(8,128)S(1)}, u32[]{:S(2)}, u32[]{:S(2)}) %collective-permute-start.37) | collective-permute-done | bytes 65568 | tf_op jit(solution)/shard_map/ppermute | solution.py:52
  (134 shorter events, 36.6 us)
Async XLA Ops:
  0.6 56.7 %collective-permute-start.13 = (f32[768,768]{1,0:T(8,128)}, f32[768,768]{1,0:T(8,128)}, u32[]{:S(2)}, u32[]{:S(2)}) collective-permute-start(f32[768,768]{1,0:T(8,128)} %param.4), channel_id=1, source_target_pairs={{0,1},{1,0},{2,3},{3,2},{4,5},{5,4},{6,7},{7,6},{8,9},{9,8},{10,11... | collective-permute-start | bytes 7077896 | tf_op jit(solution)/shard_map/ppermute | solution.py:52
  5.6 13.4 %collective-permute-start.1 = (f32[32,1536]{1,0:T(8,128)S(1)}, f32[32,1536]{1,0:T(8,128)S(1)}, u32[]{:S(2)}, u32[]{:S(2)}) collective-permute-start(f32[32,1536]{1,0:T(8,128)S(1)} %get-tuple-element.49.refs_0_), channel_id=1, source_target_pairs={{0,16},{1,17},{2,18},{3,19},{4,20},{5,21},{6,22},{7,23},{8,24},{9,... | collective-permute-start | bytes 589832 | tf_op jit(solution)/shard_map/ppermute | solution.py:52
  9.0 13.8 %collective-permute-start.2 = (f32[32,1536]{1,0:T(8,128)S(1)}, f32[32,1536]{1,0:T(8,128)S(1)}, u32[]{:S(2)}, u32[]{:S(2)}) collective-permute-start(f32[32,1536]{1,0:T(8,128)S(1)} %get-tuple-element.49.refs_0_), channel_id=1, source_target_pairs={{0,48},{1,49},{2,50},{3,51},{4,52},{5,53},{6,54},{7,55},{8,56},{9,... | collective-permute-start | bytes 589832 | tf_op jit(solution)/shard_map/ppermute | solution.py:52
  19.0 9.0 %collective-permute-start.3 = (f32[16,1536]{1,0:T(8,128)S(1)}, f32[16,1536]{1,0:T(8,128)S(1)}, u32[]{:S(2)}, u32[]{:S(2)}) collective-permute-start(f32[16,1536]{1,0:T(8,128)S(1)} %slice.68), channel_id=1, source_target_pairs={{0,16},{1,17},{2,18},{3,19},{4,20},{5,21},{6,22},{7,23},{8,24},{9,... | collective-permute-start | bytes 294920 | tf_op jit(solution)/shard_map/ppermute | solution.py:52
  22.9 7.8 %collective-permute-start.4 = (f32[16,1536]{1,0:T(8,128)S(1)}, f32[16,1536]{1,0:T(8,128)S(1)}, u32[]{:S(2)}, u32[]{:S(2)}) collective-permute-start(f32[16,1536]{1,0:T(8,128)S(1)} %slice.69), channel_id=1, source_target_pairs={{0,48},{1,49},{2,50},{3,51},{4,52},{5,53},{6,54},{7,55},{8,56},{9,... | collective-permute-start | bytes 294920 | tf_op jit(solution)/shard_map/ppermute | solution.py:52
  30.7 18.4 %collective-permute-start.9 = (f32[128,1536]{1,0:T(8,128)S(1)}, f32[128,1536]{1,0:T(8,128)S(1)}, u32[]{:S(2)}, u32[]{:S(2)}) collective-permute-start(f32[128,1536]{1,0:T(8,128)S(1)} %get-tuple-element.23.refs_5_), channel_id=1, source_target_pairs={{0,64},{1,65},{2,66},{3,67},{4,68},{5,69},{6,70},{7,71},{8,72},{9,... | collective-permute-start | bytes 2359304 | tf_op jit(solution)/shard_map/ppermute | solution.py:52
  32.2 17.7 %collective-permute-start.10 = (f32[128,1536]{1,0:T(8,128)S(1)}, f32[128,1536]{1,0:T(8,128)S(1)}, u32[]{:S(2)}, u32[]{:S(2)}) collective-permute-start(f32[128,1536]{1,0:T(8,128)S(1)} %get-tuple-element.23.refs_5_), channel_id=1, source_target_pairs={{0,192},{1,193},{2,194},{3,195},{4,196},{5,197},{6,198},{7,199},{8... | collective-permute-start | bytes 2359304 | tf_op jit(solution)/shard_map/ppermute | solution.py:52
  34.0 19.0 %collective-permute-start.5 = (f32[32,1536]{1,0:T(8,128)S(1)}, f32[32,1536]{1,0:T(8,128)S(1)}, u32[]{:S(2)}, u32[]{:S(2)}) collective-permute-start(f32[32,1536]{1,0:T(8,128)S(1)} %get-tuple-element.22.refs_0_), channel_id=1, source_target_pairs={{0,16},{1,17},{2,18},{3,19},{4,20},{5,21},{6,22},{7,23},{8,24},{9,... | collective-permute-start | bytes 589832 | tf_op jit(solution)/shard_map/ppermute | solution.py:52
  38.2 18.6 %collective-permute-start.6 = (f32[32,1536]{1,0:T(8,128)S(1)}, f32[32,1536]{1,0:T(8,128)S(1)}, u32[]{:S(2)}, u32[]{:S(2)}) collective-permute-start(f32[32,1536]{1,0:T(8,128)S(1)} %get-tuple-element.22.refs_0_), channel_id=1, source_target_pairs={{0,48},{1,49},{2,50},{3,51},{4,52},{5,53},{6,54},{7,55},{8,56},{9,... | collective-permute-start | bytes 589832 | tf_op jit(solution)/shard_map/ppermute | solution.py:52
  49.1 13.8 %collective-permute-start.11 = (f32[64,1536]{1,0:T(8,128)S(1)}, f32[64,1536]{1,0:T(8,128)S(1)}, u32[]{:S(2)}, u32[]{:S(2)}) collective-permute-start(f32[64,1536]{1,0:T(8,128)S(1)} %slice.72), channel_id=1, source_target_pairs={{0,64},{1,65},{2,66},{3,67},{4,68},{5,69},{6,70},{7,71},{8,72},{9,... | collective-permute-start | bytes 1179656 | tf_op jit(solution)/shard_map/ppermute | solution.py:52
  50.0 13.0 %collective-permute-start.12 = (f32[64,1536]{1,0:T(8,128)S(1)}, f32[64,1536]{1,0:T(8,128)S(1)}, u32[]{:S(2)}, u32[]{:S(2)}) collective-permute-start(f32[64,1536]{1,0:T(8,128)S(1)} %slice.73), channel_id=1, source_target_pairs={{0,192},{1,193},{2,194},{3,195},{4,196},{5,197},{6,198},{7,199},{8... | collective-permute-start | bytes 1179656 | tf_op jit(solution)/shard_map/ppermute | solution.py:52
  53.0 8.0 %collective-permute-start.7 = (f32[16,1536]{1,0:T(8,128)S(1)}, f32[16,1536]{1,0:T(8,128)S(1)}, u32[]{:S(2)}, u32[]{:S(2)}) collective-permute-start(f32[16,1536]{1,0:T(8,128)S(1)} %slice.70), channel_id=1, source_target_pairs={{0,16},{1,17},{2,18},{3,19},{4,20},{5,21},{6,22},{7,23},{8,24},{9,... | collective-permute-start | bytes 294920 | tf_op jit(solution)/shard_map/ppermute | solution.py:52
  56.8 6.1 %collective-permute-start.8 = (f32[16,1536]{1,0:T(8,128)S(1)}, f32[16,1536]{1,0:T(8,128)S(1)}, u32[]{:S(2)}, u32[]{:S(2)}) collective-permute-start(f32[16,1536]{1,0:T(8,128)S(1)} %slice.71), channel_id=1, source_target_pairs={{0,48},{1,49},{2,50},{3,51},{4,52},{5,53},{6,54},{7,55},{8,56},{9,... | collective-permute-start | bytes 294920 | tf_op jit(solution)/shard_map/ppermute | solution.py:52
  65.0 18.0 %collective-permute-start.19 = (f32[128,1536]{1,0:T(8,128)}, f32[128,1536]{1,0:T(8,128)S(1)}, u32[]{:S(2)}, u32[]{:S(2)}) collective-permute-start(f32[128,1536]{1,0:T(8,128)} %get-tuple-element.29.refs_0_), channel_id=1, source_target_pairs={{0,64},{1,65},{2,66},{3,67},{4,68},{5,69},{6,70},{7,71},{8,72},{9,... | collective-permute-start | bytes 2359304 | tf_op jit(solution)/shard_map/ppermute | solution.py:52
  65.2 18.9 %collective-permute-start.20 = (f32[128,1536]{1,0:T(8,128)}, f32[128,1536]{1,0:T(8,128)S(1)}, u32[]{:S(2)}, u32[]{:S(2)}) collective-permute-start(f32[128,1536]{1,0:T(8,128)} %get-tuple-element.29.refs_0_), channel_id=1, source_target_pairs={{0,192},{1,193},{2,194},{3,195},{4,196},{5,197},{6,198},{7,199},{8... | collective-permute-start | bytes 2359304 | tf_op jit(solution)/shard_map/ppermute | solution.py:52
  84.0 9.1 %collective-permute-start.21 = (f32[64,1536]{1,0:T(8,128)S(1)}, f32[64,1536]{1,0:T(8,128)S(1)}, u32[]{:S(2)}, u32[]{:S(2)}) collective-permute-start(f32[64,1536]{1,0:T(8,128)S(1)} %slice.75), channel_id=1, source_target_pairs={{0,64},{1,65},{2,66},{3,67},{4,68},{5,69},{6,70},{7,71},{8,72},{9,... | collective-permute-start | bytes 1179656 | tf_op jit(solution)/shard_map/ppermute | solution.py:52
  84.1 8.9 %collective-permute-start.22 = (f32[64,1536]{1,0:T(8,128)S(1)}, f32[64,1536]{1,0:T(8,128)S(1)}, u32[]{:S(2)}, u32[]{:S(2)}) collective-permute-start(f32[64,1536]{1,0:T(8,128)S(1)} %slice.76), channel_id=1, source_target_pairs={{0,192},{1,193},{2,194},{3,195},{4,196},{5,197},{6,198},{7,199},{8... | collective-permute-start | bytes 1179656 | tf_op jit(solution)/shard_map/ppermute | solution.py:52
  87.4 19.2 %collective-permute-start.14 = (f32[128,768]{1,0:T(8,128)S(1)}, f32[128,768]{1,0:T(8,128)S(1)}, u32[]{:S(2)}, u32[]{:S(2)}) collective-permute-start(f32[128,768]{1,0:T(8,128)S(1)} %copy-done.15), channel_id=1, source_target_pairs={{0,2},{1,3},{2,4},{3,5},{4,6},{5,7},{6,0},{7,1},{8,10},{9,11},{10,... | collective-permute-start | bytes 1179656 | tf_op jit(solution)/shard_map/ppermute | solution.py:52
  87.7 20.8 %collective-permute-start.15 = (f32[128,768]{1,0:T(8,128)}, f32[128,768]{1,0:T(8,128)S(1)}, u32[]{:S(2)}, u32[]{:S(2)}) collective-permute-start(f32[128,768]{1,0:T(8,128)} %get-tuple-element.27), channel_id=1, source_target_pairs={{0,6},{1,7},{2,0},{3,1},{4,2},{5,3},{6,4},{7,5},{8,14},{9,15},{10,... | collective-permute-start | bytes 1179656 | tf_op jit(solution)/shard_map/ppermute | solution.py:52
  89.5 19.0 %collective-permute-start.16 = (f32[128,768]{1,0:T(8,128)S(1)}, f32[128,768]{1,0:T(8,128)S(1)}, u32[]{:S(2)}, u32[]{:S(2)}) collective-permute-start(f32[128,768]{1,0:T(8,128)S(1)} %copy-done.23), channel_id=1, source_target_pairs={{0,4},{1,5},{2,6},{3,7},{4,0},{5,1},{6,2},{7,3},{8,12},{9,13},{10,... | collective-permute-start | bytes 1179656 | tf_op jit(solution)/shard_map/ppermute | solution.py:52
  104.5 10.7 %collective-permute-start.23 = (f32[128,768]{1,0:T(8,128)}, f32[128,768]{1,0:T(8,128)S(1)}, u32[]{:S(2)}, u32[]{:S(2)}) collective-permute-start(f32[128,768]{1,0:T(8,128)} %get-tuple-element.31), channel_id=1, source_target_pairs={{0,2},{1,3},{2,4},{3,5},{4,6},{5,7},{6,0},{7,1},{8,10},{9,11},{10,... | collective-permute-start | bytes 1179656 | tf_op jit(solution)/shard_map/ppermute | solution.py:52
  104.8 16.0 %collective-permute-start.24 = (f32[128,768]{1,0:T(8,128)}, f32[128,768]{1,0:T(8,128)S(1)}, u32[]{:S(2)}, u32[]{:S(2)}) collective-permute-start(f32[128,768]{1,0:T(8,128)} %get-tuple-element.32), channel_id=1, source_target_pairs={{0,6},{1,7},{2,0},{3,1},{4,2},{5,3},{6,4},{7,5},{8,14},{9,15},{10,... | collective-permute-start | bytes 1179656 | tf_op jit(solution)/shard_map/ppermute | solution.py:52
  106.6 14.2 %collective-permute-start.25 = (f32[128,768]{1,0:T(8,128)}, f32[128,768]{1,0:T(8,128)S(1)}, u32[]{:S(2)}, u32[]{:S(2)}) collective-permute-start(f32[128,768]{1,0:T(8,128)} %get-tuple-element.33), channel_id=1, source_target_pairs={{0,4},{1,5},{2,6},{3,7},{4,0},{5,1},{6,2},{7,3},{8,12},{9,13},{10,... | collective-permute-start | bytes 1179656 | tf_op jit(solution)/shard_map/ppermute | solution.py:52
  108.6 13.4 %collective-permute-start.17 = (f32[2,32,768]{2,1,0:T(8,128)S(1)}, f32[2,32,768]{2,1,0:T(8,128)S(1)}, u32[]{:S(2)}, u32[]{:S(2)}) collective-permute-start(f32[2,32,768]{2,1,0:T(8,128)S(1)} %dynamic-slice_bitcast_fusion.1), channel_id=1, source_target_pairs={{0,8},{1,9},{2,10},{3,11},{4,12},{5,13},{6,14},{7,15},{8,0},{9,1},... | collective-permute-start | bytes 589832 | tf_op jit(solution)/shard_map/ppermute | solution.py:52
  126.8 10.8 %collective-permute-start.27 = (f32[32,768]{1,0:T(8,128)S(1)}, f32[32,768]{1,0:T(8,128)S(1)}, u32[]{:S(2)}, u32[]{:S(2)}) collective-permute-start(f32[32,768]{1,0:T(8,128)S(1)} %get-tuple-element.59), channel_id=1, source_target_pairs={{0,1},{1,0},{2,3},{3,2},{4,5},{5,4},{6,7},{7,6},{8,9},{9,8},{10,11... | collective-permute-start | bytes 294920 | tf_op jit(solution)/shard_map/ppermute | solution.py:52
  126.9 22.0 %collective-permute-start.28 = (f32[64,768]{1,0:T(8,128)S(1)}, f32[64,768]{1,0:T(8,128)S(1)}, u32[]{:S(2)}, u32[]{:S(2)}) collective-permute-start(f32[64,768]{1,0:T(8,128)S(1)} %maximum_select_fusion), channel_id=1, source_target_pairs={{0,0},{1,160},{2,96},{3,192},{4,128},{5,32},{6,224},{7,64},{8,16},... | collective-permute-start | bytes 589832 | tf_op jit(solution)/shard_map/ppermute | solution.py:52
  137.6 14.6 %collective-permute-start.30 = (f32[64,768]{1,0:T(8,128)S(1)}, f32[64,768]{1,0:T(8,128)S(1)}, u32[]{:S(2)}, u32[]{:S(2)}) collective-permute-start(f32[64,768]{1,0:T(8,128)S(1)} %maximum_select_fusion.1), channel_id=1, source_target_pairs={{0,0},{1,160},{2,96},{3,192},{4,128},{5,32},{6,224},{7,64},{8,16},... | collective-permute-start | bytes 589832 | tf_op jit(solution)/shard_map/ppermute | solution.py:52
  156.2 16.0 %collective-permute-start.32 = (f32[256,128]{1,0:T(8,128)S(1)}, f32[256,128]{1,0:T(8,128)S(1)}, u32[]{:S(2)}, u32[]{:S(2)}) collective-permute-start(f32[256,128]{1,0:T(8,128)S(1)} %get-tuple-element.39), channel_id=1, source_target_pairs={{0,2},{1,3},{2,4},{3,5},{4,6},{5,7},{6,0},{7,1},{8,10},{9,11},{10,... | collective-permute-start | bytes 393224 | tf_op jit(solution)/shard_map/ppermute | solution.py:52
  156.4 18.2 %collective-permute-start.33 = (f32[256,128]{1,0:T(8,128)S(1)}, f32[256,128]{1,0:T(8,128)S(1)}, u32[]{:S(2)}, u32[]{:S(2)}) collective-permute-start(f32[256,128]{1,0:T(8,128)S(1)} %get-tuple-element.40), channel_id=1, source_target_pairs={{0,6},{1,7},{2,0},{3,1},{4,2},{5,3},{6,4},{7,5},{8,14},{9,15},{10,... | collective-permute-start | bytes 393224 | tf_op jit(solution)/shard_map/ppermute | solution.py:52
  165.5 13.0 %collective-permute-start.34 = (f32[256,128]{1,0:T(8,128)S(1)}, f32[256,128]{1,0:T(8,128)S(1)}, u32[]{:S(2)}, u32[]{:S(2)}) collective-permute-start(f32[256,128]{1,0:T(8,128)S(1)} %get-tuple-element.41), channel_id=1, source_target_pairs={{0,4},{1,5},{2,6},{3,7},{4,0},{5,1},{6,2},{7,3},{8,12},{9,13},{10,... | collective-permute-start | bytes 393224 | tf_op jit(solution)/shard_map/ppermute | solution.py:52
  178.6 7.1 %collective-permute-start.35 = (f32[2,64,128]{2,1,0:T(8,128)S(1)}, f32[2,64,128]{2,1,0:T(8,128)S(1)}, u32[]{:S(2)}, u32[]{:S(2)}) collective-permute-start(f32[2,64,128]{2,1,0:T(8,128)S(1)} %dynamic-slice_bitcast_fusion.6), channel_id=1, source_target_pairs={{0,8},{1,9},{2,10},{3,11},{4,12},{5,13},{6,14},{7,15},{8,0},{9,1},... | collective-permute-start | bytes 196616 | tf_op jit(solution)/shard_map/ppermute | solution.py:52
  187.1 14.4 %collective-permute-start.37 = (f32[128,128]{1,0:T(8,128)S(1)}, f32[128,128]{1,0:T(8,128)S(1)}, u32[]{:S(2)}, u32[]{:S(2)}) collective-permute-start(f32[128,128]{1,0:T(8,128)S(1)} %maximum_select_fusion.2), channel_id=1, source_target_pairs={{0,0},{160,1},{96,2},{192,3},{128,4},{32,5},{224,6},{64,7},{16,8},... | collective-permute-start | bytes 196616 | tf_op jit(solution)/shard_map/ppermute | solution.py:52
  (30 other events, 356.1 us)

commit v4 on v3

--- a/solution.py
+++ b/solution.py
@@ -280,7 +280,10 @@
     kept = jnp.concatenate([kept0[:32], kept1[:32], kept0[32:], kept1[32:]])
     off_diagonal = -kept.T
     gram = ring_scatter(gram, "dy").reshape(2, 2, 64, 128)
-    gram = whole(pick(gram, zl) + send(pick(gram, 1 - zl), shift(dzl=1)))
+    block = lambda z, e: lax.dynamic_slice(gram, (z, e, 0, 0), (1, 1, 64, 128)).reshape(64, 128)
+    theirs = send(block(1 - zl, 1 - core), shift(dzl=1, dcore=1)) + send(block(zl, 1 - core), swap)
+    half = block(zl, core) + send(block(1 - zl, core), shift(dzl=1))
+    gram = jnp.where(first, jnp.concatenate([half, theirs]), jnp.concatenate([theirs, half]))
     gram = send(gram, TO_PLACE)
     return off_diagonal, pivot_inverse + gram
 

time: 203 us -> 202 us (level)
    ppermute x38 -> x39, waiting for transfers between devices: 80 us -> 79.6 us  [send(): return lax.ppermute(value, AXES, pairs)]
    ppermute x38 -> x39, starting transfers between devices: 84.9 us -> 85 us  [send(): return lax.ppermute(value, AXES, pairs)]
  transfers between devices with their start and end apart: 38 -> 39, of which waited for: 21 -> 21; matrix products, arithmetic and copies ran while one was open for 3% -> 3% of each run, Pallas kernels for 10% -> 10%
where the time goes in v4:
time: 202 us
  starting transfers between devices  85 us (42%)
  waiting for transfers between devices  79.6 us (39%)
  Pallas kernels  23.6 us (12%)
  local copies, waits for them, and re-layouts  7.13 us (4%)
  other arithmetic  4.09 us (2%)
  between operations  2.39 us (1%)
    ppermute x39, starting transfers between devices, send(): return lax.ppermute(value, AXES, pairs)  85 us
    ppermute x39, waiting for transfers between devices, send(): return lax.ppermute(value, AXES, pairs)  79.6 us
    pallas_call x2, Pallas kernels, product(): pl.pallas_call(functools.partial(product_kernel, rows), out_shape=[jax.Sh...  19.9 us
    unnamed x50, local copies, waits for them, and re-layouts  5.53 us
  transfers between devices with their start and end apart: 39, of which 21 were waited for; matrix products, arithmetic and copies ran while one was open for 3% of the time, Pallas kernels for 10%

profile of v4, /device:TPU:24, one launch (start us, length us, event | category | flops | bytes accessed | tf_op | source)
XLA Modules:
  0.0 201.9 jit_solution(17760981951636977333)
XLA Ops:
  5.6 3.4 %collective-permute-start.1 = (f32[32,1536]{1,0:T(8,128)S(1)}, f32[32,1536]{1,0:T(8,128)S(1)}, u32[]{:S(2)}, u32[]{:S(2)}) collective-permute-start(f32[32,1536]{1,0:T(8,128)S(1)} %get-tuple-element.49.refs_0_), channel_id=1, source_target_pairs={{0,16},{1,17},{2,18},{3,19},{4,20},{5,21},{6,22},{7,23},{8,24},{9,... | collective-permute-start | bytes 589832 | tf_op jit(solution)/shard_map/ppermute | solution.py:52
  9.0 3.1 %collective-permute-start.2 = (f32[32,1536]{1,0:T(8,128)S(1)}, f32[32,1536]{1,0:T(8,128)S(1)}, u32[]{:S(2)}, u32[]{:S(2)}) collective-permute-start(f32[32,1536]{1,0:T(8,128)S(1)} %get-tuple-element.49.refs_0_), channel_id=1, source_target_pairs={{0,48},{1,49},{2,50},{3,51},{4,52},{5,53},{6,54},{7,55},{8,56},{9,... | collective-permute-start | bytes 589832 | tf_op jit(solution)/shard_map/ppermute | solution.py:52
  12.1 6.9 %collective-permute-done.1.refs_1_ = f32[32,1536]{1,0:T(8,128)S(1)} collective-permute-done((f32[32,1536]{1,0:T(8,128)S(1)}, f32[32,1536]{1,0:T(8,128)S(1)}, u32[]{:S(2)}, u32[]{:S(2)}) %collective-permute-start.1) | collective-permute-done | bytes 196640 | tf_op jit(solution)/shard_map/ppermute | solution.py:52
  19.0 3.2 %collective-permute-start.3 = (f32[16,1536]{1,0:T(8,128)S(1)}, f32[16,1536]{1,0:T(8,128)S(1)}, u32[]{:S(2)}, u32[]{:S(2)}) collective-permute-start(f32[16,1536]{1,0:T(8,128)S(1)} %slice.68), channel_id=1, source_target_pairs={{0,16},{1,17},{2,18},{3,19},{4,20},{5,21},{6,22},{7,23},{8,24},{9,... | collective-permute-start | bytes 294920 | tf_op jit(solution)/shard_map/ppermute | solution.py:52
  22.9 2.8 %collective-permute-start.4 = (f32[16,1536]{1,0:T(8,128)S(1)}, f32[16,1536]{1,0:T(8,128)S(1)}, u32[]{:S(2)}, u32[]{:S(2)}) collective-permute-start(f32[16,1536]{1,0:T(8,128)S(1)} %slice.69), channel_id=1, source_target_pairs={{0,48},{1,49},{2,50},{3,51},{4,52},{5,53},{6,54},{7,55},{8,56},{9,... | collective-permute-start | bytes 294920 | tf_op jit(solution)/shard_map/ppermute | solution.py:52
  25.7 2.3 %collective-permute-done.3.refs_3_ = f32[16,1536]{1,0:T(8,128)S(1)} collective-permute-done((f32[16,1536]{1,0:T(8,128)S(1)}, f32[16,1536]{1,0:T(8,128)S(1)}, u32[]{:S(2)}, u32[]{:S(2)}) %collective-permute-start.3) | collective-permute-done | bytes 98336 | tf_op jit(solution)/shard_map/ppermute | solution.py:52
  28.0 2.6 %collective-permute-done.4.refs_4_ = f32[16,1536]{1,0:T(8,128)S(1)} collective-permute-done((f32[16,1536]{1,0:T(8,128)S(1)}, f32[16,1536]{1,0:T(8,128)S(1)}, u32[]{:S(2)}, u32[]{:S(2)}) %collective-permute-start.4) | collective-permute-done | bytes 98336 | tf_op jit(solution)/shard_map/ppermute | solution.py:52
  34.0 4.2 %collective-permute-start.5 = (f32[32,1536]{1,0:T(8,128)S(1)}, f32[32,1536]{1,0:T(8,128)S(1)}, u32[]{:S(2)}, u32[]{:S(2)}) collective-permute-start(f32[32,1536]{1,0:T(8,128)S(1)} %get-tuple-element.22.refs_0_), channel_id=1, source_target_pairs={{0,16},{1,17},{2,18},{3,19},{4,20},{5,21},{6,22},{7,23},{8,24},{9,... | collective-permute-start | bytes 589832 | tf_op jit(solution)/shard_map/ppermute | solution.py:52
  38.2 10.9 %collective-permute-done.9.refs_6_.refs_1_ = f32[128,1536]{1,0:T(8,128)S(1)} collective-permute-done((f32[128,1536]{1,0:T(8,128)S(1)}, f32[128,1536]{1,0:T(8,128)S(1)}, u32[]{:S(2)}, u32[]{:S(2)}) %collective-permute-start.9) | collective-permute-done | bytes 786464 | tf_op jit(solution)/shard_map/ppermute | solution.py:52
  50.0 2.6 %collective-permute-start.12 = (f32[64,1536]{1,0:T(8,128)S(1)}, f32[64,1536]{1,0:T(8,128)S(1)}, u32[]{:S(2)}, u32[]{:S(2)}) collective-permute-start(f32[64,1536]{1,0:T(8,128)S(1)} %slice.73), channel_id=1, source_target_pairs={{0,192},{1,193},{2,194},{3,195},{4,196},{5,197},{6,198},{7,199},{8... | collective-permute-start | bytes 1179656 | tf_op jit(solution)/shard_map/ppermute | solution.py:52
  53.0 3.8 %collective-permute-start.7 = (f32[16,1536]{1,0:T(8,128)S(1)}, f32[16,1536]{1,0:T(8,128)S(1)}, u32[]{:S(2)}, u32[]{:S(2)}) collective-permute-start(f32[16,1536]{1,0:T(8,128)S(1)} %slice.70), channel_id=1, source_target_pairs={{0,16},{1,17},{2,18},{3,19},{4,20},{5,21},{6,22},{7,23},{8,24},{9,... | collective-permute-start | bytes 294920 | tf_op jit(solution)/shard_map/ppermute | solution.py:52
  65.2 3.1 %collective-permute-start.20 = (f32[128,1536]{1,0:T(8,128)}, f32[128,1536]{1,0:T(8,128)S(1)}, u32[]{:S(2)}, u32[]{:S(2)}) collective-permute-start(f32[128,1536]{1,0:T(8,128)} %get-tuple-element.29.refs_0_), channel_id=1, source_target_pairs={{0,192},{1,193},{2,194},{3,195},{4,196},{5,197},{6,198},{7,199},{8... | collective-permute-start | bytes 2359304 | tf_op jit(solution)/shard_map/ppermute | solution.py:52
  68.9 10.0 %product.2 = (f32[128,768]{1,0:T(8,128)}, f32[128,768]{1,0:T(8,128)}, f32[128,768]{1,0:T(8,128)}, f32[128,768]{1,0:T(8,128)}, bf16[512,1536]{1,0:T(8,128)(2,1)}, /*index=5*/bf16[512,1536]{1,0:T(8,128)(2,1)}) custom-call(s32[3]{0:T(128)} %pad_add_fusion.me_ref, f32[128,1536]{1,0:T(8,128)} %copy-done.7, f32[128,1536]{1,0:T(8,128)} %copy-done.4, ...), custom_call_target="tpu_custom_call" | custom-call | flops 1000 | bytes 1000 | tf_op jit(solution)/shard_map/product/pallas_call | solution.py:149
  78.9 4.1 %collective-permute-done.19.refs_0_ = f32[128,1536]{1,0:T(8,128)S(1)} collective-permute-done((f32[128,1536]{1,0:T(8,128)}, f32[128,1536]{1,0:T(8,128)S(1)}, u32[]{:S(2)}, u32[]{:S(2)}) %collective-permute-start.19) | collective-permute-done | bytes 786464 | tf_op jit(solution)/shard_map/ppermute | solution.py:52
  84.1 3.3 %collective-permute-start.22 = (f32[64,1536]{1,0:T(8,128)S(1)}, f32[64,1536]{1,0:T(8,128)S(1)}, u32[]{:S(2)}, u32[]{:S(2)}) collective-permute-start(f32[64,1536]{1,0:T(8,128)S(1)} %slice.76), channel_id=1, source_target_pairs={{0,192},{1,193},{2,194},{3,195},{4,196},{5,197},{6,198},{7,199},{8... | collective-permute-start | bytes 1179656 | tf_op jit(solution)/shard_map/ppermute | solution.py:52
  90.7 2.4 %collective-permute-done.21.refs_3_ = f32[64,1536]{1,0:T(8,128)S(1)} collective-permute-done((f32[64,1536]{1,0:T(8,128)S(1)}, f32[64,1536]{1,0:T(8,128)S(1)}, u32[]{:S(2)}, u32[]{:S(2)}) %collective-permute-start.21) | collective-permute-done | bytes 393248 | tf_op jit(solution)/shard_map/ppermute | solution.py:52
  94.6 10.0 %product.3 = (f32[128,768]{1,0:T(8,128)}, f32[128,768]{1,0:T(8,128)}, f32[128,768]{1,0:T(8,128)}, f32[128,768]{1,0:T(8,128)}, bf16[512,1536]{1,0:T(8,128)(2,1)}, /*index=5*/bf16[512,1536]{1,0:T(8,128)(2,1)}) custom-call(s32[3]{0:T(128)} %pad_add_fusion.me_ref, f32[128,1536]{1,0:T(8,128)} %get-tuple-element.29.refs_0_, f32[128,1536]{1,0:T(8,128)} %copy-done.6, ...), custom_call_target="tpu_custom_call" | custom-call | flops 1000 | bytes 1000 | tf_op jit(solution)/shard_map/product/pallas_call | solution.py:149
  109.3 5.9 %collective-permute-done.23 = f32[128,768]{1,0:T(8,128)S(1)} collective-permute-done((f32[128,768]{1,0:T(8,128)}, f32[128,768]{1,0:T(8,128)S(1)}, u32[]{:S(2)}, u32[]{:S(2)}) %collective-permute-start.23) | collective-permute-done | bytes 393248 | tf_op jit(solution)/shard_map/ppermute | solution.py:52
  115.2 5.6 %collective-permute-done.24 = f32[128,768]{1,0:T(8,128)S(1)} collective-permute-done((f32[128,768]{1,0:T(8,128)}, f32[128,768]{1,0:T(8,128)S(1)}, u32[]{:S(2)}, u32[]{:S(2)}) %collective-permute-start.24) | collective-permute-done | bytes 393248 | tf_op jit(solution)/shard_map/ppermute | solution.py:52
  122.1 4.6 %collective-permute-done.26 = f32[2,32,768]{2,1,0:T(8,128)S(1)} collective-permute-done((f32[2,32,768]{2,1,0:T(8,128)S(1)}, f32[2,32,768]{2,1,0:T(8,128)S(1)}, u32[]{:S(2)}, u32[]{:S(2)}) %collective-permute-start.26) | collective-permute-done | bytes 196640 | tf_op jit(solution)/shard_map/ppermute | solution.py:52
  126.9 10.7 %collective-permute-start.28 = (f32[64,768]{1,0:T(8,128)S(1)}, f32[64,768]{1,0:T(8,128)S(1)}, u32[]{:S(2)}, u32[]{:S(2)}) collective-permute-start(f32[64,768]{1,0:T(8,128)S(1)} %maximum_select_fusion), channel_id=1, source_target_pairs={{0,0},{1,160},{2,96},{3,192},{4,128},{5,32},{6,224},{7,64},{8,16},... | collective-permute-start | bytes 589832 | tf_op jit(solution)/shard_map/ppermute | solution.py:52
  137.7 2.7 %collective-permute-start.30 = (f32[64,768]{1,0:T(8,128)S(1)}, f32[64,768]{1,0:T(8,128)S(1)}, u32[]{:S(2)}, u32[]{:S(2)}) collective-permute-start(f32[64,768]{1,0:T(8,128)S(1)} %maximum_select_fusion.1), channel_id=1, source_target_pairs={{0,0},{1,160},{2,96},{3,192},{4,128},{5,32},{6,224},{7,64},{8,16},... | collective-permute-start | bytes 589832 | tf_op jit(solution)/shard_map/ppermute | solution.py:52
  140.4 8.5 %collective-permute-done.28.refs_4_ = f32[64,768]{1,0:T(8,128)S(1)} collective-permute-done((f32[64,768]{1,0:T(8,128)S(1)}, f32[64,768]{1,0:T(8,128)S(1)}, u32[]{:S(2)}, u32[]{:S(2)}) %collective-permute-start.28) | collective-permute-done | bytes 196640 | tf_op jit(solution)/shard_map/ppermute | solution.py:52
  148.9 3.3 %collective-permute-done.30.refs_6_ = f32[64,768]{1,0:T(8,128)S(1)} collective-permute-done((f32[64,768]{1,0:T(8,128)S(1)}, f32[64,768]{1,0:T(8,128)S(1)}, u32[]{:S(2)}, u32[]{:S(2)}) %collective-permute-start.30) | collective-permute-done | bytes 196640 | tf_op jit(solution)/shard_map/ppermute | solution.py:52
  153.7 2.6 %gram.1 = (f32[256,128]{1,0:T(8,128)S(1)}, f32[256,128]{1,0:T(8,128)S(1)}, f32[256,128]{1,0:T(8,128)S(1)}, f32[256,128]{1,0:T(8,128)S(1)}) custom-call(bf16[512,1536]{1,0:T(8,128)(2,1)S(1)} %copy-done.10, bf16[512,1536]{1,0:T(8,128)(2,1)S(1)} %copy-done.11, bf16[512,1536]{1,0:T(8,128)(2,1)S(1)} %copy-done.12, bf16[512,1536]{1,0:T(8,128)(2,1)S(1)} %copy-done.13, ...), custom_call_target="tpu_custom_call" | custom-call | flops 1000 | bytes 1000 | tf_op jit(solution)/shard_map/gram/pallas_call | solution.py:186
  156.4 9.1 %collective-permute-start.33 = (f32[256,128]{1,0:T(8,128)S(1)}, f32[256,128]{1,0:T(8,128)S(1)}, u32[]{:S(2)}, u32[]{:S(2)}) collective-permute-start(f32[256,128]{1,0:T(8,128)S(1)} %get-tuple-element.40), channel_id=1, source_target_pairs={{0,6},{1,7},{2,0},{3,1},{4,2},{5,3},{6,4},{7,5},{8,14},{9,15},{10,... | collective-permute-start | bytes 393224 | tf_op jit(solution)/shard_map/ppermute | solution.py:52
  165.6 6.7 %collective-permute-start.34 = (f32[256,128]{1,0:T(8,128)S(1)}, f32[256,128]{1,0:T(8,128)S(1)}, u32[]{:S(2)}, u32[]{:S(2)}) collective-permute-start(f32[256,128]{1,0:T(8,128)S(1)} %get-tuple-element.41), channel_id=1, source_target_pairs={{0,4},{1,5},{2,6},{3,7},{4,0},{5,1},{6,2},{7,3},{8,12},{9,13},{10,... | collective-permute-start | bytes 393224 | tf_op jit(solution)/shard_map/ppermute | solution.py:52
  172.4 2.2 %collective-permute-done.33 = f32[256,128]{1,0:T(8,128)S(1)} collective-permute-done((f32[256,128]{1,0:T(8,128)S(1)}, f32[256,128]{1,0:T(8,128)S(1)}, u32[]{:S(2)}, u32[]{:S(2)}) %collective-permute-start.33) | collective-permute-done | bytes 131104 | tf_op jit(solution)/shard_map/ppermute | solution.py:52
  174.6 4.0 %collective-permute-done.34 = f32[256,128]{1,0:T(8,128)S(1)} collective-permute-done((f32[256,128]{1,0:T(8,128)S(1)}, f32[256,128]{1,0:T(8,128)S(1)}, u32[]{:S(2)}, u32[]{:S(2)}) %collective-permute-start.34) | collective-permute-done | bytes 131104 | tf_op jit(solution)/shard_map/ppermute | solution.py:52
  178.7 4.8 %collective-permute-start.35 = (f32[64,128]{1,0:T(8,128)S(1)}, f32[64,128]{1,0:T(8,128)S(1)}, u32[]{:S(2)}, u32[]{:S(2)}) collective-permute-start(f32[64,128]{1,0:T(8,128)S(1)} %get-tuple-element.60), channel_id=1, source_target_pairs={{0,8},{1,9},{2,10},{3,11},{4,12},{5,13},{6,14},{7,15},{8,0},{9,1},... | collective-permute-start | bytes 98312 | tf_op jit(solution)/shard_map/ppermute | solution.py:52
  187.0 7.0 %collective-permute-start.38 = (f32[128,128]{1,0:T(8,128)S(1)}, f32[128,128]{1,0:T(8,128)S(1)}, u32[]{:S(2)}, u32[]{:S(2)}) collective-permute-start(f32[128,128]{1,0:T(8,128)S(1)} %maximum_select_fusion.2), channel_id=1, source_target_pairs={{0,0},{160,1},{96,2},{192,3},{128,4},{32,5},{224,6},{64,7},{16,8},... | collective-permute-start | bytes 196616 | tf_op jit(solution)/shard_map/ppermute | solution.py:52
  195.0 6.3 %collective-permute-done.38 = f32[128,128]{1,0:T(8,128)S(1)} collective-permute-done((f32[128,128]{1,0:T(8,128)S(1)}, f32[128,128]{1,0:T(8,128)S(1)}, u32[]{:S(2)}, u32[]{:S(2)}) %collective-permute-start.38) | collective-permute-done | bytes 65568 | tf_op jit(solution)/shard_map/ppermute | solution.py:52
  (136 shorter events, 36.6 us)
Async XLA Ops:
  0.6 56.7 %collective-permute-start.13 = (f32[768,768]{1,0:T(8,128)}, f32[768,768]{1,0:T(8,128)}, u32[]{:S(2)}, u32[]{:S(2)}) collective-permute-start(f32[768,768]{1,0:T(8,128)} %param.4), channel_id=1, source_target_pairs={{0,1},{1,0},{2,3},{3,2},{4,5},{5,4},{6,7},{7,6},{8,9},{9,8},{10,11... | collective-permute-start | bytes 7077896 | tf_op jit(solution)/shard_map/ppermute | solution.py:52
  5.6 13.4 %collective-permute-start.1 = (f32[32,1536]{1,0:T(8,128)S(1)}, f32[32,1536]{1,0:T(8,128)S(1)}, u32[]{:S(2)}, u32[]{:S(2)}) collective-permute-start(f32[32,1536]{1,0:T(8,128)S(1)} %get-tuple-element.49.refs_0_), channel_id=1, source_target_pairs={{0,16},{1,17},{2,18},{3,19},{4,20},{5,21},{6,22},{7,23},{8,24},{9,... | collective-permute-start | bytes 589832 | tf_op jit(solution)/shard_map/ppermute | solution.py:52
  9.0 13.8 %collective-permute-start.2 = (f32[32,1536]{1,0:T(8,128)S(1)}, f32[32,1536]{1,0:T(8,128)S(1)}, u32[]{:S(2)}, u32[]{:S(2)}) collective-permute-start(f32[32,1536]{1,0:T(8,128)S(1)} %get-tuple-element.49.refs_0_), channel_id=1, source_target_pairs={{0,48},{1,49},{2,50},{3,51},{4,52},{5,53},{6,54},{7,55},{8,56},{9,... | collective-permute-start | bytes 589832 | tf_op jit(solution)/shard_map/ppermute | solution.py:52
  19.0 9.0 %collective-permute-start.3 = (f32[16,1536]{1,0:T(8,128)S(1)}, f32[16,1536]{1,0:T(8,128)S(1)}, u32[]{:S(2)}, u32[]{:S(2)}) collective-permute-start(f32[16,1536]{1,0:T(8,128)S(1)} %slice.68), channel_id=1, source_target_pairs={{0,16},{1,17},{2,18},{3,19},{4,20},{5,21},{6,22},{7,23},{8,24},{9,... | collective-permute-start | bytes 294920 | tf_op jit(solution)/shard_map/ppermute | solution.py:52
  22.9 7.8 %collective-permute-start.4 = (f32[16,1536]{1,0:T(8,128)S(1)}, f32[16,1536]{1,0:T(8,128)S(1)}, u32[]{:S(2)}, u32[]{:S(2)}) collective-permute-start(f32[16,1536]{1,0:T(8,128)S(1)} %slice.69), channel_id=1, source_target_pairs={{0,48},{1,49},{2,50},{3,51},{4,52},{5,53},{6,54},{7,55},{8,56},{9,... | collective-permute-start | bytes 294920 | tf_op jit(solution)/shard_map/ppermute | solution.py:52
  30.7 18.4 %collective-permute-start.9 = (f32[128,1536]{1,0:T(8,128)S(1)}, f32[128,1536]{1,0:T(8,128)S(1)}, u32[]{:S(2)}, u32[]{:S(2)}) collective-permute-start(f32[128,1536]{1,0:T(8,128)S(1)} %get-tuple-element.23.refs_5_), channel_id=1, source_target_pairs={{0,64},{1,65},{2,66},{3,67},{4,68},{5,69},{6,70},{7,71},{8,72},{9,... | collective-permute-start | bytes 2359304 | tf_op jit(solution)/shard_map/ppermute | solution.py:52
  32.2 17.7 %collective-permute-start.10 = (f32[128,1536]{1,0:T(8,128)S(1)}, f32[128,1536]{1,0:T(8,128)S(1)}, u32[]{:S(2)}, u32[]{:S(2)}) collective-permute-start(f32[128,1536]{1,0:T(8,128)S(1)} %get-tuple-element.23.refs_5_), channel_id=1, source_target_pairs={{0,192},{1,193},{2,194},{3,195},{4,196},{5,197},{6,198},{7,199},{8... | collective-permute-start | bytes 2359304 | tf_op jit(solution)/shard_map/ppermute | solution.py:52
  34.0 19.0 %collective-permute-start.5 = (f32[32,1536]{1,0:T(8,128)S(1)}, f32[32,1536]{1,0:T(8,128)S(1)}, u32[]{:S(2)}, u32[]{:S(2)}) collective-permute-start(f32[32,1536]{1,0:T(8,128)S(1)} %get-tuple-element.22.refs_0_), channel_id=1, source_target_pairs={{0,16},{1,17},{2,18},{3,19},{4,20},{5,21},{6,22},{7,23},{8,24},{9,... | collective-permute-start | bytes 589832 | tf_op jit(solution)/shard_map/ppermute | solution.py:52
  38.2 18.6 %collective-permute-start.6 = (f32[32,1536]{1,0:T(8,128)S(1)}, f32[32,1536]{1,0:T(8,128)S(1)}, u32[]{:S(2)}, u32[]{:S(2)}) collective-permute-start(f32[32,1536]{1,0:T(8,128)S(1)} %get-tuple-element.22.refs_0_), channel_id=1, source_target_pairs={{0,48},{1,49},{2,50},{3,51},{4,52},{5,53},{6,54},{7,55},{8,56},{9,... | collective-permute-start | bytes 589832 | tf_op jit(solution)/shard_map/ppermute | solution.py:52
  49.1 13.8 %collective-permute-start.11 = (f32[64,1536]{1,0:T(8,128)S(1)}, f32[64,1536]{1,0:T(8,128)S(1)}, u32[]{:S(2)}, u32[]{:S(2)}) collective-permute-start(f32[64,1536]{1,0:T(8,128)S(1)} %slice.72), channel_id=1, source_target_pairs={{0,64},{1,65},{2,66},{3,67},{4,68},{5,69},{6,70},{7,71},{8,72},{9,... | collective-permute-start | bytes 1179656 | tf_op jit(solution)/shard_map/ppermute | solution.py:52
  50.0 13.0 %collective-permute-start.12 = (f32[64,1536]{1,0:T(8,128)S(1)}, f32[64,1536]{1,0:T(8,128)S(1)}, u32[]{:S(2)}, u32[]{:S(2)}) collective-permute-start(f32[64,1536]{1,0:T(8,128)S(1)} %slice.73), channel_id=1, source_target_pairs={{0,192},{1,193},{2,194},{3,195},{4,196},{5,197},{6,198},{7,199},{8... | collective-permute-start | bytes 1179656 | tf_op jit(solution)/shard_map/ppermute | solution.py:52
  53.0 8.0 %collective-permute-start.7 = (f32[16,1536]{1,0:T(8,128)S(1)}, f32[16,1536]{1,0:T(8,128)S(1)}, u32[]{:S(2)}, u32[]{:S(2)}) collective-permute-start(f32[16,1536]{1,0:T(8,128)S(1)} %slice.70), channel_id=1, source_target_pairs={{0,16},{1,17},{2,18},{3,19},{4,20},{5,21},{6,22},{7,23},{8,24},{9,... | collective-permute-start | bytes 294920 | tf_op jit(solution)/shard_map/ppermute | solution.py:52
  56.8 6.1 %collective-permute-start.8 = (f32[16,1536]{1,0:T(8,128)S(1)}, f32[16,1536]{1,0:T(8,128)S(1)}, u32[]{:S(2)}, u32[]{:S(2)}) collective-permute-start(f32[16,1536]{1,0:T(8,128)S(1)} %slice.71), channel_id=1, source_target_pairs={{0,48},{1,49},{2,50},{3,51},{4,52},{5,53},{6,54},{7,55},{8,56},{9,... | collective-permute-start | bytes 294920 | tf_op jit(solution)/shard_map/ppermute | solution.py:52
  65.0 18.0 %collective-permute-start.19 = (f32[128,1536]{1,0:T(8,128)}, f32[128,1536]{1,0:T(8,128)S(1)}, u32[]{:S(2)}, u32[]{:S(2)}) collective-permute-start(f32[128,1536]{1,0:T(8,128)} %get-tuple-element.29.refs_0_), channel_id=1, source_target_pairs={{0,64},{1,65},{2,66},{3,67},{4,68},{5,69},{6,70},{7,71},{8,72},{9,... | collective-permute-start | bytes 2359304 | tf_op jit(solution)/shard_map/ppermute | solution.py:52
  65.2 18.9 %collective-permute-start.20 = (f32[128,1536]{1,0:T(8,128)}, f32[128,1536]{1,0:T(8,128)S(1)}, u32[]{:S(2)}, u32[]{:S(2)}) collective-permute-start(f32[128,1536]{1,0:T(8,128)} %get-tuple-element.29.refs_0_), channel_id=1, source_target_pairs={{0,192},{1,193},{2,194},{3,195},{4,196},{5,197},{6,198},{7,199},{8... | collective-permute-start | bytes 2359304 | tf_op jit(solution)/shard_map/ppermute | solution.py:52
  84.0 9.1 %collective-permute-start.21 = (f32[64,1536]{1,0:T(8,128)S(1)}, f32[64,1536]{1,0:T(8,128)S(1)}, u32[]{:S(2)}, u32[]{:S(2)}) collective-permute-start(f32[64,1536]{1,0:T(8,128)S(1)} %slice.75), channel_id=1, source_target_pairs={{0,64},{1,65},{2,66},{3,67},{4,68},{5,69},{6,70},{7,71},{8,72},{9,... | collective-permute-start | bytes 1179656 | tf_op jit(solution)/shard_map/ppermute | solution.py:52
  84.1 8.9 %collective-permute-start.22 = (f32[64,1536]{1,0:T(8,128)S(1)}, f32[64,1536]{1,0:T(8,128)S(1)}, u32[]{:S(2)}, u32[]{:S(2)}) collective-permute-start(f32[64,1536]{1,0:T(8,128)S(1)} %slice.76), channel_id=1, source_target_pairs={{0,192},{1,193},{2,194},{3,195},{4,196},{5,197},{6,198},{7,199},{8... | collective-permute-start | bytes 1179656 | tf_op jit(solution)/shard_map/ppermute | solution.py:52
  87.4 19.2 %collective-permute-start.14 = (f32[128,768]{1,0:T(8,128)S(1)}, f32[128,768]{1,0:T(8,128)S(1)}, u32[]{:S(2)}, u32[]{:S(2)}) collective-permute-start(f32[128,768]{1,0:T(8,128)S(1)} %copy-done.15), channel_id=1, source_target_pairs={{0,2},{1,3},{2,4},{3,5},{4,6},{5,7},{6,0},{7,1},{8,10},{9,11},{10,... | collective-permute-start | bytes 1179656 | tf_op jit(solution)/shard_map/ppermute | solution.py:52
  87.7 20.8 %collective-permute-start.15 = (f32[128,768]{1,0:T(8,128)}, f32[128,768]{1,0:T(8,128)S(1)}, u32[]{:S(2)}, u32[]{:S(2)}) collective-permute-start(f32[128,768]{1,0:T(8,128)} %get-tuple-element.27), channel_id=1, source_target_pairs={{0,6},{1,7},{2,0},{3,1},{4,2},{5,3},{6,4},{7,5},{8,14},{9,15},{10,... | collective-permute-start | bytes 1179656 | tf_op jit(solution)/shard_map/ppermute | solution.py:52
  89.5 19.0 %collective-permute-start.16 = (f32[128,768]{1,0:T(8,128)S(1)}, f32[128,768]{1,0:T(8,128)S(1)}, u32[]{:S(2)}, u32[]{:S(2)}) collective-permute-start(f32[128,768]{1,0:T(8,128)S(1)} %copy-done.23), channel_id=1, source_target_pairs={{0,4},{1,5},{2,6},{3,7},{4,0},{5,1},{6,2},{7,3},{8,12},{9,13},{10,... | collective-permute-start | bytes 1179656 | tf_op jit(solution)/shard_map/ppermute | solution.py:52
  104.5 10.7 %collective-permute-start.23 = (f32[128,768]{1,0:T(8,128)}, f32[128,768]{1,0:T(8,128)S(1)}, u32[]{:S(2)}, u32[]{:S(2)}) collective-permute-start(f32[128,768]{1,0:T(8,128)} %get-tuple-element.31), channel_id=1, source_target_pairs={{0,2},{1,3},{2,4},{3,5},{4,6},{5,7},{6,0},{7,1},{8,10},{9,11},{10,... | collective-permute-start | bytes 1179656 | tf_op jit(solution)/shard_map/ppermute | solution.py:52
  104.9 15.9 %collective-permute-start.24 = (f32[128,768]{1,0:T(8,128)}, f32[128,768]{1,0:T(8,128)S(1)}, u32[]{:S(2)}, u32[]{:S(2)}) collective-permute-start(f32[128,768]{1,0:T(8,128)} %get-tuple-element.32), channel_id=1, source_target_pairs={{0,6},{1,7},{2,0},{3,1},{4,2},{5,3},{6,4},{7,5},{8,14},{9,15},{10,... | collective-permute-start | bytes 1179656 | tf_op jit(solution)/shard_map/ppermute | solution.py:52
  106.7 14.1 %collective-permute-start.25 = (f32[128,768]{1,0:T(8,128)}, f32[128,768]{1,0:T(8,128)S(1)}, u32[]{:S(2)}, u32[]{:S(2)}) collective-permute-start(f32[128,768]{1,0:T(8,128)} %get-tuple-element.33), channel_id=1, source_target_pairs={{0,4},{1,5},{2,6},{3,7},{4,0},{5,1},{6,2},{7,3},{8,12},{9,13},{10,... | collective-permute-start | bytes 1179656 | tf_op jit(solution)/shard_map/ppermute | solution.py:52
  108.6 13.3 %collective-permute-start.17 = (f32[2,32,768]{2,1,0:T(8,128)S(1)}, f32[2,32,768]{2,1,0:T(8,128)S(1)}, u32[]{:S(2)}, u32[]{:S(2)}) collective-permute-start(f32[2,32,768]{2,1,0:T(8,128)S(1)} %dynamic-slice_bitcast_fusion.1), channel_id=1, source_target_pairs={{0,8},{1,9},{2,10},{3,11},{4,12},{5,13},{6,14},{7,15},{8,0},{9,1},... | collective-permute-start | bytes 589832 | tf_op jit(solution)/shard_map/ppermute | solution.py:52
  126.8 10.9 %collective-permute-start.27 = (f32[32,768]{1,0:T(8,128)S(1)}, f32[32,768]{1,0:T(8,128)S(1)}, u32[]{:S(2)}, u32[]{:S(2)}) collective-permute-start(f32[32,768]{1,0:T(8,128)S(1)} %get-tuple-element.59), channel_id=1, source_target_pairs={{0,1},{1,0},{2,3},{3,2},{4,5},{5,4},{6,7},{7,6},{8,9},{9,8},{10,11... | collective-permute-start | bytes 294920 | tf_op jit(solution)/shard_map/ppermute | solution.py:52
  126.9 22.0 %collective-permute-start.28 = (f32[64,768]{1,0:T(8,128)S(1)}, f32[64,768]{1,0:T(8,128)S(1)}, u32[]{:S(2)}, u32[]{:S(2)}) collective-permute-start(f32[64,768]{1,0:T(8,128)S(1)} %maximum_select_fusion), channel_id=1, source_target_pairs={{0,0},{1,160},{2,96},{3,192},{4,128},{5,32},{6,224},{7,64},{8,16},... | collective-permute-start | bytes 589832 | tf_op jit(solution)/shard_map/ppermute | solution.py:52
  137.7 14.6 %collective-permute-start.30 = (f32[64,768]{1,0:T(8,128)S(1)}, f32[64,768]{1,0:T(8,128)S(1)}, u32[]{:S(2)}, u32[]{:S(2)}) collective-permute-start(f32[64,768]{1,0:T(8,128)S(1)} %maximum_select_fusion.1), channel_id=1, source_target_pairs={{0,0},{1,160},{2,96},{3,192},{4,128},{5,32},{6,224},{7,64},{8,16},... | collective-permute-start | bytes 589832 | tf_op jit(solution)/shard_map/ppermute | solution.py:52
  156.3 16.1 %collective-permute-start.32 = (f32[256,128]{1,0:T(8,128)S(1)}, f32[256,128]{1,0:T(8,128)S(1)}, u32[]{:S(2)}, u32[]{:S(2)}) collective-permute-start(f32[256,128]{1,0:T(8,128)S(1)} %get-tuple-element.39), channel_id=1, source_target_pairs={{0,2},{1,3},{2,4},{3,5},{4,6},{5,7},{6,0},{7,1},{8,10},{9,11},{10,... | collective-permute-start | bytes 393224 | tf_op jit(solution)/shard_map/ppermute | solution.py:52
  156.4 18.2 %collective-permute-start.33 = (f32[256,128]{1,0:T(8,128)S(1)}, f32[256,128]{1,0:T(8,128)S(1)}, u32[]{:S(2)}, u32[]{:S(2)}) collective-permute-start(f32[256,128]{1,0:T(8,128)S(1)} %get-tuple-element.40), channel_id=1, source_target_pairs={{0,6},{1,7},{2,0},{3,1},{4,2},{5,3},{6,4},{7,5},{8,14},{9,15},{10,... | collective-permute-start | bytes 393224 | tf_op jit(solution)/shard_map/ppermute | solution.py:52
  165.6 13.0 %collective-permute-start.34 = (f32[256,128]{1,0:T(8,128)S(1)}, f32[256,128]{1,0:T(8,128)S(1)}, u32[]{:S(2)}, u32[]{:S(2)}) collective-permute-start(f32[256,128]{1,0:T(8,128)S(1)} %get-tuple-element.41), channel_id=1, source_target_pairs={{0,4},{1,5},{2,6},{3,7},{4,0},{5,1},{6,2},{7,3},{8,12},{9,13},{10,... | collective-permute-start | bytes 393224 | tf_op jit(solution)/shard_map/ppermute | solution.py:52
  178.7 6.7 %collective-permute-start.35 = (f32[64,128]{1,0:T(8,128)S(1)}, f32[64,128]{1,0:T(8,128)S(1)}, u32[]{:S(2)}, u32[]{:S(2)}) collective-permute-start(f32[64,128]{1,0:T(8,128)S(1)} %get-tuple-element.60), channel_id=1, source_target_pairs={{0,8},{1,9},{2,10},{3,11},{4,12},{5,13},{6,14},{7,15},{8,0},{9,1},... | collective-permute-start | bytes 98312 | tf_op jit(solution)/shard_map/ppermute | solution.py:52
  187.0 14.3 %collective-permute-start.38 = (f32[128,128]{1,0:T(8,128)S(1)}, f32[128,128]{1,0:T(8,128)S(1)}, u32[]{:S(2)}, u32[]{:S(2)}) collective-permute-start(f32[128,128]{1,0:T(8,128)S(1)} %maximum_select_fusion.2), channel_id=1, source_target_pairs={{0,0},{160,1},{96,2},{192,3},{128,4},{32,5},{224,6},{64,7},{16,8},... | collective-permute-start | bytes 196616 | tf_op jit(solution)/shard_map/ppermute | solution.py:52
  (31 other events, 361.4 us)
